TPU v7x, 32 devices: a whole 2x2x4 slice. The times are simulated.
32 devices in a mesh: dp: 8 (over y, x, core), seq: 4 (over z).
Axes of the slice: x: 2, y: 2, z: 4, core: 2. Of those that a mesh axis runs over, the one named last changes fastest.
Arguments:
- tokens: bfloat16 [15360, 768], P(('dp', 'seq')), may hold values from -6 to 6
- cotangent: bfloat16 [15360, 768], P(('dp', 'seq')), may hold values from -6 to 6
- doc_lengths: int32 [8, 8], P('dp'), may hold values from 1 to 960, 1920 in all within a row
- pad_counts: int32 [8], P('dp'), may hold values from 0 to 479
- w_in: float32 [2, 2304, 768], P(None, ('dp', 'seq')), may hold values from -0.21875 to 0.21875
- w_ao: float32 [768, 768], P(('dp', 'seq')), may hold values from -3.5 to 3.5
- w_fo: float32 [768, 1152], P(('dp', 'seq')), may hold values from -0.1875 to 0.1875
- norm_gains: float32 [2, 768], P(None, ('dp', 'seq')), may hold values from 0.5 to 1.5
- gain_moment: float32 [2, 768], P(None, ('dp', 'seq'))
- gain_second: float32 [2, 768], P(None, ('dp', 'seq')), as said below
- stat_l_in: float32 [2, 2304, 2304], P(None, ('dp', 'seq')), as said below
- stat_r_in: float32 [2, 768, 768], P(None, ('dp', 'seq')), as said below
- stat_l_ao: float32 [768, 768], P(('dp', 'seq')), as said below
- stat_r_ao: float32 [768, 768], P(('dp', 'seq')), as said below
- stat_l_fo: float32 [768, 768], P(('dp', 'seq')), as said below
- stat_r_fo: float32 [1152, 1152], P(('dp', 'seq')), as said below
- root_l_in: float32 [2, 2304, 2304], P(None, ('dp', 'seq')), as said below
- root_r_in: float32 [2, 768, 768], P(None, ('dp', 'seq')), as said below
- root_l_ao: float32 [768, 768], P(('dp', 'seq')), as said below
- root_r_ao: float32 [768, 768], P(('dp', 'seq')), as said below
- root_l_fo: float32 [768, 768], P(('dp', 'seq')), as said below
- root_r_fo: float32 [1152, 1152], P(('dp', 'seq')), as said below
Outputs:
- layer_out: bfloat16 [15360, 768], P(('dp', 'seq'))
- grad_input: float32 [15360, 768], P(('dp', 'seq'))
- grad_w_in: float32 [2, 2304, 768], P(None, ('dp', 'seq'))
- grad_w_ao: float32 [768, 768], P(('dp', 'seq'))
- grad_w_fo: float32 [768, 1152], P(('dp', 'seq'))
- grad_gains: float32 [2, 768], P(None, ('dp', 'seq'))
- new_gain_moment: float32 [2, 768], P(None, ('dp', 'seq'))
- new_gain_second: float32 [2, 768], P(None, ('dp', 'seq'))
- new_gains: float32 [2, 768], P(None, ('dp', 'seq'))
- new_stat_l_in: float32 [2, 2304, 2304], P(None, ('dp', 'seq'))
- new_stat_r_in: float32 [2, 768, 768], P(None, ('dp', 'seq'))
- new_stat_l_ao: float32 [768, 768], P(('dp', 'seq'))
- new_stat_r_ao: float32 [768, 768], P(('dp', 'seq'))
- new_stat_l_fo: float32 [768, 768], P(('dp', 'seq'))
- new_stat_r_fo: float32 [1152, 1152], P(('dp', 'seq'))
- new_w_in: float32 [2, 2304, 768], P(None, ('dp', 'seq'))
- new_w_ao: float32 [768, 768], P(('dp', 'seq'))
- new_w_fo: float32 [768, 1152], P(('dp', 'seq'))
Inputs may be any that keep to these rules, and one draw needn't show every extreme that they name: `doc_lengths`: each row's 8 lengths sum to 1920; the longest of each row is exactly 960. `gain_second`: positive. `stat_l_in`: symmetric in its last two dimensions. `stat_r_in`: symmetric in its last two dimensions. `stat_l_ao`: symmetric. `stat_r_ao`: symmetric. `stat_l_fo`: symmetric. `stat_r_fo`: symmetric. `root_l_in`: symmetric in its last two dimensions. `root_r_in`: symmetric in its last two dimensions. `root_l_ao`: symmetric. `root_r_ao`: symmetric. `root_l_fo`: symmetric. `root_r_fo`: symmetric.
All inputs are finite; a program needn't handle non-finite values.
Results may differ from a plain program's by a relative error of at most 0.013.
The roundings to bfloat16 on the way count: a program that leaves them out, or rounds other values in their place, can miss the bound.
Values may be sent and summed in bfloat16 or wider, within the bound.
No kernel may reach another device: no remote copies, remote signals or barrier semaphores. Data moves between devices by JAX's collectives and lax.ppermute only.
A program may use at most 256 MiB of HBM per device.

v0:
```python
import math

import jax
import jax.numpy as jnp
from jax import lax
from jax.sharding import PartitionSpec as P

HEAD_DIM = 64


NORM_EPS = 1e-05
ROPE_THETA = 160000.0
SCORE_SCALE = 0.125
MASK_FILL = -1e30
ADAM_RATE = 0.2
SHAMPOO_RATE = 1.0
HIGHEST = lax.Precision.HIGHEST


def norm_forward(values):
    center = values - jnp.mean(values, axis=-1, keepdims=True)
    inv_spread = lax.rsqrt(jnp.mean(center * center, axis=-1, keepdims=True) + NORM_EPS)
    return (center * inv_spread, inv_spread)


def norm_backward(grad_out, normed, inv_spread, gain_row):
    scaled = grad_out * gain_row
    inner_term = (
        scaled
        - jnp.mean(scaled, axis=-1, keepdims=True)
        - normed * jnp.mean(scaled * normed, axis=-1, keepdims=True)
    )
    return (inner_term * inv_spread, jnp.sum(grad_out * normed, axis=0))


def gelu_value(inputs):
    return 0.5 * inputs * (1.0 + lax.erf(inputs * (1.0 / math.sqrt(2.0))))


def gelu_slope(inputs):
    cumulative = 0.5 * (1.0 + lax.erf(inputs * (1.0 / math.sqrt(2.0))))
    return cumulative + inputs * jnp.exp(-0.5 * inputs * inputs) * (1.0 / math.sqrt(2.0 * math.pi))


def rotate(values, cos_table, sin_table):
    half_dim = values.shape[-1] // 2
    turned = jnp.concatenate([-values[..., half_dim:], values[..., :half_dim]], axis=-1)
    return values * cos_table + turned * sin_table


def unrotate(gradient, cos_table, sin_table):
    half_dim = gradient.shape[-1] // 2
    shifted = gradient * sin_table
    back_turn = jnp.concatenate([shifted[..., half_dim:], -shifted[..., :half_dim]], axis=-1)
    return gradient * cos_table + back_turn


def rope_tables(within):
    freq_index = jnp.arange(0, HEAD_DIM, 2, dtype=jnp.float32)
    inverse = 1.0 / jnp.power(ROPE_THETA, freq_index / HEAD_DIM)
    angles = within.astype(jnp.float32)[:, None] * inverse[None, :]
    angles = jnp.concatenate([angles, angles], axis=-1)
    return (jnp.cos(angles), jnp.sin(angles))


def doc_tables(lengths_row, pad_count, row_length):
    doc_ends = jnp.cumsum(lengths_row)
    starts = doc_ends - lengths_row
    places = jnp.arange(row_length, dtype=jnp.int32)
    segment = jnp.sum((places[:, None] >= doc_ends[None, :]).astype(jnp.int32), axis=1)
    doc_ids = jnp.arange(lengths_row.shape[0], dtype=jnp.int32)
    doc_begin = jnp.sum(jnp.where(segment[:, None] == doc_ids[None, :], starts[None, :], 0), axis=1)
    is_valid = places < row_length - pad_count
    return (segment, places - doc_begin, is_valid)


def apply_rows(activations, weight):
    return lax.dot_general(
        activations, weight, (((1,), (1,)), ((), ())), preferred_element_type=jnp.float32
    )


def outer_sum(grad_rows, act_rows):
    return lax.dot_general(
        grad_rows, act_rows, (((0,), (0,)), ((), ())), preferred_element_type=jnp.float32
    )


def body(
    tokens,
    cotangent,
    doc_lengths,
    pad_counts,
    w_in,
    w_ao,
    w_fo,
    norm_gains,
    gain_moment,
    gain_second,
    stat_l_in,
    stat_r_in,
    stat_l_ao,
    stat_r_ao,
    stat_l_fo,
    stat_r_fo,
    root_l_in,
    root_r_in,
    root_l_ao,
    root_r_ao,
    root_l_fo,
    root_r_fo,
):
    token_count, model_width = tokens.shape
    head_count = model_width // HEAD_DIM
    pair_count = head_count // 2
    pair_width = 2 * HEAD_DIM
    hidden_width = w_fo.shape[1]
    seq_count = lax.axis_size("seq")
    row_length = token_count * seq_count
    first_place = lax.axis_index("seq") * token_count
    segment, within, is_valid = doc_tables(doc_lengths[0], pad_counts[0], row_length)
    own_places = first_place + jnp.arange(token_count, dtype=jnp.int32)
    all_places = jnp.arange(row_length, dtype=jnp.int32)
    own_segment = lax.dynamic_slice_in_dim(segment, first_place, token_count)
    own_within = lax.dynamic_slice_in_dim(within, first_place, token_count)
    allowed = (own_segment[:, None] == segment[None, :]) & (
        is_valid[None, :] | (own_places[:, None] == all_places[None, :])
    )
    cos_table, sin_table = rope_tables(own_within)
    cos_table = cos_table[:, None, :]
    sin_table = sin_table[:, None, :]
    low_weights = (
        w_in.astype(jnp.bfloat16),
        w_ao.astype(jnp.bfloat16),
        w_fo.astype(jnp.bfloat16),
        norm_gains.astype(jnp.bfloat16),
    )
    full_in, full_ao, full_fo, full_gains = (
        lax.all_gather(low_weights[0], ("dp", "seq"), axis=1, tiled=True),
        lax.all_gather(low_weights[1], ("dp", "seq"), axis=0, tiled=True),
        lax.all_gather(low_weights[2], ("dp", "seq"), axis=0, tiled=True),
        lax.all_gather(low_weights[3], ("dp", "seq"), axis=1, tiled=True),
    )
    gain_rows = full_gains.astype(jnp.float32)
    inputs = tokens.astype(jnp.float32)
    normed_one, spread_one = norm_forward(inputs)
    attn_in = (normed_one * gain_rows[0]).astype(jnp.bfloat16)
    qkv_raw = apply_rows(attn_in, full_in[0])
    query_low = (
        rotate(
            qkv_raw[:, :model_width].reshape(token_count, head_count, HEAD_DIM),
            cos_table,
            sin_table,
        )
        .reshape(token_count, model_width)
        .astype(jnp.bfloat16)
    )
    key_low = (
        rotate(
            qkv_raw[:, model_width : 2 * model_width].reshape(token_count, head_count, HEAD_DIM),
            cos_table,
            sin_table,
        )
        .reshape(token_count, model_width)
        .astype(jnp.bfloat16)
    )
    value_low = qkv_raw[:, 2 * model_width :].astype(jnp.bfloat16)
    keys_all, values_all = (
        lax.all_gather(key_low, "seq", axis=0, tiled=True),
        lax.all_gather(value_low, "seq", axis=0, tiled=True),
    )

    def pair_slice(matrix, pair_index):
        return lax.dynamic_slice_in_dim(matrix, pair_index * pair_width, pair_width, 1).reshape(
            matrix.shape[0], 2, HEAD_DIM
        )

    def pair_scores(query_pair, key_pair, allow_mask):
        raw_scores = (
            jnp.einsum("thd,khd->htk", query_pair, key_pair, preferred_element_type=jnp.float32)
            * SCORE_SCALE
        )
        return jnp.where(allow_mask[None], raw_scores, MASK_FILL)

    def forward_pair(loop_carry, pair_index):
        scores = pair_scores(
            pair_slice(query_low, pair_index), pair_slice(keys_all, pair_index), allowed
        )
        row_max = jnp.max(scores, axis=-1, keepdims=True)
        exponent = jnp.exp(scores - row_max)
        row_sum = jnp.sum(exponent, axis=-1, keepdims=True)
        weights_low = (exponent / row_sum).astype(jnp.bfloat16)
        attended = jnp.einsum(
            "htk,khd->thd",
            weights_low,
            pair_slice(values_all, pair_index),
            preferred_element_type=jnp.float32,
        )
        return (
            loop_carry,
            (attended.reshape(token_count, pair_width), (row_max + jnp.log(row_sum))[..., 0]),
        )

    unused, (attended_pairs, log_norms) = lax.scan(forward_pair, 0, jnp.arange(pair_count))
    attn_low = (
        jnp.transpose(attended_pairs, (1, 0, 2))
        .reshape(token_count, model_width)
        .astype(jnp.bfloat16)
    )
    residual = inputs + apply_rows(attn_low, full_ao)
    normed_two, spread_two = norm_forward(residual)
    ffn_in = (normed_two * gain_rows[1]).astype(jnp.bfloat16)
    projected = apply_rows(ffn_in, full_in[1])
    inner_part = projected[:, :hidden_width]
    gate_part = projected[:, hidden_width:]
    activated = gelu_value(inner_part)
    mid_low = (activated * gate_part).astype(jnp.bfloat16)
    layer_out = (residual + apply_rows(mid_low, full_fo)).astype(jnp.bfloat16)
    back_in, back_ao, back_fo, back_gains = (
        lax.all_gather(low_weights[0], ("dp", "seq"), axis=1, tiled=True),
        lax.all_gather(low_weights[1], ("dp", "seq"), axis=0, tiled=True),
        lax.all_gather(low_weights[2], ("dp", "seq"), axis=0, tiled=True),
        lax.all_gather(low_weights[3], ("dp", "seq"), axis=1, tiled=True),
    )
    back_rows = back_gains.astype(jnp.float32)
    grad_fo_w = outer_sum(cotangent, mid_low)
    grad_mid = jnp.dot(cotangent, back_fo, preferred_element_type=jnp.float32)
    grad_proj = jnp.concatenate(
        [grad_mid * gate_part * gelu_slope(inner_part), grad_mid * activated], axis=1
    ).astype(jnp.bfloat16)
    grad_ffn_w = outer_sum(grad_proj, ffn_in)
    grad_ffn_in = jnp.dot(grad_proj, back_in[1], preferred_element_type=jnp.float32)
    grad_norm_two, grad_gain_two = norm_backward(grad_ffn_in, normed_two, spread_two, back_rows[1])
    grad_resid = cotangent.astype(jnp.float32) + grad_norm_two
    grad_out_attn = grad_resid.astype(jnp.bfloat16)
    grad_ao_w = outer_sum(grad_out_attn, attn_low)
    grad_attn = jnp.dot(grad_out_attn, back_ao, preferred_element_type=jnp.float32).astype(
        jnp.bfloat16
    )

    def query_side_grads(pair_index):
        query_pair = pair_slice(query_low, pair_index)
        key_pair = pair_slice(keys_all, pair_index)
        value_pair = pair_slice(values_all, pair_index)
        grad_pair = pair_slice(grad_attn, pair_index)
        scores = pair_scores(query_pair, key_pair, allowed)
        softmax_out = jnp.exp(scores - log_norms[pair_index][..., None])
        grad_weights = jnp.einsum(
            "thd,khd->htk", grad_pair, value_pair, preferred_element_type=jnp.float32
        )
        delta_row = jnp.sum(softmax_out * grad_weights, axis=-1, keepdims=True)
        grad_scores = (softmax_out * (grad_weights - delta_row)).astype(jnp.bfloat16)
        grad_query = (
            jnp.einsum("htk,khd->thd", grad_scores, key_pair, preferred_element_type=jnp.float32)
            * SCORE_SCALE
        )
        return (query_pair, grad_pair, softmax_out, grad_scores, grad_query, delta_row)

    def backward_pair(loop_carry, pair_index):
        query_pair, grad_pair, softmax_out, grad_scores, grad_query, delta_row = query_side_grads(
            pair_index
        )
        grad_key = (
            jnp.einsum("htk,thd->khd", grad_scores, query_pair, preferred_element_type=jnp.float32)
            * SCORE_SCALE
        )
        grad_value = jnp.einsum(
            "htk,thd->khd",
            softmax_out.astype(jnp.bfloat16),
            grad_pair,
            preferred_element_type=jnp.float32,
        )
        return (
            loop_carry,
            (
                grad_query.reshape(token_count, pair_width),
                grad_key.reshape(row_length, pair_width),
                grad_value.reshape(row_length, pair_width),
            ),
        )

    unused, (grad_query_pairs, grad_key_parts, grad_value_parts) = lax.scan(
        backward_pair, 0, jnp.arange(pair_count)
    )
    grad_key_pairs, grad_value_pairs = (
        lax.psum_scatter(
            grad_key_parts.astype(jnp.bfloat16), "seq", scatter_dimension=1, tiled=True
        ).astype(jnp.float32),
        lax.psum_scatter(
            grad_value_parts.astype(jnp.bfloat16), "seq", scatter_dimension=1, tiled=True
        ).astype(jnp.float32),
    )

    def heads_of(pairs_array):
        return jnp.transpose(pairs_array, (1, 0, 2)).reshape(token_count, head_count, HEAD_DIM)

    grad_qkv = jnp.concatenate(
        [
            unrotate(heads_of(grad_query_pairs), cos_table, sin_table).reshape(
                token_count, model_width
            ),
            unrotate(heads_of(grad_key_pairs), cos_table, sin_table).reshape(
                token_count, model_width
            ),
            heads_of(grad_value_pairs).reshape(token_count, model_width),
        ],
        axis=1,
    ).astype(jnp.bfloat16)
    grad_qkv_w = outer_sum(grad_qkv, attn_in)
    grad_attn_in = jnp.dot(grad_qkv, back_in[0], preferred_element_type=jnp.float32)
    grad_norm_one, grad_gain_one = norm_backward(grad_attn_in, normed_one, spread_one, back_rows[0])
    grad_input = grad_resid + grad_norm_one
    w_terms = jnp.stack([grad_qkv_w, grad_ffn_w])
    gain_terms = jnp.stack([grad_gain_one, grad_gain_two])
    summed_in, summed_ao, summed_fo, summed_gains = (
        lax.psum_scatter(w_terms, ("dp", "seq"), scatter_dimension=1, tiled=True),
        lax.psum_scatter(grad_ao_w, ("dp", "seq"), scatter_dimension=0, tiled=True),
        lax.psum_scatter(grad_fo_w, ("dp", "seq"), scatter_dimension=0, tiled=True),
        lax.psum_scatter(gain_terms, ("dp", "seq"), scatter_dimension=1, tiled=True),
    )
    new_moment = 0.9 * gain_moment + 0.1 * summed_gains
    new_second = 0.999 * gain_second + 0.001 * summed_gains * summed_gains
    new_gains = norm_gains - ADAM_RATE * new_moment / (jnp.sqrt(new_second) + 1e-08)
    whole_in, whole_ao, whole_fo = (
        lax.all_gather(summed_in.astype(jnp.bfloat16), ("dp", "seq"), axis=1, tiled=True).astype(
            summed_in.dtype
        ),
        lax.all_gather(summed_ao.astype(jnp.bfloat16), ("dp", "seq"), axis=0, tiled=True).astype(
            summed_ao.dtype
        ),
        lax.all_gather(summed_fo.astype(jnp.bfloat16), ("dp", "seq"), axis=0, tiled=True).astype(
            summed_fo.dtype
        ),
    )
    dev_index = lax.axis_index(("dp", "seq"))

    def refresh(grad_shard, grad_full, stat_left, stat_right, root_right):
        col_count = stat_right.shape[1]
        new_left = 0.5 * stat_left + 0.5 * jnp.einsum(
            "arn,amn->arm", grad_shard, grad_full, precision=HIGHEST
        )
        full_cols = lax.dynamic_slice_in_dim(grad_full, dev_index * col_count, col_count, 2)
        new_right = 0.5 * stat_right + 0.5 * jnp.einsum(
            "amc,amn->acn", full_cols, grad_full, precision=HIGHEST
        )
        applied = jnp.einsum("amn,acn->amc", grad_full, root_right, precision=HIGHEST)
        return (new_left, new_right, applied)

    left_in, right_in, applied_in = refresh(summed_in, whole_in, stat_l_in, stat_r_in, root_r_in)
    left_ao, right_ao, applied_ao = refresh(
        summed_ao[None], whole_ao[None], stat_l_ao[None], stat_r_ao[None], root_r_ao[None]
    )
    left_fo, right_fo, applied_fo = refresh(
        summed_fo[None], whole_fo[None], stat_l_fo[None], stat_r_fo[None], root_r_fo[None]
    )
    product_in, product_ao, product_fo = (
        lax.all_gather(applied_in.astype(jnp.bfloat16), ("dp", "seq"), axis=2, tiled=True).astype(
            applied_in.dtype
        ),
        lax.all_gather(applied_ao.astype(jnp.bfloat16), ("dp", "seq"), axis=2, tiled=True).astype(
            applied_ao.dtype
        ),
        lax.all_gather(applied_fo.astype(jnp.bfloat16), ("dp", "seq"), axis=2, tiled=True).astype(
            applied_fo.dtype
        ),
    )
    new_w_in = w_in - SHAMPOO_RATE * jnp.einsum(
        "arm,amn->arn", root_l_in, product_in, precision=HIGHEST
    )
    new_w_ao = (
        w_ao
        - SHAMPOO_RATE
        * jnp.einsum("arm,amn->arn", root_l_ao[None], product_ao, precision=HIGHEST)[0]
    )
    new_w_fo = (
        w_fo
        - SHAMPOO_RATE
        * jnp.einsum("arm,amn->arn", root_l_fo[None], product_fo, precision=HIGHEST)[0]
    )
    return (
        layer_out,
        grad_input,
        summed_in,
        summed_ao,
        summed_fo,
        summed_gains,
        new_moment,
        new_second,
        new_gains,
        left_in,
        right_in,
        left_ao[0],
        right_ao[0],
        left_fo[0],
        right_fo[0],
        new_w_in,
        new_w_ao,
        new_w_fo,
    )


def solution(mesh):
    in_specs = (
        P(("dp", "seq"), None),
        P(("dp", "seq"), None),
        P("dp", None),
        P("dp"),
        P(None, ("dp", "seq"), None),
        P(("dp", "seq"), None),
        P(("dp", "seq"), None),
        P(None, ("dp", "seq")),
        P(None, ("dp", "seq")),
        P(None, ("dp", "seq")),
        P(None, ("dp", "seq"), None),
        P(None, ("dp", "seq"), None),
        P(("dp", "seq"), None),
        P(("dp", "seq"), None),
        P(("dp", "seq"), None),
        P(("dp", "seq"), None),
        P(None, ("dp", "seq"), None),
        P(None, ("dp", "seq"), None),
        P(("dp", "seq"), None),
        P(("dp", "seq"), None),
        P(("dp", "seq"), None),
        P(("dp", "seq"), None),
    )
    out_specs = (
        P(("dp", "seq"), None),
        P(("dp", "seq"), None),
        P(None, ("dp", "seq"), None),
        P(("dp", "seq"), None),
        P(("dp", "seq"), None),
        P(None, ("dp", "seq")),
        P(None, ("dp", "seq")),
        P(None, ("dp", "seq")),
        P(None, ("dp", "seq")),
        P(None, ("dp", "seq"), None),
        P(None, ("dp", "seq"), None),
        P(("dp", "seq"), None),
        P(("dp", "seq"), None),
        P(("dp", "seq"), None),
        P(("dp", "seq"), None),
        P(None, ("dp", "seq"), None),
        P(("dp", "seq"), None),
        P(("dp", "seq"), None),
    )
    return jax.shard_map(body, mesh=mesh, in_specs=in_specs, out_specs=out_specs, check_vma=False)
```

profile of v0, /device:TPU:0, one launch (start us, length us, event | category | flops | bytes accessed | tf_op | source)
XLA Modules:
  0.0 1455.7 jit_solution(10830905520235701600)
XLA Ops:
  9.9 69.6 %all-gather.2 = bf16[32,24,2]{1,2,0:T(2,128)(2,1)S(1)} all-gather(bf16[1,24,2]{1,2,0:T(2,128)(2,1)S(1)} %convert_bitcast_fusion), channel_id=1, replica_groups=mesh['dp'=8,'seq'=4] {'dp','seq'}, dimensions={0}, use_global_device_ids=true | all-gather | bytes 3168 | tf_op jit(solution)/shard_map/all_gather | solution.py:142
  82.0 5.0 all-gather.16.cloned.1.call-done
  130.3 22.9 %all-gather.18.cloned.1.call-done = bf16[1920,768]{1,0:T(8,128)(2,1)} async-done(((bf16[480,768]{1,0:T(8,128)(2,1)}), bf16[1920,768]{1,0:T(8,128)(2,1)}) %all-gather.18.cloned.1.call-update) | async-done | bytes 2949136 | tf_op jit(solution)/shard_map/all_gather | solution.py:170
  153.1 4.9 copy.112
  158.0 56.3 %all-gather.20.cloned.1.call-done = bf16[1920,768]{1,0:T(8,128)(2,1)} async-done(((bf16[480,768]{1,0:T(8,128)(2,1)}), bf16[1920,768]{1,0:T(8,128)(2,1)}) %all-gather.20.cloned.1.call-update) | async-done | bytes 2949136 | tf_op jit(solution)/shard_map/all_gather | solution.py:169
  214.3 4.6 copy.114
  218.9 69.0 %while.30 = (s32[]{:T(128)}, bf16[6,480,128]{1,2,0:T(8,128)(2,1)}, f32[6,2,480]{2,1,0:T(2,128)}, s32[6]{0:T(128)S(1)}, bf16[1920,768]{0,1:T(8,128)(2,1)}, /*inde...) while((s32[]{:T(128)}, bf16[6,480,128]{1,2,0:T(8,128)(2,1)}, ...), condition=%wide.region_8.9_spmd.clone.clone, body=%wide.region_5.8_spmd.clone.sunk.clone | while | flops 497663040 | bytes 29544008 | solution.py:204
  292.3 6.1 fusion.19
  298.4 29.8 %all-gather.24.cloned.1.call-done = bf16[768,1152]{1,0:T(8,128)(2,1)} async-done(((bf16[24,1152]{1,0:T(8,128)(2,1)}), bf16[768,1152]{1,0:T(8,128)(2,1)}) %all-gather.24.cloned.1.call-update) | async-done | bytes 1769488 | tf_op jit(solution)/shard_map/all_gather | solution.py:141
  328.2 5.4 fusion.27
  333.6 5.5 multiply_reduce_fusion.1
  342.8 172.7 %while.31 = (s32[]{:T(128)}, f32[6,480,128]{1,2,0:T(8,128)}, bf16[6,1920,128]{1,2,0:T(8,128)(2,1)}, bf16[6,1920,128]{1,2,0:T(8,128)(2,1)}, s32[6]{0:T(128)S(1)},...) while((s32[]{:T(128)}, f32[6,480,128]{1,2,0:T(8,128)}, ...), condition=%wide.region_15.16_spmd.clone.clone, body=%wide.region_13.15_spmd.clone.sunk.clone | while | flops 1200475136 | bytes 80289944 | solution.py:282
  353.2 4.8 multiply_reduce_fusion.8
  358.0 5.8 multiply_convert_fusion.8
  382.0 4.8 multiply_reduce_fusion.8
  386.8 5.8 multiply_convert_fusion.8
  410.8 4.8 multiply_reduce_fusion.8
  415.6 5.8 multiply_convert_fusion.8
  439.5 4.8 multiply_reduce_fusion.8
  444.3 5.8 multiply_convert_fusion.8
  468.3 4.8 multiply_reduce_fusion.8
  473.1 5.8 multiply_convert_fusion.8
  497.1 4.8 multiply_reduce_fusion.8
  501.9 5.8 multiply_convert_fusion.8
  515.5 6.0 copy.123
  521.6 4.4 copy.137
  526.1 6.0 copy.125
  532.1 4.4 copy.136
  544.6 7.1 convolution_bitcast_fusion
  551.8 30.6 %reduce-scatter.15.cloned.1.call-done = bf16[480,768]{1,0:T(8,128)(2,1)} async-done(((bf16[1920,768]{1,0:T(8,128)(2,1)}), bf16[480,768]{1,0:T(8,128)(2,1)}) %reduce-scatter.15.cloned.1.call-update) | async-done | bytes 737296
  592.1 49.9 %reduce-scatter.17.cloned.1.call-done = bf16[480,768]{1,0:T(8,128)(2,1)} async-done(((bf16[1920,768]{1,0:T(8,128)(2,1)}), bf16[480,768]{1,0:T(8,128)(2,1)}) %reduce-scatter.17.cloned.1.call-update) | async-done | bytes 737296
  652.2 5.1 convolution_bitcast_fusion.1
  657.3 11.1 pad_maximum_fusion
  668.5 78.2 %reduce-scatter.13.cloned.1.call-done = f32[24,768]{1,0:T(8,128)} async-done(((f32[768,768]{1,0:T(8,128)}), f32[24,768]{1,0:T(8,128)}) %reduce-scatter.13.cloned.1.call-update) | async-done | bytes 73744 | tf_op jit(solution)/shard_map/reduce_scatter | solution.py:317
  748.6 142.7 %all-reduce.4.cloned.1.call-done = f32[768,1152]{0,1:T(8,128)} async-done(((f32[768,1152]{0,1:T(8,128)}), f32[768,1152]{0,1:T(8,128)}) %all-reduce.4.cloned.1.call-update) | async-done | bytes 3538960
  895.6 164.0 %reduce-scatter.11.cloned.1.call-done = f32[2,72,768]{2,1,0:T(8,128)} async-done(((f32[2,2304,768]{2,1,0:T(8,128)}), f32[2,72,768]{2,1,0:T(8,128)}) %reduce-scatter.11.cloned.1.call-update) | async-done | bytes 442384 | tf_op jit(solution)/shard_map/reduce_scatter | solution.py:316
  1061.4 54.6 %all-gather.28.cloned.1.call-done = bf16[768,768]{1,0:T(8,128)(2,1)} async-done(((bf16[24,768]{1,0:T(8,128)(2,1)}), bf16[768,768]{1,0:T(8,128)(2,1)}) %all-gather.28.cloned.1.call-update) | async-done | bytes 1179664 | tf_op jit(solution)/shard_map/all_gather | solution.py:328
  1119.0 54.8 %all-gather.30.cloned.1.call-done = bf16[768,1152]{1,0:T(8,128)(2,1)} async-done(((bf16[24,1152]{1,0:T(8,128)(2,1)}), bf16[768,1152]{1,0:T(8,128)(2,1)}) %all-gather.30.cloned.1.call-update) | async-done | bytes 1769488 | tf_op jit(solution)/shard_map/all_gather | solution.py:331
  1177.5 71.6 %all-gather.26.cloned.1.call-done = bf16[2,2304,768]{2,1,0:T(8,128)(2,1)} async-done(((bf16[2,72,768]{2,1,0:T(8,128)(2,1)}), bf16[2,2304,768]{2,1,0:T(8,128)(2,1)}) %all-gather.26.cloned.1.call-update) | async-done | bytes 7077904 | tf_op jit(solution)/shard_map/all_gather | solution.py:325
  1249.1 9.3 convolution_convert_fusion
  1258.5 4.4 add_convert_fusion
  1269.2 5.3 fusion.43
  1274.5 39.9 %all-reduce.1 = f32[2,768]{1,0:T(2,128)S(1)} all-reduce(f32[2,768]{1,0:T(2,128)S(1)} %pad_maximum_fusion.10), channel_id=9, replica_groups=mesh['dp'=8,'seq'=4] {'dp','seq'}, use_global_device_ids=true, to_apply=%region_25.26.clone | all-reduce | flops 1536 | bytes 12288
  1321.4 42.0 %all-gather.36.cloned.1.call-done = bf16[32,36,768]{2,1,0:T(8,128)(2,1)} async-done(((bf16[1,36,768]{2,1,0:T(8,128)(2,1)}), bf16[32,36,768]{2,1,0:T(8,128)(2,1)}) %all-gather.36.cloned.1.call-update) | async-done | bytes 1769488 | tf_op jit(solution)/shard_map/all_gather | solution.py:363
  1368.0 6.2 fusion.51
  1374.2 10.8 fusion.15
  1385.0 53.4 %all-gather.32.cloned.1.call-done = bf16[2,2304,768]{1,2,0:T(8,128)(2,1)} async-done(((bf16[2,2304,24]{1,2,0:T(8,128)(2,1)}), bf16[2,2304,768]{1,2,0:T(8,128)(2,1)}) %all-gather.32.cloned.1.call-update) | async-done | bytes 7077904 | tf_op jit(solution)/shard_map/all_gather | solution.py:357
  1438.4 10.3 fusion.45
  (405 shorter events, 274.3 us)
Async XLA Ops:
  7.2 1431.2 %copy-start = (f32[2,72,2304]{2,1,0:T(8,128)S(1)}, f32[2,72,2304]{2,1,0:T(8,128)}, u32[]{:S(2)}) copy-start(f32[2,72,2304]{2,1,0:T(8,128)} %param.42) | copy-start | bytes 3981316
  7.2 74.4 %copy-start.6 = (bf16[480,768]{1,0:T(8,128)(2,1)S(1)}, bf16[480,768]{1,0:T(8,128)(2,1)}, u32[]{:S(2)}) copy-start(bf16[480,768]{1,0:T(8,128)(2,1)} %param.26) | copy-start | bytes 2211844
  7.2 79.9 %all-gather.16.cloned.1.call-start = ((), (), s32[]{:S(2)}) async-start(), calls=%async_computation.4 | async-start | bytes 7299072 | tf_op jit(solution)/shard_map/all_gather | solution.py:139
  9.1 144.0 %all-gather.18.cloned.1.call-start = ((), (), s32[]{:S(2)}) async-start(), calls=%async_computation.5 | async-start | bytes 3686400 | tf_op jit(solution)/shard_map/all_gather | solution.py:170
  80.3 10.8 copy-start.51
  81.7 9.4 copy-start.46
  82.0 9.1 copy-start.56
  94.1 120.1 %all-gather.20.cloned.1.call-start = ((), (), s32[]{:S(2)}) async-start(), calls=%async_computation.6 | async-start | bytes 3686400 | tf_op jit(solution)/shard_map/all_gather | solution.py:169
  123.9 164.0 %all-gather.22.cloned.1.call-start = ((), (), s32[]{:S(2)}) async-start(), calls=%async_computation.7 | async-start | bytes 1216512 | tf_op jit(solution)/shard_map/all_gather | solution.py:140
  125.5 202.7 %all-gather.24.cloned.1.call-start = ((), (), s32[]{:S(2)}) async-start(), calls=%async_computation.8 | async-start | bytes 1824768 | tf_op jit(solution)/shard_map/all_gather | solution.py:141
  127.1 455.3 %reduce-scatter.15.cloned.1.call-start = ((), (), s32[]{:S(2)}) async-start(), calls=%async_computation.17 | async-start | bytes 3686400
  291.2 42.3 %copy-start.12 = (f32[480,768]{1,0:T(8,128)}, f32[480,768]{1,0:T(8,128)S(1)}, u32[]{:S(2)}) copy-start(f32[480,768]{1,0:T(8,128)S(1)} %get-tuple-element.496) | copy-start | bytes 4423684
  292.3 35.9 %copy-start.15 = (bf16[480,768]{1,0:T(8,128)(2,1)S(1)}, bf16[480,768]{1,0:T(8,128)(2,1)}, u32[]{:S(2)}) copy-start(bf16[480,768]{1,0:T(8,128)(2,1)} %param.27) | copy-start | bytes 2211844
  328.2 5.4 copy-start.49
  328.2 5.4 copy-start.54
  328.2 5.4 copy-start.59
  333.5 5.6 copy-start.67
  333.6 5.6 copy-start.68
  333.6 5.6 copy-start.16
  526.0 115.9 %reduce-scatter.17.cloned.1.call-start = ((), (), s32[]{:S(2)}) async-start(), calls=%async_computation.18 | async-start | bytes 3686400
  536.6 210.2 %reduce-scatter.13.cloned.1.call-start = ((), (), s32[]{:S(2)}) async-start(), calls=%async_computation.10 | async-start | bytes 2433024 | tf_op jit(solution)/shard_map/reduce_scatter | solution.py:317
  540.2 351.0 %all-reduce.4.cloned.1.call-start = ((), (), s32[]{:S(2)}) async-start(), calls=%async_computation.19 | async-start | bytes 7077888
  540.2 4.4 copy-start.50
  540.3 4.4 copy-start.55
  540.3 4.4 copy-start.60
  551.8 507.8 %reduce-scatter.11.cloned.1.call-start = ((), (), s32[]{:S(2)}) async-start(), calls=%async_computation.9 | async-start | bytes 14598144 | tf_op jit(solution)/shard_map/reduce_scatter | solution.py:316
  668.5 447.5 %copy-start.40 = (f32[24,768]{1,0:T(8,128)S(1)}, f32[24,768]{1,0:T(8,128)}, u32[]{:S(2)}) copy-start(f32[24,768]{1,0:T(8,128)} %param.45) | copy-start | bytes 221188
  668.5 447.4 %all-gather.28.cloned.1.call-start = ((), (), s32[]{:S(2)}) async-start(), calls=%async_computation.12 | async-start | bytes 1216512 | tf_op jit(solution)/shard_map/all_gather | solution.py:328
  748.3 425.5 %all-gather.30.cloned.1.call-start = ((), (), s32[]{:S(2)}) async-start(), calls=%async_computation.13 | async-start | bytes 1824768 | tf_op jit(solution)/shard_map/all_gather | solution.py:331
  893.5 280.3 %copy-start.38 = (f32[36,1152]{1,0:T(8,128)S(1)}, f32[36,1152]{1,0:T(8,128)}, u32[]{:S(2)}) copy-start(f32[36,1152]{1,0:T(8,128)} %param.47) | copy-start | bytes 497668
  894.8 282.6 %copy-start.32 = (f32[24,1152]{1,0:T(8,128)}, f32[24,1152]{1,0:T(8,128)S(1)}, u32[]{:S(2)}) copy-start(f32[24,1152]{1,0:T(8,128)S(1)} %copy.121) | copy-start | bytes 331780
  895.5 353.6 %all-gather.26.cloned.1.call-start = ((), (), s32[]{:S(2)}) async-start(), calls=%async_computation.11 | async-start | bytes 7299072 | tf_op jit(solution)/shard_map/all_gather | solution.py:325
  1061.3 187.8 %copy-start.39 = (f32[2,24,768]{2,1,0:T(8,128)S(1)}, f32[2,24,768]{2,1,0:T(8,128)}, u32[]{:S(2)}) copy-start(f32[2,24,768]{2,1,0:T(8,128)} %param.43) | copy-start | bytes 442372
  1061.3 257.1 %all-gather.34.cloned.1.call-start = ((), (), s32[]{:S(2)}) async-start(), calls=%async_computation.15 | async-start | bytes 1216512 | tf_op jit(solution)/shard_map/all_gather | solution.py:360
  1118.9 244.5 %all-gather.36.cloned.1.call-start = ((), (), s32[]{:S(2)}) async-start(), calls=%async_computation.16 | async-start | bytes 2027520 | tf_op jit(solution)/shard_map/all_gather | solution.py:363
  1177.4 81.0 %copy-start.61 = (f32[768]{0:T(1024)S(1)}, f32[768]{0:T(1024)}, u32[]{:S(2)}) copy-start(f32[768]{0:T(1024)} %get-tuple-element.402) | copy-start | bytes 9220
  1177.5 260.9 %all-gather.32.cloned.1.call-start = ((), (), s32[]{:S(2)}) async-start(), calls=%async_computation.14 | async-start | bytes 7299072 | tf_op jit(solution)/shard_map/all_gather | solution.py:357
  1258.4 4.5 copy-start.2
  1258.4 4.5 copy-start.37
  1264.2 5.0 copy-start.29
  1269.2 45.3 %copy-start.62 = (f32[2,24]{1,0:T(2,128)S(1)}, f32[2,24]{1,0:T(2,128)}, u32[]{:S(2)}) copy-start(f32[2,24]{1,0:T(2,128)} %param.33) | copy-start | bytes 580
  1269.2 45.2 %copy-start.63 = (f32[2,24]{1,0:T(2,128)S(1)}, f32[2,24]{1,0:T(2,128)}, u32[]{:S(2)}) copy-start(f32[2,24]{1,0:T(2,128)} %param.35) | copy-start | bytes 580
  1269.2 45.2 %copy-start.64 = (f32[2,24]{1,0:T(2,128)S(1)}, f32[2,24]{1,0:T(2,128)}, u32[]{:S(2)}) copy-start(f32[2,24]{1,0:T(2,128)} %param.34) | copy-start | bytes 580
  1321.4 44.5 %copy-start.31 = (f32[24,1152]{1,0:T(8,128)S(1)}, f32[24,1152]{1,0:T(8,128)}, u32[]{:S(2)}) copy-start(f32[24,1152]{1,0:T(8,128)} %param.32) | copy-start | bytes 331780
  1321.4 44.5 %copy-start.45 = (f32[24,768]{1,0:T(8,128)S(1)}, f32[24,768]{1,0:T(8,128)}, u32[]{:S(2)}) copy-start(f32[24,768]{1,0:T(8,128)} %param.46) | copy-start | bytes 221188
  1368.0 6.2 copy-start.18
  1368.0 6.2 copy-start.19
  1374.2 64.2 %copy-start.17 = (f32[2,72,768]{2,1,0:T(8,128)S(1)}, f32[2,72,768]{2,1,0:T(8,128)}, u32[]{:S(2)}) copy-start(f32[2,72,768]{2,1,0:T(8,128)} %param.30) | copy-start | bytes 1327108
  (42 other events, 96.5 us)
Sparse Core Ops, SparseCore 0:
  11.7 75.3 all-gather.15
  94.3 58.8 all-gather.17
  155.3 58.9 all-gather.19
  217.5 52.7 all-gather.21
  273.6 54.5 all-gather.23
  526.1 56.2 reduce-scatter.14
  584.8 57.0 reduce-scatter.16
  647.8 98.9 reduce-scatter.12
  753.3 137.8 all-reduce.3
  897.6 161.9 reduce-scatter.10
  1063.0 52.9 all-gather.27
  1119.2 54.5 all-gather.29
  1177.4 71.6 all-gather.25
  1252.3 52.5 all-gather.33
  1308.2 55.1 all-gather.35
  1366.9 71.4 all-gather.31
where the time goes:
time: 1460 us
  waiting for transfers between devices  856 us (59%)
  matrix products  206 us (14%)
  local copies, waits for them, and re-layouts  135 us (9%)
  other arithmetic  113 us (8%)
  blocking collectives  109 us (7%)
  loops' own time  20 us (1%)
  between operations  15.8 us (1%)
    unnamed x19, waiting for transfers between devices  223 us
    reduce_scatter x1, waiting for transfers between devices, body(): lax.psum_scatter(w_terms, ('dp', 'seq'), scatter_dimension=1, tiled=True)  164 us
    reduce_scatter x1, waiting for transfers between devices, body(): lax.psum_scatter(grad_ao_w, ('dp', 'seq'), scatter_dimension=0, tiled=True)  78.2 us
    all_gather x1, waiting for transfers between devices, body(): lax.all_gather(summed_in.astype(jnp.bfloat16), ('dp', 'seq'), axis=1, til...  71.6 us
    all_gather x1, blocking collectives, body(): lax.all_gather(low_weights[3], ('dp', 'seq'), axis=1, tiled=True)  69.6 us
    all_gather x1, waiting for transfers between devices, body(): lax.all_gather(key_low, 'seq', axis=0, tiled=True)  56.3 us
    all_gather x1, waiting for transfers between devices, body(): lax.all_gather(summed_fo.astype(jnp.bfloat16), ('dp', 'seq'), axis=0, til...  54.8 us
    unnamed x150, local copies, waits for them, and re-layouts  54.6 us
  transfers between devices with their start and end apart: 16, of which 14 were waited for; matrix products, arithmetic and copies ran while one was open for 17% of the time, Pallas kernels for 0%

commit v1 on v0

--- a/solution.py
+++ b/solution.py
@@ -64,7 +64,10 @@
 
 
 def doc_tables(lengths_row, pad_count, row_length):
-    doc_ends = jnp.cumsum(lengths_row)
+    doc_order = jnp.arange(lengths_row.shape[0], dtype=jnp.int32)
+    doc_ends = jnp.sum(
+        jnp.where(doc_order[:, None] >= doc_order[None, :], lengths_row[None, :], 0), axis=1
+    )
     starts = doc_ends - lengths_row
     places = jnp.arange(row_length, dtype=jnp.int32)
     segment = jnp.sum((places[:, None] >= doc_ends[None, :]).astype(jnp.int32), axis=1)

time: 1460 us -> 1460 us (level)
  no operation moved by 1% of the time
where the time goes in v1:
time: 1460 us
  waiting for transfers between devices  856 us (59%)
  matrix products  206 us (14%)
  local copies, waits for them, and re-layouts  135 us (9%)
  other arithmetic  113 us (8%)
  blocking collectives  109 us (7%)
  loops' own time  20 us (1%)
  between operations  15.8 us (1%)
    unnamed x19, waiting for transfers between devices  223 us
    reduce_scatter x1, waiting for transfers between devices, body(): lax.psum_scatter(w_terms, ('dp', 'seq'), scatter_dimension=1, tiled=True)  164 us
    reduce_scatter x1, waiting for transfers between devices, body(): lax.psum_scatter(grad_ao_w, ('dp', 'seq'), scatter_dimension=0, tiled=True)  78.2 us
    all_gather x1, waiting for transfers between devices, body(): lax.all_gather(summed_in.astype(jnp.bfloat16), ('dp', 'seq'), axis=1, til...  71.6 us
    all_gather x1, blocking collectives, body(): lax.all_gather(low_weights[3], ('dp', 'seq'), axis=1, tiled=True)  69.6 us
    all_gather x1, waiting for transfers between devices, body(): lax.all_gather(key_low, 'seq', axis=0, tiled=True)  56.3 us
    all_gather x1, waiting for transfers between devices, body(): lax.all_gather(summed_fo.astype(jnp.bfloat16), ('dp', 'seq'), axis=0, til...  54.8 us
    unnamed x150, local copies, waits for them, and re-layouts  54.6 us
  transfers between devices with their start and end apart: 16, of which 14 were waited for; matrix products, arithmetic and copies ran while one was open for 17% of the time, Pallas kernels for 0%

profile of v1, /device:TPU:0, one launch (start us, length us, event | category | flops | bytes accessed | tf_op | source)
XLA Modules:
  0.0 1455.7 jit_solution(311089714665160988)
XLA Ops:
  9.9 69.6 %all-gather.2 = bf16[32,24,2]{1,2,0:T(2,128)(2,1)S(1)} all-gather(bf16[1,24,2]{1,2,0:T(2,128)(2,1)S(1)} %convert_bitcast_fusion), channel_id=1, replica_groups=mesh['dp'=8,'seq'=4] {'dp','seq'}, dimensions={0}, use_global_device_ids=true | all-gather | bytes 3168 | tf_op jit(solution)/shard_map/all_gather | solution.py:145
  82.0 5.0 all-gather.16.cloned.1.call-done
  130.2 22.9 %all-gather.18.cloned.1.call-done = bf16[1920,768]{1,0:T(8,128)(2,1)} async-done(((bf16[480,768]{1,0:T(8,128)(2,1)}), bf16[1920,768]{1,0:T(8,128)(2,1)}) %all-gather.18.cloned.1.call-update) | async-done | bytes 2949136 | tf_op jit(solution)/shard_map/all_gather | solution.py:173
  153.1 4.9 copy.112
  158.0 56.3 %all-gather.20.cloned.1.call-done = bf16[1920,768]{1,0:T(8,128)(2,1)} async-done(((bf16[480,768]{1,0:T(8,128)(2,1)}), bf16[1920,768]{1,0:T(8,128)(2,1)}) %all-gather.20.cloned.1.call-update) | async-done | bytes 2949136 | tf_op jit(solution)/shard_map/all_gather | solution.py:172
  214.3 4.6 copy.114
  218.9 69.0 %while.30 = (s32[]{:T(128)}, bf16[6,480,128]{1,2,0:T(8,128)(2,1)}, f32[6,2,480]{2,1,0:T(2,128)}, s32[6]{0:T(128)S(1)}, bf16[1920,768]{0,1:T(8,128)(2,1)}, /*inde...) while((s32[]{:T(128)}, bf16[6,480,128]{1,2,0:T(8,128)(2,1)}, ...), condition=%wide.region_8.9_spmd.clone.clone, body=%wide.region_5.8_spmd.clone.sunk.clone | while | flops 497663040 | bytes 29544008 | solution.py:207
  292.3 6.1 fusion.19
  298.4 29.8 %all-gather.24.cloned.1.call-done = bf16[768,1152]{1,0:T(8,128)(2,1)} async-done(((bf16[24,1152]{1,0:T(8,128)(2,1)}), bf16[768,1152]{1,0:T(8,128)(2,1)}) %all-gather.24.cloned.1.call-update) | async-done | bytes 1769488 | tf_op jit(solution)/shard_map/all_gather | solution.py:144
  328.2 5.4 fusion.27
  333.6 5.5 multiply_reduce_fusion.1
  342.8 172.7 %while.31 = (s32[]{:T(128)}, f32[6,480,128]{1,2,0:T(8,128)}, bf16[6,1920,128]{1,2,0:T(8,128)(2,1)}, bf16[6,1920,128]{1,2,0:T(8,128)(2,1)}, s32[6]{0:T(128)S(1)},...) while((s32[]{:T(128)}, f32[6,480,128]{1,2,0:T(8,128)}, ...), condition=%wide.region_15.16_spmd.clone.clone, body=%wide.region_13.15_spmd.clone.sunk.clone | while | flops 1200475136 | bytes 80289944 | solution.py:285
  353.2 4.8 multiply_reduce_fusion.8
  358.0 5.8 multiply_convert_fusion.8
  382.0 4.8 multiply_reduce_fusion.8
  386.8 5.8 multiply_convert_fusion.8
  410.8 4.8 multiply_reduce_fusion.8
  415.6 5.8 multiply_convert_fusion.8
  439.5 4.8 multiply_reduce_fusion.8
  444.3 5.8 multiply_convert_fusion.8
  468.3 4.8 multiply_reduce_fusion.8
  473.1 5.8 multiply_convert_fusion.8
  497.1 4.8 multiply_reduce_fusion.8
  501.9 5.8 multiply_convert_fusion.8
  515.5 6.0 copy.123
  521.6 4.4 copy.137
  526.1 6.0 copy.125
  532.1 4.4 copy.136
  544.6 7.1 convolution_bitcast_fusion
  551.8 30.6 %reduce-scatter.15.cloned.1.call-done = bf16[480,768]{1,0:T(8,128)(2,1)} async-done(((bf16[1920,768]{1,0:T(8,128)(2,1)}), bf16[480,768]{1,0:T(8,128)(2,1)}) %reduce-scatter.15.cloned.1.call-update) | async-done | bytes 737296
  592.1 49.9 %reduce-scatter.17.cloned.1.call-done = bf16[480,768]{1,0:T(8,128)(2,1)} async-done(((bf16[1920,768]{1,0:T(8,128)(2,1)}), bf16[480,768]{1,0:T(8,128)(2,1)}) %reduce-scatter.17.cloned.1.call-update) | async-done | bytes 737296
  652.2 5.1 convolution_bitcast_fusion.1
  657.3 11.1 pad_maximum_fusion
  668.5 78.2 %reduce-scatter.13.cloned.1.call-done = f32[24,768]{1,0:T(8,128)} async-done(((f32[768,768]{1,0:T(8,128)}), f32[24,768]{1,0:T(8,128)}) %reduce-scatter.13.cloned.1.call-update) | async-done | bytes 73744 | tf_op jit(solution)/shard_map/reduce_scatter | solution.py:320
  748.6 142.7 %all-reduce.4.cloned.1.call-done = f32[768,1152]{0,1:T(8,128)} async-done(((f32[768,1152]{0,1:T(8,128)}), f32[768,1152]{0,1:T(8,128)}) %all-reduce.4.cloned.1.call-update) | async-done | bytes 3538960
  895.6 164.0 %reduce-scatter.11.cloned.1.call-done = f32[2,72,768]{2,1,0:T(8,128)} async-done(((f32[2,2304,768]{2,1,0:T(8,128)}), f32[2,72,768]{2,1,0:T(8,128)}) %reduce-scatter.11.cloned.1.call-update) | async-done | bytes 442384 | tf_op jit(solution)/shard_map/reduce_scatter | solution.py:319
  1061.4 54.6 %all-gather.28.cloned.1.call-done = bf16[768,768]{1,0:T(8,128)(2,1)} async-done(((bf16[24,768]{1,0:T(8,128)(2,1)}), bf16[768,768]{1,0:T(8,128)(2,1)}) %all-gather.28.cloned.1.call-update) | async-done | bytes 1179664 | tf_op jit(solution)/shard_map/all_gather | solution.py:331
  1119.0 54.8 %all-gather.30.cloned.1.call-done = bf16[768,1152]{1,0:T(8,128)(2,1)} async-done(((bf16[24,1152]{1,0:T(8,128)(2,1)}), bf16[768,1152]{1,0:T(8,128)(2,1)}) %all-gather.30.cloned.1.call-update) | async-done | bytes 1769488 | tf_op jit(solution)/shard_map/all_gather | solution.py:334
  1177.5 71.6 %all-gather.26.cloned.1.call-done = bf16[2,2304,768]{2,1,0:T(8,128)(2,1)} async-done(((bf16[2,72,768]{2,1,0:T(8,128)(2,1)}), bf16[2,2304,768]{2,1,0:T(8,128)(2,1)}) %all-gather.26.cloned.1.call-update) | async-done | bytes 7077904 | tf_op jit(solution)/shard_map/all_gather | solution.py:328
  1249.1 9.3 convolution_convert_fusion
  1258.5 4.4 add_convert_fusion
  1269.2 5.3 fusion.43
  1274.5 39.9 %all-reduce.1 = f32[2,768]{1,0:T(2,128)S(1)} all-reduce(f32[2,768]{1,0:T(2,128)S(1)} %pad_maximum_fusion.10), channel_id=9, replica_groups=mesh['dp'=8,'seq'=4] {'dp','seq'}, use_global_device_ids=true, to_apply=%region_25.26.clone | all-reduce | flops 1536 | bytes 12288
  1321.4 42.0 %all-gather.36.cloned.1.call-done = bf16[32,36,768]{2,1,0:T(8,128)(2,1)} async-done(((bf16[1,36,768]{2,1,0:T(8,128)(2,1)}), bf16[32,36,768]{2,1,0:T(8,128)(2,1)}) %all-gather.36.cloned.1.call-update) | async-done | bytes 1769488 | tf_op jit(solution)/shard_map/all_gather | solution.py:366
  1368.0 6.2 fusion.51
  1374.2 10.8 fusion.15
  1385.0 53.4 %all-gather.32.cloned.1.call-done = bf16[2,2304,768]{1,2,0:T(8,128)(2,1)} async-done(((bf16[2,2304,24]{1,2,0:T(8,128)(2,1)}), bf16[2,2304,768]{1,2,0:T(8,128)(2,1)}) %all-gather.32.cloned.1.call-update) | async-done | bytes 7077904 | tf_op jit(solution)/shard_map/all_gather | solution.py:360
  1438.4 10.3 fusion.45
  (405 shorter events, 274.2 us)
Async XLA Ops:
  7.2 1431.2 %copy-start = (f32[2,72,2304]{2,1,0:T(8,128)S(1)}, f32[2,72,2304]{2,1,0:T(8,128)}, u32[]{:S(2)}) copy-start(f32[2,72,2304]{2,1,0:T(8,128)} %param.42) | copy-start | bytes 3981316
  7.2 74.4 %copy-start.6 = (bf16[480,768]{1,0:T(8,128)(2,1)S(1)}, bf16[480,768]{1,0:T(8,128)(2,1)}, u32[]{:S(2)}) copy-start(bf16[480,768]{1,0:T(8,128)(2,1)} %param.26) | copy-start | bytes 2211844
  7.2 79.9 %all-gather.16.cloned.1.call-start = ((), (), s32[]{:S(2)}) async-start(), calls=%async_computation.4 | async-start | bytes 7299072 | tf_op jit(solution)/shard_map/all_gather | solution.py:142
  9.1 144.0 %all-gather.18.cloned.1.call-start = ((), (), s32[]{:S(2)}) async-start(), calls=%async_computation.5 | async-start | bytes 3686400 | tf_op jit(solution)/shard_map/all_gather | solution.py:173
  80.3 10.8 copy-start.51
  81.7 9.4 copy-start.46
  82.0 9.1 copy-start.56
  94.1 120.1 %all-gather.20.cloned.1.call-start = ((), (), s32[]{:S(2)}) async-start(), calls=%async_computation.6 | async-start | bytes 3686400 | tf_op jit(solution)/shard_map/all_gather | solution.py:172
  123.9 164.0 %all-gather.22.cloned.1.call-start = ((), (), s32[]{:S(2)}) async-start(), calls=%async_computation.7 | async-start | bytes 1216512 | tf_op jit(solution)/shard_map/all_gather | solution.py:143
  125.4 202.7 %all-gather.24.cloned.1.call-start = ((), (), s32[]{:S(2)}) async-start(), calls=%async_computation.8 | async-start | bytes 1824768 | tf_op jit(solution)/shard_map/all_gather | solution.py:144
  127.0 455.4 %reduce-scatter.15.cloned.1.call-start = ((), (), s32[]{:S(2)}) async-start(), calls=%async_computation.17 | async-start | bytes 3686400
  291.2 42.3 %copy-start.12 = (f32[480,768]{1,0:T(8,128)}, f32[480,768]{1,0:T(8,128)S(1)}, u32[]{:S(2)}) copy-start(f32[480,768]{1,0:T(8,128)S(1)} %get-tuple-element.496) | copy-start | bytes 4423684
  292.3 35.9 %copy-start.15 = (bf16[480,768]{1,0:T(8,128)(2,1)S(1)}, bf16[480,768]{1,0:T(8,128)(2,1)}, u32[]{:S(2)}) copy-start(bf16[480,768]{1,0:T(8,128)(2,1)} %param.27) | copy-start | bytes 2211844
  328.2 5.4 copy-start.49
  328.2 5.4 copy-start.54
  328.2 5.4 copy-start.59
  333.5 5.6 copy-start.67
  333.6 5.6 copy-start.68
  333.6 5.6 copy-start.16
  526.0 115.9 %reduce-scatter.17.cloned.1.call-start = ((), (), s32[]{:S(2)}) async-start(), calls=%async_computation.18 | async-start | bytes 3686400
  536.6 210.2 %reduce-scatter.13.cloned.1.call-start = ((), (), s32[]{:S(2)}) async-start(), calls=%async_computation.10 | async-start | bytes 2433024 | tf_op jit(solution)/shard_map/reduce_scatter | solution.py:320
  540.2 351.0 %all-reduce.4.cloned.1.call-start = ((), (), s32[]{:S(2)}) async-start(), calls=%async_computation.19 | async-start | bytes 7077888
  540.2 4.4 copy-start.50
  540.3 4.4 copy-start.55
  540.3 4.4 copy-start.60
  551.8 507.8 %reduce-scatter.11.cloned.1.call-start = ((), (), s32[]{:S(2)}) async-start(), calls=%async_computation.9 | async-start | bytes 14598144 | tf_op jit(solution)/shard_map/reduce_scatter | solution.py:319
  668.5 447.5 %copy-start.40 = (f32[24,768]{1,0:T(8,128)S(1)}, f32[24,768]{1,0:T(8,128)}, u32[]{:S(2)}) copy-start(f32[24,768]{1,0:T(8,128)} %param.45) | copy-start | bytes 221188
  668.5 447.4 %all-gather.28.cloned.1.call-start = ((), (), s32[]{:S(2)}) async-start(), calls=%async_computation.12 | async-start | bytes 1216512 | tf_op jit(solution)/shard_map/all_gather | solution.py:331
  748.3 425.5 %all-gather.30.cloned.1.call-start = ((), (), s32[]{:S(2)}) async-start(), calls=%async_computation.13 | async-start | bytes 1824768 | tf_op jit(solution)/shard_map/all_gather | solution.py:334
  893.5 280.3 %copy-start.38 = (f32[36,1152]{1,0:T(8,128)S(1)}, f32[36,1152]{1,0:T(8,128)}, u32[]{:S(2)}) copy-start(f32[36,1152]{1,0:T(8,128)} %param.47) | copy-start | bytes 497668
  894.8 282.6 %copy-start.32 = (f32[24,1152]{1,0:T(8,128)}, f32[24,1152]{1,0:T(8,128)S(1)}, u32[]{:S(2)}) copy-start(f32[24,1152]{1,0:T(8,128)S(1)} %copy.121) | copy-start | bytes 331780
  895.5 353.6 %all-gather.26.cloned.1.call-start = ((), (), s32[]{:S(2)}) async-start(), calls=%async_computation.11 | async-start | bytes 7299072 | tf_op jit(solution)/shard_map/all_gather | solution.py:328
  1061.3 187.8 %copy-start.39 = (f32[2,24,768]{2,1,0:T(8,128)S(1)}, f32[2,24,768]{2,1,0:T(8,128)}, u32[]{:S(2)}) copy-start(f32[2,24,768]{2,1,0:T(8,128)} %param.43) | copy-start | bytes 442372
  1061.3 257.1 %all-gather.34.cloned.1.call-start = ((), (), s32[]{:S(2)}) async-start(), calls=%async_computation.15 | async-start | bytes 1216512 | tf_op jit(solution)/shard_map/all_gather | solution.py:363
  1118.9 244.5 %all-gather.36.cloned.1.call-start = ((), (), s32[]{:S(2)}) async-start(), calls=%async_computation.16 | async-start | bytes 2027520 | tf_op jit(solution)/shard_map/all_gather | solution.py:366
  1177.4 81.0 %copy-start.61 = (f32[768]{0:T(1024)S(1)}, f32[768]{0:T(1024)}, u32[]{:S(2)}) copy-start(f32[768]{0:T(1024)} %get-tuple-element.402) | copy-start | bytes 9220
  1177.5 260.9 %all-gather.32.cloned.1.call-start = ((), (), s32[]{:S(2)}) async-start(), calls=%async_computation.14 | async-start | bytes 7299072 | tf_op jit(solution)/shard_map/all_gather | solution.py:360
  1258.4 4.5 copy-start.2
  1258.4 4.5 copy-start.37
  1264.2 5.0 copy-start.29
  1269.2 45.3 %copy-start.62 = (f32[2,24]{1,0:T(2,128)S(1)}, f32[2,24]{1,0:T(2,128)}, u32[]{:S(2)}) copy-start(f32[2,24]{1,0:T(2,128)} %param.33) | copy-start | bytes 580
  1269.2 45.2 %copy-start.63 = (f32[2,24]{1,0:T(2,128)S(1)}, f32[2,24]{1,0:T(2,128)}, u32[]{:S(2)}) copy-start(f32[2,24]{1,0:T(2,128)} %param.35) | copy-start | bytes 580
  1269.2 45.2 %copy-start.64 = (f32[2,24]{1,0:T(2,128)S(1)}, f32[2,24]{1,0:T(2,128)}, u32[]{:S(2)}) copy-start(f32[2,24]{1,0:T(2,128)} %param.34) | copy-start | bytes 580
  1321.4 44.5 %copy-start.31 = (f32[24,1152]{1,0:T(8,128)S(1)}, f32[24,1152]{1,0:T(8,128)}, u32[]{:S(2)}) copy-start(f32[24,1152]{1,0:T(8,128)} %param.32) | copy-start | bytes 331780
  1321.4 44.5 %copy-start.45 = (f32[24,768]{1,0:T(8,128)S(1)}, f32[24,768]{1,0:T(8,128)}, u32[]{:S(2)}) copy-start(f32[24,768]{1,0:T(8,128)} %param.46) | copy-start | bytes 221188
  1368.0 6.2 copy-start.18
  1368.0 6.2 copy-start.19
  1374.2 64.2 %copy-start.17 = (f32[2,72,768]{2,1,0:T(8,128)S(1)}, f32[2,72,768]{2,1,0:T(8,128)}, u32[]{:S(2)}) copy-start(f32[2,72,768]{2,1,0:T(8,128)} %param.30) | copy-start | bytes 1327108
  (42 other events, 96.5 us)
Sparse Core Ops, SparseCore 0:
  11.7 75.3 all-gather.15
  94.3 58.8 all-gather.17
  155.3 58.9 all-gather.19
  217.5 52.7 all-gather.21
  273.6 54.5 all-gather.23
  526.1 56.2 reduce-scatter.14
  584.8 57.0 reduce-scatter.16
  647.8 98.9 reduce-scatter.12
  753.3 137.8 all-reduce.3
  897.6 161.9 reduce-scatter.10
  1063.0 52.9 all-gather.27
  1119.2 54.5 all-gather.29
  1177.4 71.6 all-gather.25
  1252.3 52.5 all-gather.33
  1308.2 55.1 all-gather.35
  1366.9 71.4 all-gather.31

commit v2 on v1

--- a/solution.py
+++ b/solution.py
@@ -3,6 +3,8 @@
 import jax
 import jax.numpy as jnp
 from jax import lax
+from jax.experimental import pallas as pl
+from jax.experimental.pallas import tpu as pltpu
 from jax.sharding import PartitionSpec as P
 
 HEAD_DIM = 64
@@ -89,7 +91,7 @@
     )
 
 
-def body(
+def sequence_body(
     tokens,
     cotangent,
     doc_lengths,
@@ -402,6 +404,741 @@
     )
 
 
+QUERY_TILE = 384
+KEY_STEP = 256
+KEY_ALIGN = 128
+PREP_TILE = 480
+LANES = 128
+MASK_BIT = -(2.0**100)
+NO_MAX = -3e38
+BF16 = jnp.bfloat16
+F32 = jnp.float32
+VMEM_BYTES = 56 * 2**20
+
+
+def dot_rows(left, right):
+    return lax.dot_general(left, right, (((1,), (1,)), ((), ())), preferred_element_type=F32)
+
+
+def dot_plain(left, right):
+    return lax.dot_general(left, right, (((1,), (0,)), ((), ())), preferred_element_type=F32)
+
+
+def dot_first(left, right):
+    return lax.dot_general(left, right, (((0,), (0,)), ((), ())), preferred_element_type=F32)
+
+
+def lane_index(rows):
+    return lax.broadcasted_iota(jnp.int32, (rows, LANES), 1)
+
+
+def three_pieces(column):
+    first = column.astype(BF16).astype(F32)
+    second = (column - first).astype(BF16).astype(F32)
+    return first, second, column - first - second
+
+
+def project_kernel(
+    tokens, weight, gain, cosine, sine, query_mask, key_mask, attn_in, query, key, value
+):
+    step = pl.program_id(0)
+    last = pl.num_programs(0) - 1
+    own_heads = query.shape[0]
+    rows = tokens.shape[0]
+    lane = lane_index(rows)
+    low_lanes = lane < HEAD_DIM
+
+    @pl.when(step < last)
+    def compute():
+        normed = norm_forward(tokens[...].astype(F32))[0]
+        low = (normed * gain[...]).astype(BF16)
+        attn_in[...] = low
+        raw = dot_rows(low, weight[...])
+        first_half = lane % HEAD_DIM < HEAD_DIM // 2
+        ones = jnp.where(lane < HEAD_DIM + 3, 1.0, 0.0)
+        for head in range(own_heads):
+            both = raw[:, head * LANES : (head + 1) * LANES]
+            turned = jnp.where(
+                first_half,
+                -pltpu.roll(both, LANES - HEAD_DIM // 2, 1),
+                pltpu.roll(both, HEAD_DIM // 2, 1),
+            )
+            both = both * cosine[...] + turned * sine[...]
+            query[head] = jnp.where(
+                low_lanes, both * SCORE_SCALE, query_mask[...].astype(F32)
+            ).astype(BF16)
+            key[head] = jnp.where(
+                low_lanes, pltpu.roll(both, HEAD_DIM, 1), key_mask[...].astype(F32)
+            ).astype(BF16)
+            at = own_heads + head // 2
+            pair = raw[:, at * LANES : (at + 1) * LANES]
+            if head % 2:
+                pair = pltpu.roll(pair, HEAD_DIM, 1)
+            value[head] = jnp.where(low_lanes, pair, ones).astype(BF16)
+
+    @pl.when(step == last)
+    def pad():
+        blocked = jnp.where(
+            low_lanes,
+            0.0,
+            jnp.where(lane < HEAD_DIM + 8, MASK_BIT, jnp.where(lane < HEAD_DIM + 11, 1.0, 0.0)),
+        ).astype(BF16)
+        for head in range(own_heads):
+            key[head] = blocked
+            value[head] = jnp.zeros((rows, LANES), BF16)
+
+
+def attend_kernel(
+    start_at, step_count, pad_from, query, key, value, pair_out, extra_out, wide_out, query_out
+):
+    tile = pl.program_id(0)
+    own_heads, rows, _ = query.shape
+    lane = lane_index(rows)
+    low_lanes = lane < HEAD_DIM
+    place = tile * rows + lax.broadcasted_iota(jnp.int32, (rows, 1), 0)
+    padded = place >= pad_from[0]
+    own_rows = pl.ds(pl.multiple_of(tile * rows, KEY_ALIGN), rows)
+    maxima, totals = [], []
+    for head in range(own_heads):
+        products = query[head].astype(F32) * key[head, own_rows, :].astype(F32)
+        self_score = jnp.sum(jnp.where(low_lanes, products, 0.0), axis=1, keepdims=True)
+        maxima.append(jnp.where(padded, self_score, NO_MAX))
+        totals.append(jnp.where(padded, value[head, own_rows, :].astype(F32), 0.0))
+    first = start_at[tile] * KEY_ALIGN
+
+    def step(index, carry):
+        maxima, totals = carry
+        at = pl.ds(pl.multiple_of(first + index * KEY_STEP, KEY_ALIGN), KEY_STEP)
+        new_maxima, new_totals = [], []
+        for head in range(own_heads):
+            scores = dot_rows(query[head], key[head, at, :])
+            row_max = jnp.maximum(maxima[head], jnp.max(scores, axis=1, keepdims=True))
+            weights = jnp.exp(scores - row_max).astype(BF16)
+            new_totals.append(
+                totals[head] * jnp.exp(maxima[head] - row_max)
+                + dot_plain(weights, value[head, at, :])
+            )
+            new_maxima.append(row_max)
+        return new_maxima, new_totals
+
+    maxima, totals = lax.fori_loop(0, step_count[tile], step, (maxima, totals))
+    outs = []
+    for head in range(own_heads):
+        row_sum = totals[head][:, HEAD_DIM : HEAD_DIM + 1]
+        attended = jnp.where(low_lanes, totals[head] / row_sum, 0.0)
+        wide_out[head] = attended
+        outs.append(attended)
+        one, two, three = three_pieces(-(maxima[head] + jnp.log(row_sum)))
+        at = HEAD_DIM + 8
+        query_out[head] = jnp.where(
+            lane == at,
+            one,
+            jnp.where(
+                lane == at + 1, two, jnp.where(lane == at + 2, three, query[head].astype(F32))
+            ),
+        ).astype(BF16)
+    pair_out[...] = (outs[0] + pltpu.roll(outs[1], HEAD_DIM, 1)).astype(BF16)
+    extra_out[...] = outs[2].astype(BF16)
+
+
+def attend_back_kernel(
+    start_at,
+    step_count,
+    pad_from,
+    query,
+    wide,
+    grad_pair,
+    grad_extra,
+    key,
+    value,
+    cosine,
+    sine,
+    grads,
+    grad_query,
+    grad_key,
+    grad_value,
+):
+    tile = pl.program_id(0)
+    own_heads, rows, _ = query.shape
+    tile_count = grad_query.shape[1] // rows
+
+    @pl.when(tile == 0)
+    def clear():
+        grad_key[...] = jnp.zeros_like(grad_key)
+        grad_value[...] = jnp.zeros_like(grad_value)
+
+    @pl.when(tile < tile_count)
+    def accumulate():
+        lane = lane_index(rows)
+        low_lanes = lane < HEAD_DIM
+        own_rows = pl.ds(pl.multiple_of(tile * rows, KEY_ALIGN), rows)
+        first = start_at[tile] * KEY_ALIGN
+        pair = grad_pair[...].astype(F32)
+        incoming = [pair, pltpu.roll(pair, HEAD_DIM, 1), grad_extra[...].astype(F32)]
+        grads_out = []
+        for head in range(own_heads):
+            own = jnp.where(low_lanes, incoming[head], 0.0)
+            one, two, three = three_pieces(-jnp.sum(own * wide[head], axis=1, keepdims=True))
+            grads_out.append(
+                jnp.where(
+                    lane == HEAD_DIM,
+                    one,
+                    jnp.where(
+                        lane == HEAD_DIM + 1, two, jnp.where(lane == HEAD_DIM + 2, three, own)
+                    ),
+                ).astype(BF16)
+            )
+
+        def step(index, carry):
+            at = pl.ds(pl.multiple_of(first + index * KEY_STEP, KEY_ALIGN), KEY_STEP)
+            sums = []
+            for head in range(own_heads):
+                keys = key[head, at, :]
+                probs = jnp.exp(dot_rows(keys, query[head]))
+                grad_scores = (probs * dot_rows(value[head, at, :], grads_out[head])).astype(BF16)
+                grad_value[head, at, :] += dot_plain(probs.astype(BF16), grads_out[head])
+                grad_key[head, at, :] += dot_plain(grad_scores, query[head])
+                sums.append(carry[head] + dot_first(grad_scores, keys))
+            return sums
+
+        zeros = [jnp.zeros((rows, LANES), F32) for _ in range(own_heads)]
+        sums = lax.fori_loop(0, step_count[tile], step, zeros)
+        for head in range(own_heads):
+            grad_query[head, own_rows, :] = sums[head]
+
+        @pl.when((tile + 1) * rows > pad_from[0])
+        def self_terms():
+            place = tile * rows + lax.broadcasted_iota(jnp.int32, (rows, 1), 0)
+            padded = place >= pad_from[0]
+            for head in range(own_heads):
+                keys = key[head, own_rows, :].astype(F32)
+                queries = query[head].astype(F32)
+                outs = grads_out[head].astype(F32)
+                counted = low_lanes | (lane >= HEAD_DIM + 8)
+                score = jnp.sum(jnp.where(counted, queries * keys, 0.0), axis=1, keepdims=True)
+                prob = jnp.where(padded, jnp.exp(jnp.where(padded, score, 0.0)), 0.0)
+                grad_prob = jnp.sum(
+                    outs * value[head, own_rows, :].astype(F32), axis=1, keepdims=True
+                )
+                grad_score = (prob * grad_prob).astype(BF16).astype(F32)
+                low_prob = prob.astype(BF16).astype(F32)
+                grad_query[head, own_rows, :] += grad_score * jnp.where(low_lanes, keys, 0.0)
+                grad_key[head, own_rows, :] += grad_score * queries
+                grad_value[head, own_rows, :] += low_prob * outs
+
+    @pl.when(tile >= tile_count)
+    def finish():
+        size = grads.shape[0]
+        at = pl.ds(pl.multiple_of((tile - tile_count) * size, 16), size)
+        lane = lane_index(size)
+        low_lanes = lane < HEAD_DIM
+        first_half = lane % HEAD_DIM < HEAD_DIM // 2
+        values = []
+        for head in range(own_heads):
+            both = jnp.where(
+                low_lanes,
+                grad_query[head, at, :] * SCORE_SCALE,
+                pltpu.roll(grad_key[head, at, :], HEAD_DIM, 1),
+            )
+            shifted = both * sine[...]
+            turned = jnp.where(
+                first_half,
+                pltpu.roll(shifted, LANES - HEAD_DIM // 2, 1),
+                -pltpu.roll(shifted, HEAD_DIM // 2, 1),
+            )
+            grads[:, head * LANES : (head + 1) * LANES] = (both * cosine[...] + turned).astype(BF16)
+            values.append(jnp.where(low_lanes, grad_value[head, at, :], 0.0))
+        base = own_heads * LANES
+        grads[:, base : base + LANES] = (values[0] + pltpu.roll(values[1], HEAD_DIM, 1)).astype(
+            BF16
+        )
+        grads[:, base + LANES : base + 2 * LANES] = values[2].astype(BF16)
+
+
+def exchange(values, axis, offset):
+    size = lax.axis_size(axis)
+    return lax.ppermute(values, axis, [(i, i ^ offset) for i in range(size)])
+
+
+def bit_count(size):
+    return size.bit_length() - 1
+
+
+def gather_blocks(values):
+    seq_count, dp_count = lax.axis_size("seq"), lax.axis_size("dp")
+    seq_at, dp_at = lax.axis_index("seq"), lax.axis_index("dp")
+    parts = jnp.stack([values] + [exchange(values, "seq", k) for k in range(1, seq_count)])
+    for bit in range(bit_count(seq_count)):
+        split = parts.reshape((seq_count >> (bit + 1), 2, 1 << bit) + values.shape)
+        split = jnp.where(((seq_at >> bit) & 1) == 1, split[:, ::-1], split)
+        parts = split.reshape((seq_count,) + values.shape)
+    bits = bit_count(dp_count)
+    half = values.shape[1] // 2
+
+    def spread(block, order):
+        block = block.reshape((1,) * bits + block.shape)
+        for bit in order:
+            other = exchange(block, "dp", 1 << bit)
+            upper = ((dp_at >> bit) & 1) == 1
+            block = jnp.concatenate(
+                [jnp.where(upper, other, block), jnp.where(upper, block, other)], bits - 1 - bit
+            )
+        return block
+
+    ahead = list(range(1, bits))
+    left = spread(parts[..., :half], ahead + [0])
+    right = spread(parts[..., half:], ahead[::-1] + [0])
+    return jnp.concatenate([left, right], -1).reshape((dp_count, seq_count) + values.shape)
+
+
+def sum_to_owner(values):
+    seq_count, dp_count = lax.axis_size("seq"), lax.axis_size("dp")
+    part = sum_over_dp(values)
+    pieces = lax.all_to_all(part, "seq", 0, 0, tiled=True)
+    return jnp.sum(pieces.astype(F32), axis=0)
+
+
+def sum_over_dp(values):
+    dp_count = lax.axis_size("dp")
+    dp_at = lax.axis_index("dp")
+    bits = bit_count(dp_count)
+
+    def halve(block, bit):
+        at = bits - 1 - bit
+        upper = (dp_at >> bit) & 1
+        send = lax.dynamic_index_in_dim(block, 1 - upper, at, keepdims=True)
+        keep = lax.dynamic_index_in_dim(block, upper, at, keepdims=True)
+        other = exchange(send, "dp", 1 << bit)
+        return (keep.astype(F32) + other.astype(F32)).astype(BF16)
+
+    block = halve(values.reshape((2,) * bits + values.shape[1:]), 0)
+    half = values.shape[-1] // 2
+    left, right = block[..., :half], block[..., half:]
+    for bit in range(1, bits):
+        left = halve(left, bit)
+        right = halve(right, bits - bit)
+    return jnp.concatenate([left, right], -1).reshape(values.shape[1:])
+
+
+def head_body(
+    tokens,
+    cotangent,
+    doc_lengths,
+    pad_counts,
+    w_in,
+    w_ao,
+    w_fo,
+    norm_gains,
+    gain_moment,
+    gain_second,
+    stat_l_in,
+    stat_r_in,
+    stat_l_ao,
+    stat_r_ao,
+    stat_l_fo,
+    stat_r_fo,
+    root_l_in,
+    root_r_in,
+    root_l_ao,
+    root_r_ao,
+    root_l_fo,
+    root_r_fo,
+):
+    token_count, width = tokens.shape
+    hidden = w_fo.shape[1]
+    seq_count, dp_count = lax.axis_size("seq"), lax.axis_size("dp")
+    all_count = seq_count * dp_count
+    row_length = token_count * seq_count
+    seq_at = lax.axis_index("seq")
+    dev_at = lax.axis_index(("dp", "seq"))
+    head_count = width // HEAD_DIM
+    own_heads = head_count // seq_count
+    own_width = own_heads * HEAD_DIM
+    in_rows = w_in.shape[1]
+    ao_rows, fo_rows = w_ao.shape[0], w_fo.shape[0]
+    out_rows = fo_rows * hidden // width
+    gain_cols = norm_gains.shape[1]
+
+    row_tokens = lax.all_gather(tokens, "seq", axis=0, tiled=True)
+    gain_tile = jnp.zeros((8, width), F32).at[:2, :gain_cols].set(norm_gains)
+    first_pack = gather_blocks(jnp.concatenate([w_in[0].astype(BF16), gain_tile.astype(BF16)]))
+    full_qkv = first_pack[:, :, :in_rows].reshape(all_count * in_rows, width)
+    gain_rows = (
+        jnp.transpose(first_pack[:, :, in_rows : in_rows + 2, :gain_cols], (2, 0, 1, 3))
+        .reshape(2, width)
+        .astype(F32)
+    )
+    rest = jnp.concatenate(
+        [
+            w_in[1].astype(BF16),
+            w_ao.astype(BF16),
+            w_fo.astype(BF16).reshape(out_rows, width),
+        ]
+    )
+    rest = lax.all_gather(rest, ("dp", "seq"), axis=0, tiled=False)
+    full_up = rest[:, :in_rows].reshape(all_count * in_rows, width)
+    full_ao = rest[:, in_rows : in_rows + ao_rows].reshape(width, width)
+    full_fo = rest[:, in_rows + ao_rows :].reshape(width, hidden)
+    root_rows = stat_r_in.shape[1]
+    fo_root_rows = root_r_fo.shape[0] * hidden // width
+    roots = jnp.concatenate(
+        [
+            root_r_in.astype(BF16).reshape(2 * root_rows, width),
+            root_r_ao.astype(BF16),
+            root_r_fo.astype(BF16).reshape(fo_root_rows, width),
+        ]
+    )
+    roots = lax.all_gather(roots, ("dp", "seq"), axis=0, tiled=False)
+    right_qkv = roots[:, :root_rows].reshape(width, width)
+    right_up = roots[:, root_rows : 2 * root_rows].reshape(width, width)
+    right_ao = roots[:, 2 * root_rows : 3 * root_rows].reshape(width, width)
+    right_fo = roots[:, 3 * root_rows :].reshape(hidden, hidden)
+
+    lengths = doc_lengths[0]
+    segment, within, is_valid = doc_tables(lengths, pad_counts[0], row_length)
+    pad_from = row_length - pad_counts[0]
+    doc_ids = jnp.arange(lengths.shape[0], dtype=jnp.int32)
+    places = jnp.arange(row_length, dtype=jnp.int32)
+    doc_begin = places - within
+    doc_end = doc_begin + jnp.sum(
+        jnp.where(segment[:, None] == doc_ids[None, :], lengths[None, :], 0), axis=1
+    )
+    freq_index = jnp.arange(0, HEAD_DIM, 2, dtype=F32)
+    inverse = 1.0 / jnp.power(ROPE_THETA, freq_index / HEAD_DIM)
+    angles = within.astype(F32)[:, None] * inverse[None, :]
+    copies = LANES // (HEAD_DIM // 2)
+    cos_table = jnp.concatenate([jnp.cos(angles)] * copies, axis=1)
+    sin_table = jnp.concatenate([jnp.sin(angles)] * copies, axis=1)
+    lane = jnp.arange(LANES, dtype=jnp.int32)
+    in_doc = lane[None, :] - HEAD_DIM == segment[:, None]
+    mask_lanes = (lane >= HEAD_DIM) & (lane < HEAD_DIM + 8)
+    one_lanes = (lane >= HEAD_DIM + 8) & (lane < HEAD_DIM + 11)
+    query_mask = in_doc.astype(BF16)
+    key_mask = jnp.where(
+        mask_lanes[None, :] & ~(in_doc & is_valid[:, None]),
+        MASK_BIT,
+        jnp.where(one_lanes[None, :], 1.0, 0.0),
+    ).astype(BF16)
+    tile_starts = doc_begin[::QUERY_TILE] // KEY_ALIGN
+    tile_ends = jnp.minimum(doc_end[QUERY_TILE - 1 :: QUERY_TILE], pad_from)
+    tile_steps = jnp.maximum(-((tile_starts * KEY_ALIGN - tile_ends) // KEY_STEP), 0)
+    tile_count = row_length // QUERY_TILE
+    pad_at = pad_from[None]
+
+    qkv_heads = lax.dynamic_slice_in_dim(
+        full_qkv.reshape(3, head_count, HEAD_DIM, width), seq_at * own_heads, own_heads, 1
+    )
+    own_weight = jnp.concatenate(
+        [
+            jnp.transpose(qkv_heads[:2], (1, 0, 2, 3)).reshape(2 * own_width, width),
+            qkv_heads[2].reshape(own_width, width),
+            jnp.zeros((HEAD_DIM, width), BF16),
+        ]
+    )
+    own_columns = own_weight.shape[0]
+    prep_count = row_length // PREP_TILE
+    key_length = row_length + PREP_TILE
+
+    def row_block(columns):
+        return pl.BlockSpec(
+            (PREP_TILE, columns), lambda i: (jnp.minimum(i, prep_count - 1), 0)
+        )
+
+    def fixed_block(*shape):
+        return pl.BlockSpec(shape, lambda i, *_: (0,) * len(shape))
+
+    head_block = pl.BlockSpec((own_heads, PREP_TILE, LANES), lambda i: (0, i, 0))
+    attn_in, query_ext, key_ext, value_ext = pl.pallas_call(
+        project_kernel,
+        grid=(prep_count + 1,),
+        in_specs=[
+            row_block(width),
+            fixed_block(own_columns, width),
+            fixed_block(1, width),
+            row_block(LANES),
+            row_block(LANES),
+            row_block(LANES),
+            row_block(LANES),
+        ],
+        out_specs=[
+            row_block(width),
+            pl.BlockSpec(
+                (own_heads, PREP_TILE, LANES), lambda i: (0, jnp.minimum(i, prep_count - 1), 0)
+            ),
+            head_block,
+            head_block,
+        ],
+        out_shape=[
+            jax.ShapeDtypeStruct((row_length, width), BF16),
+            jax.ShapeDtypeStruct((own_heads, row_length, LANES), BF16),
+            jax.ShapeDtypeStruct((own_heads, key_length, LANES), BF16),
+            jax.ShapeDtypeStruct((own_heads, key_length, LANES), BF16),
+        ],
+        compiler_params=pltpu.CompilerParams(vmem_limit_bytes=VMEM_BYTES),
+        cost_estimate=pl.CostEstimate(
+            flops=2 * row_length * own_columns * width,
+            bytes_accessed=14_000_000,
+            transcendentals=0,
+        ),
+        name="project",
+    )(
+        row_tokens,
+        own_weight,
+        gain_rows[:1],
+        cos_table,
+        sin_table,
+        query_mask,
+        key_mask,
+    )
+
+    def tile_block(columns):
+        return pl.BlockSpec(
+            (QUERY_TILE, columns), lambda i, *_: (jnp.minimum(i, tile_count - 1), 0)
+        )
+
+    head_tile = pl.BlockSpec(
+        (own_heads, QUERY_TILE, LANES), lambda i, *_: (0, jnp.minimum(i, tile_count - 1), 0)
+    )
+    whole_keys = fixed_block(own_heads, key_length, LANES)
+    pair_out, extra_out, wide_out, query_low = pl.pallas_call(
+        attend_kernel,
+        grid_spec=pltpu.PrefetchScalarGridSpec(
+            num_scalar_prefetch=3,
+            grid=(tile_count,),
+            in_specs=[head_tile, whole_keys, whole_keys],
+            out_specs=[tile_block(LANES), tile_block(LANES), head_tile, head_tile],
+        ),
+        out_shape=[
+            jax.ShapeDtypeStruct((row_length, LANES), BF16),
+            jax.ShapeDtypeStruct((row_length, LANES), BF16),
+            jax.ShapeDtypeStruct((own_heads, row_length, LANES), F32),
+            jax.ShapeDtypeStruct((own_heads, row_length, LANES), BF16),
+        ],
+        compiler_params=pltpu.CompilerParams(vmem_limit_bytes=VMEM_BYTES),
+        cost_estimate=pl.CostEstimate(
+            flops=2 * own_heads * row_length * row_length * LANES,
+            bytes_accessed=12_000_000,
+            transcendentals=0,
+        ),
+        name="attend",
+    )(tile_starts, tile_steps, pad_at, query_ext, key_ext, value_ext)
+
+    half_tokens = token_count // 2
+
+    def fold(extra):
+        blocks = extra[:, :HEAD_DIM].reshape(seq_count, 2, half_tokens, HEAD_DIM)
+        return jnp.concatenate([blocks[:, 0], blocks[:, 1]], axis=-1)
+
+    def unfold(folded):
+        return jnp.concatenate([folded[:, :, :HEAD_DIM], folded[:, :, HEAD_DIM:]], axis=1)
+
+    packed = jnp.concatenate(
+        [pair_out.reshape(seq_count, token_count, LANES), fold(extra_out)], axis=1
+    )
+    packed = lax.all_to_all(packed, "seq", 0, 0, tiled=True)
+    attn_low = jnp.concatenate([packed[:, :token_count], unfold(packed[:, token_count:])], axis=-1)
+    attn_low = jnp.transpose(attn_low, (1, 0, 2)).reshape(token_count, width)
+
+    inputs = tokens.astype(F32)
+    residual = inputs + apply_rows(attn_low, full_ao)
+    normed_two, spread_two = norm_forward(residual)
+    ffn_in = (normed_two * gain_rows[1]).astype(BF16)
+    projected = apply_rows(ffn_in, full_up)
+    inner_part = projected[:, :hidden]
+    gate_part = projected[:, hidden:]
+    activated = gelu_value(inner_part)
+    mid_low = (activated * gate_part).astype(BF16)
+    layer_out = (residual + apply_rows(mid_low, full_fo)).astype(BF16)
+    grad_mid = jnp.dot(cotangent, full_fo, preferred_element_type=F32)
+    grad_proj = jnp.concatenate(
+        [grad_mid * gate_part * gelu_slope(inner_part), grad_mid * activated], axis=1
+    ).astype(BF16)
+    grad_ffn_in = jnp.dot(grad_proj, full_up, preferred_element_type=F32)
+    grad_norm_two, _ = norm_backward(grad_ffn_in, normed_two, spread_two, gain_rows[1])
+    grad_resid = cotangent.astype(F32) + grad_norm_two
+    grad_out_attn = grad_resid.astype(BF16)
+    grad_attn = jnp.dot(grad_out_attn, full_ao, preferred_element_type=F32).astype(BF16)
+
+    grad_blocks = jnp.transpose(
+        grad_attn.reshape(token_count, seq_count, own_width), (1, 0, 2)
+    )
+    folded = grad_blocks[:, :, LANES:].reshape(seq_count, 2, half_tokens, HEAD_DIM)
+    packed_back = jnp.concatenate(
+        [grad_blocks[:, :, :LANES], jnp.concatenate([folded[:, 0], folded[:, 1]], axis=-1)], axis=1
+    )
+    packed_back = lax.all_to_all(packed_back, "seq", 0, 0, tiled=True)
+    grad_pair = packed_back[:, :token_count].reshape(row_length, LANES)
+    grad_extra = unfold(packed_back[:, token_count:]).reshape(row_length, HEAD_DIM)
+    grad_extra = jnp.pad(grad_extra, ((0, 0), (0, LANES - HEAD_DIM)))
+
+    grad_up_term = outer_sum(grad_proj, ffn_in).astype(BF16).reshape(all_count, in_rows, width)
+    grad_ao_term = outer_sum(grad_out_attn, attn_low).astype(BF16)
+    grad_fo_term = outer_sum(cotangent, mid_low).astype(BF16)
+    terms = jnp.concatenate(
+        [
+            grad_up_term,
+            grad_ao_term.reshape(all_count, ao_rows, width),
+            grad_fo_term.reshape(all_count, out_rows, width),
+        ],
+        axis=1,
+    )
+    summed = sum_to_owner(terms.reshape((dp_count, seq_count) + terms.shape[1:]))
+    summed_up = summed[:in_rows]
+    summed_ao = summed[in_rows : in_rows + ao_rows]
+    summed_fo = summed[in_rows + ao_rows :].reshape(fo_rows, hidden)
+    whole = gather_blocks(summed.astype(BF16)).reshape(all_count, summed.shape[0], width)
+    whole_up = whole[:, :in_rows].reshape(all_count * in_rows, width)
+    whole_ao = whole[:, in_rows : in_rows + ao_rows].reshape(width, width)
+    whole_fo = whole[:, in_rows + ao_rows :].reshape(width, hidden)
+
+    finish_count = prep_count
+
+    def finish_block(columns):
+        return pl.BlockSpec(
+            (PREP_TILE, columns), lambda i, *_: (jnp.maximum(i - tile_count, 0), 0)
+        )
+
+    grad_qkv = pl.pallas_call(
+        attend_back_kernel,
+        grid_spec=pltpu.PrefetchScalarGridSpec(
+            num_scalar_prefetch=3,
+            grid=(tile_count + finish_count,),
+            in_specs=[
+                head_tile,
+                head_tile,
+                tile_block(LANES),
+                tile_block(LANES),
+                whole_keys,
+                whole_keys,
+                finish_block(LANES),
+                finish_block(LANES),
+            ],
+            out_specs=finish_block(own_columns),
+            scratch_shapes=[
+                pltpu.VMEM((own_heads, row_length, LANES), F32),
+                pltpu.VMEM((own_heads, key_length, LANES), F32),
+                pltpu.VMEM((own_heads, key_length, LANES), F32),
+            ],
+        ),
+        out_shape=jax.ShapeDtypeStruct((row_length, own_columns), BF16),
+        compiler_params=pltpu.CompilerParams(vmem_limit_bytes=VMEM_BYTES),
+        cost_estimate=pl.CostEstimate(
+            flops=5 * own_heads * row_length * row_length * LANES,
+            bytes_accessed=15_000_000,
+            transcendentals=0,
+        ),
+        name="attend_back",
+    )(
+        tile_starts,
+        tile_steps,
+        pad_at,
+        query_low,
+        wide_out,
+        grad_pair,
+        grad_extra,
+        key_ext,
+        value_ext,
+        cos_table,
+        sin_table,
+    )
+    qkv_term = outer_sum(grad_qkv, attn_in)[: 3 * own_width].astype(BF16)
+    qkv_sum = sum_over_dp(qkv_term.reshape(dp_count, 3 * own_width // dp_count, width))
+    qkv_parts = jnp.transpose(gather_blocks(qkv_sum), (1, 0, 2, 3)).reshape(
+        seq_count, 3 * own_width, width
+    )
+    whole_query_key = qkv_parts[:, : 2 * own_width].reshape(
+        seq_count, own_heads, 2, HEAD_DIM, width
+    )
+    whole_qkv = jnp.concatenate(
+        [
+            jnp.transpose(whole_query_key, (2, 0, 1, 3, 4)),
+            qkv_parts[:, 2 * own_width :].reshape(1, seq_count, own_heads, HEAD_DIM, width),
+        ]
+    ).reshape(3 * width, width)
+    summed_qkv = lax.dynamic_slice_in_dim(whole_qkv, dev_at * in_rows, in_rows, 0).astype(F32)
+
+    input_term = jnp.dot(grad_qkv, own_weight, preferred_element_type=F32).astype(BF16)
+    grad_attn_in = lax.psum_scatter(input_term, "seq", scatter_dimension=0, tiled=True).astype(F32)
+    normed_one, spread_one = norm_forward(inputs)
+    grad_norm_one, _ = norm_backward(grad_attn_in, normed_one, spread_one, gain_rows[0])
+    grad_input = grad_resid + grad_norm_one
+
+    def own_columns_of(matrix, count):
+        return lax.dynamic_slice_in_dim(matrix, dev_at * count, count, 1)
+
+    def gain_gradient(weight, gradient, gain):
+        own_weight_columns = own_columns_of(weight, gain_cols).astype(F32)
+        products = own_weight_columns * own_columns_of(gradient, gain_cols).astype(F32)
+        own_gain = lax.dynamic_slice_in_dim(gain, dev_at * gain_cols, gain_cols)
+        return jnp.sum(products, axis=0) / own_gain
+
+    summed_gains = jnp.stack(
+        [
+            gain_gradient(full_qkv, whole_qkv, gain_rows[0]),
+            gain_gradient(full_up, whole_up, gain_rows[1]),
+        ]
+    )
+    new_moment = 0.9 * gain_moment + 0.1 * summed_gains
+    new_second = 0.999 * gain_second + 0.001 * summed_gains * summed_gains
+    new_gains = norm_gains - ADAM_RATE * new_moment / (jnp.sqrt(new_second) + 1e-08)
+
+    def refresh(weight, own, full, stat_left, stat_right, root_left, right):
+        new_left = 0.5 * stat_left + 0.5 * apply_rows(own.astype(BF16), full)
+        columns = own_columns_of(full, stat_right.shape[0])
+        new_right = 0.5 * stat_right + 0.5 * outer_sum(columns, full)
+        left_product = jnp.dot(root_left.astype(BF16), full, preferred_element_type=F32)
+        update = jnp.dot(left_product.astype(BF16), right, preferred_element_type=F32)
+        return new_left, new_right, weight - SHAMPOO_RATE * update
+
+    left_up, right_stat_up, new_up = refresh(
+        w_in[1], summed_up, whole_up, stat_l_in[1], stat_r_in[1], root_l_in[1], right_up
+    )
+    left_ao, right_stat_ao, new_ao = refresh(
+        w_ao, summed_ao, whole_ao, stat_l_ao, stat_r_ao, root_l_ao, right_ao
+    )
+    left_fo, right_stat_fo, new_fo = refresh(
+        w_fo, summed_fo, whole_fo, stat_l_fo, stat_r_fo, root_l_fo, right_fo
+    )
+    left_qkv, right_stat_qkv, new_qkv = refresh(
+        w_in[0], summed_qkv, whole_qkv, stat_l_in[0], stat_r_in[0], root_l_in[0], right_qkv
+    )
+    return (
+        layer_out,
+        grad_input,
+        jnp.stack([summed_qkv, summed_up]),
+        summed_ao,
+        summed_fo,
+        summed_gains,
+        new_moment,
+        new_second,
+        new_gains,
+        jnp.stack([left_qkv, left_up]),
+        jnp.stack([right_stat_qkv, right_stat_up]),
+        left_ao,
+        right_stat_ao,
+        left_fo,
+        right_stat_fo,
+        jnp.stack([new_qkv, new_up]),
+        new_ao,
+        new_fo,
+    )
+
+
+def body(tokens, *others):
+    seq_count, dp_count = lax.axis_size("seq"), lax.axis_size("dp")
+    token_count, width = tokens.shape
+    row_length = token_count * seq_count
+    by_heads = (
+        width // HEAD_DIM == 3 * seq_count
+        and dp_count & (dp_count - 1) == 0
+        and seq_count & (seq_count - 1) == 0
+        and row_length % QUERY_TILE == 0
+        and row_length % PREP_TILE == 0
+        and others[1].shape[1] == 8
+    )
+    return head_body(tokens, *others) if by_heads else sequence_body(tokens, *others)
+
+
 def solution(mesh):
     in_specs = (
         P(("dp", "seq"), None),

time: 1460 us -> 501 us (0.34)
  waiting for transfers between devices: 856 us -> 145 us
  matrix products: 206 us -> 52.3 us
  blocking collectives: 109 us -> 0 us
  Pallas kernels: 0 us -> 78.6 us
  local copies, waits for them, and re-layouts: 135 us -> 75 us
  starting transfers between devices: 1.05 us -> 54.6 us
  other arithmetic: 113 us -> 72.8 us
  loops' own time: 20 us -> 0 us
    all_gather x11 -> x3, waiting for transfers between devices: 390 us -> 11 us  [the longest x1 7.4 us: head_body(): row_tokens = lax.all_gather(tokens, 'seq', axis=0, tiled=True)]
    reduce_scatter x2 -> x1, waiting for transfers between devices: 242 us -> 0.01 us  [head_body(): lax.psum_scatter(input_term, 'seq', scatter_dimension=0, tiled=True)]
    unnamed x19 -> x4, waiting for transfers between devices: 223 us -> 0.73 us
    dot_general x58 -> x8, matrix products: 169 us -> 22.1 us  [the longest x4 12.1 us: refresh(): jnp.dot(left_product.astype(BF16), right, preferred_element_type=F32)]
    ppermute x0 -> x37, waiting for transfers between devices: none -> 86.4 us  [exchange(): return lax.ppermute(values, axis, [(i, i ^ offset) for i in range(size)])]
    pallas_call x0 -> x3, Pallas kernels: none -> 78.6 us  [the longest x1 41.3 us: head_body(): pl.pallas_call(attend_back_kernel, grid_spec=pltpu.PrefetchScalarGridSpec...]
    all_gather x1 -> x0, blocking collectives: 69.6 us -> none  [body(): lax.all_gather(low_weights[3], ('dp', 'seq'), axis=1, tiled=True)]
    all_to_all x0 -> x3, waiting for transfers between devices: none -> 46.5 us  [the longest x1 29.9 us: head_body(): packed = lax.all_to_all(packed, 'seq', 0, 0, tiled=True)]
  transfers between devices with their start and end apart: 16 -> 44, of which waited for: 14 -> 21; matrix products, arithmetic and copies ran while one was open for 17% -> 31% of each run, Pallas kernels for 0% -> 16%
where the time goes in v2:
time: 501 us; the launch traced here: 494 us
  waiting for transfers between devices  145 us (29%)
  Pallas kernels  78.6 us (16%)
  local copies, waits for them, and re-layouts  75 us (15%)
  other arithmetic  72.8 us (15%)
  starting transfers between devices  54.6 us (11%)
  matrix products  52.3 us (10%)
  between operations  16.2 us (3%)
    ppermute x37, waiting for transfers between devices, exchange(): return lax.ppermute(values, axis, [(i, i ^ offset) for i in range(size)])  86.4 us
    pallas_call x1, Pallas kernels, head_body(): pl.pallas_call(attend_back_kernel, grid_spec=pltpu.PrefetchScalarGridSpec...  41.3 us
    ppermute x37, starting transfers between devices, exchange(): return lax.ppermute(values, axis, [(i, i ^ offset) for i in range(size)])  41.1 us
    all_to_all x1, waiting for transfers between devices, head_body(): packed = lax.all_to_all(packed, 'seq', 0, 0, tiled=True)  29.9 us
    pallas_call x1, Pallas kernels, head_body(): pl.pallas_call(attend_kernel, grid_spec=pltpu.PrefetchScalarGridSpec(num_...  27.9 us
    dot_general x8, matrix products, outer_sum(): lax.dot_general(grad_rows, act_rows, (((0,), (0,)), ((), ())), preferred_...  16.9 us
    all_to_all x1, waiting for transfers between devices, sum_to_owner(): pieces = lax.all_to_all(part, 'seq', 0, 0, tiled=True)  16.7 us
    select_n x17, other arithmetic, spread(): jnp.where(upper, other, block)  15.2 us
  transfers between devices with their start and end apart: 44, of which 21 were waited for; matrix products, arithmetic and copies ran while one was open for 31% of the time, Pallas kernels for 16%

profile of v2, /device:TPU:0, one launch (start us, length us, event | category | flops | bytes accessed | tf_op | source)
XLA Modules:
  0.0 494.1 jit_solution(9324600624709723464)
XLA Ops:
  11.8 5.1 %collective-permute-start.2 = (bf16[80,768]{1,0:T(8,128)(2,1)S(1)}, bf16[80,768]{1,0:T(8,128)(2,1)S(1)}, u32[]{:S(2)}, u32[]{:S(2)}) collective-permute-start(bf16[80,768]{1,0:T(8,128)(2,1)S(1)} %get-tuple-element.125), channel_id=1, source_target_pairs={{0,3},{1,2},{2,1},{3,0},{4,7},{5,6},{6,5},{7,4},{8,11},{9,10},{10,... | collective-permute-start | bytes 368648 | tf_op jit(solution)/shard_map/ppermute | solution.py:660
  18.8 3.5 multiply_sine_fusion
  22.3 14.8 %collective-permute-done.1 = bf16[80,768]{1,0:T(8,128)(2,1)S(1)} collective-permute-done((bf16[80,768]{1,0:T(8,128)(2,1)S(1)}, bf16[80,768]{1,0:T(8,128)(2,1)S(1)}, u32[]{:S(2)}, u32[]{:S(2)}) %collective-permute-start.1) | collective-permute-done | bytes 122912 | tf_op jit(solution)/shard_map/ppermute | solution.py:660
  42.5 2.6 collective-permute-done.3
  47.8 2.9 pad_maximum_fusion.10
  55.0 4.8 collective-permute-done.4
  68.0 7.4 %all-gather.8.cloned.1.call-done.tokens = bf16[1920,768]{1,0:T(8,128)(2,1)} async-done(((bf16[480,768]{1,0:T(8,128)(2,1)}), bf16[1920,768]{1,0:T(8,128)(2,1)}) %all-gather.8.cloned.1.call-update) | async-done | bytes 2949136 | tf_op jit(solution)/shard_map/all_gather | solution.py:762
  75.4 9.4 %project.1 = (bf16[1920,768]{1,0:T(8,128)(2,1)}, bf16[3,1920,128]{2,1,0:T(8,128)(2,1)}, bf16[3,2400,128]{2,1,0:T(8,128)(2,1)}, bf16[3,2400,128]{2,1,0:T(8,128)(2,1)}) custom-call(bf16[1920,768]{1,0:T(8,128)(2,1)} %all-gather.8.cloned.1.call-done.tokens, bf16[640,768]{1,0:T(8,128)(2,1)} %maximum_maximum_fusion.3.weight, f32[1,768]{1,0:T(1,128)} %slice.222.gain, ...), custom_call_target="tpu_custom_call" | custom-call | flops 1887436800 | bytes 14000000 | tf_op jit(solution)/shard_map/project/pallas_call | solution.py:851
  84.8 27.9 %attend.1 = (bf16[1920,128]{1,0:T(8,128)(2,1)}, bf16[1920,128]{1,0:T(8,128)(2,1)}, f32[3,1920,128]{2,1,0:T(8,128)}, bf16[3,1920,128]{2,1,0:T(8,128)(2,1)}) custom-call(s32[5]{0:T(128)} %get-tuple-element.59.start_at, s32[5]{0:T(128)} %get-tuple-element.58.step_count, s32[1]{0:T(128)} %sub.108.pad_from, bf16[3,1920,128]{2,1,0:T(8,128)(2,1)} %get-tuple-element.38.query, ...), custom_call_target="tpu_custom_call" | custom-call | flops 2831155200 | bytes 12000000 | tf_op jit(solution)/shard_map/attend/pallas_call | solution.py:903
  116.0 4.1 all-to-all-start
  121.9 29.9 %all-to-all-done = bf16[4,720,128]{2,1,0:T(8,128)(2,1)S(1)} async-done(((bf16[4,720,128]{2,1,0:T(8,128)(2,1)}), bf16[4,720,128]{2,1,0:T(8,128)(2,1)S(1)}, u32[]{:S(2)}, u32[]{:S(2)}) %all-to-all-start) | async-done | bytes 737312 | tf_op jit(solution)/shard_map/all_to_all | solution.py:938
  152.7 3.6 all-gather.10.cloned.1.call-done
  166.8 2.9 fusion.11
  175.4 4.2 all-to-all-start.1
  179.6 2.6 fusion.4
  182.2 13.1 %copy.140 = bf16[768,1152]{1,0:T(8,128)(2,1)} copy(bf16[768,1152]{0,1:T(8,128)(2,1)S(1)} %fusion.4) | data formatting | bytes 3538944 | tf_op jit(solution)/shard_map/convert_element_type | solution.py:976
  195.3 2.9 concatenate.158
  198.2 4.3 convolution_convert_fusion
  203.3 3.1 copy_dynamic-update-slice_fusion
  212.0 41.3 %attend_back.1 = bf16[1920,640]{1,0:T(8,128)(2,1)} custom-call(s32[5]{0:T(128)} %get-tuple-element.59.start_at, s32[5]{0:T(128)} %get-tuple-element.58.step_count, s32[1]{0:T(128)} %sub.108.pad_from, bf16[3,1920,128]{2,1,0:T(8,128)(2,1)} %get-tuple-element.43.query, f32[3,1920,128]{2,1,0:T(8,128)} %get-tuple-element.44.wide, bf16[1920,128]{1,0:T(8,128)(2,1)} %bitcast.272, ...), custom_call_target="tpu_custom_call" | custom-call | flops 7077888000 | bytes 15000000 | tf_op jit(solution)/shard_map/attend_back/pallas_call | solution.py:1001
  253.3 3.9 fusion.77
  259.4 4.8 constant_dynamic-slice_fusion.6
  265.1 4.9 collective-permute-done.12
  274.4 3.8 collective-permute-start.16
  278.9 3.9 fusion.69
  284.5 3.4 reshape.352
  290.0 4.3 convolution_convert_fusion.2
  296.6 4.6 add_convert_fusion
  307.2 5.1 %collective-permute-done.21 = bf16[2,1,1,4,72,384]{5,4,2,1,0,3:T(8,128)(2,1)S(1)} collective-permute-done((bf16[2,1,1,4,72,384]{5,4,2,1,0,3:T(8,128)(2,1)S(1)}, bf16[2,1,1,4,72,384]{5,4,2,1,0,3:T(8,128)(2,1)S(1)}, u32[]{:S(2)}, u32[]{:S(2)}) %collective-permute-start.21) | collective-permute-done | bytes 442400 | tf_op jit(solution)/shard_map/ppermute | solution.py:660
  313.4 10.3 %collective-permute-done.26 = bf16[1,2,1,4,132,384]{5,3,4,2,1,0:T(4,128)(2,1)S(1)} collective-permute-done((bf16[1,2,1,4,132,384]{5,3,4,2,1,0:T(4,128)(2,1)S(1)}, bf16[1,2,1,4,132,384]{5,3,4,2,1,0:T(4,128)(2,1)S(1)}, u32[]{:S(2)}, u32[]{:S(2)}) %collective-permute-start.26) | collective-permute-done | bytes 811040 | tf_op jit(solution)/shard_map/ppermute | solution.py:660
  326.2 3.4 collective-permute-done.24
  335.0 3.2 collective-permute-done.25
  339.9 5.0 %all-to-all-start.2 = ((bf16[4,132,768]{2,1,0:T(8,128)(2,1)}), bf16[4,132,768]{2,1,0:T(8,128)(2,1)}, u32[]{:S(2)}, u32[]{:S(2)}) async-start(bf16[4,132,768]{2,1,0:T(8,128)(2,1)} %copy.144), calls=%async_computation.3 | async-start | bytes 1671168 | tf_op jit(solution)/shard_map/all_to_all | solution.py:697
  344.8 3.8 add_convert_fusion.3
  352.9 16.7 %all-to-all-done.2 = bf16[4,132,768]{2,1,0:T(8,128)(2,1)} async-done(((bf16[4,132,768]{2,1,0:T(8,128)(2,1)}), bf16[4,132,768]{2,1,0:T(8,128)(2,1)}, u32[]{:S(2)}, u32[]{:S(2)}) %all-to-all-start.2) | async-done | bytes 811040 | tf_op jit(solution)/shard_map/all_to_all | solution.py:697
  372.5 2.9 collective-permute-start.28
  375.5 5.6 %collective-permute-done.30 = bf16[132,768]{1,0:T(8,128)(2,1)S(1)} collective-permute-done((bf16[132,768]{1,0:T(8,128)(2,1)S(1)}, bf16[132,768]{1,0:T(8,128)(2,1)S(1)}, u32[]{:S(2)}, u32[]{:S(2)}) %collective-permute-start.30) | collective-permute-done | bytes 202784 | tf_op jit(solution)/shard_map/ppermute | solution.py:660
  381.0 7.8 %collective-permute-done.29 = bf16[132,768]{1,0:T(8,128)(2,1)S(1)} collective-permute-done((bf16[132,768]{1,0:T(8,128)(2,1)S(1)}, bf16[132,768]{1,0:T(8,128)(2,1)S(1)}, u32[]{:S(2)}, u32[]{:S(2)}) %collective-permute-start.29) | collective-permute-done | bytes 202784 | tf_op jit(solution)/shard_map/ppermute | solution.py:660
  397.6 3.2 fusion.23
  409.1 5.2 %collective-permute-done.31 = bf16[1,1,1,4,132,384]{5,3,4,2,1,0:T(4,128)(2,1)S(1)} collective-permute-done((bf16[1,1,1,4,132,384]{5,3,4,2,1,0:T(4,128)(2,1)S(1)}, bf16[1,1,1,4,132,384]{5,3,4,2,1,0:T(4,128)(2,1)S(1)}, u32[]{:S(2)}, u32[]{:S(2)}) %collective-permute-start.31) | collective-permute-done | bytes 405536 | tf_op jit(solution)/shard_map/ppermute | solution.py:660
  417.5 12.3 %collective-permute-done.35 = bf16[2,1,1,4,132,384]{5,3,4,2,1,0:T(4,128)(2,1)S(1)} collective-permute-done((bf16[2,1,1,4,132,384]{5,3,4,2,1,0:T(4,128)(2,1)S(1)}, bf16[2,1,1,4,132,384]{5,3,4,2,1,0:T(4,128)(2,1)S(1)}, u32[]{:S(2)}, u32[]{:S(2)}) %collective-permute-start.35) | collective-permute-done | bytes 811040 | tf_op jit(solution)/shard_map/ppermute | solution.py:660
  438.9 2.6 pad_maximum_fusion.3
  446.3 3.2 broadcast_select_fusion.1
  449.5 3.1 broadcast_select_fusion.3
  452.6 3.0 maximum_maximum_fusion
  464.9 4.0 reshape.346
  468.9 3.2 fusion.22
  483.5 3.2 convolution_subtract_fusion
  (399 shorter events, 147.3 us)
Async XLA Ops:
  7.2 68.2 %all-gather.8.cloned.1.call-start = ((), (), s32[]{:S(2)}) async-start(), calls=%async_computation.4 | async-start | bytes 3686400 | tf_op jit(solution)/shard_map/all_gather | solution.py:762
  8.0 148.2 %all-gather.10.cloned.1.call-start = ((), (), s32[]{:S(2)}) async-start(), calls=%async_computation.6 | async-start | bytes 6893568 | tf_op jit(solution)/shard_map/all_gather | solution.py:778
  11.7 267.2 %all-gather.12.cloned.1.call-start = ((), (), s32[]{:S(2)}) async-start(), calls=%async_computation.7 | async-start | bytes 6488064 | tf_op jit(solution)/shard_map/all_gather | solution.py:791
  11.8 10.5 %collective-permute-start.2 = (bf16[80,768]{1,0:T(8,128)(2,1)S(1)}, bf16[80,768]{1,0:T(8,128)(2,1)S(1)}, u32[]{:S(2)}, u32[]{:S(2)}) collective-permute-start(bf16[80,768]{1,0:T(8,128)(2,1)S(1)} %get-tuple-element.125), channel_id=1, source_target_pairs={{0,3},{1,2},{2,1},{3,0},{4,7},{5,6},{6,5},{7,4},{8,11},{9,10},{10,... | collective-permute-start | bytes 368648 | tf_op jit(solution)/shard_map/ppermute | solution.py:660
  16.9 20.1 %collective-permute-start.1 = (bf16[80,768]{1,0:T(8,128)(2,1)S(1)}, bf16[80,768]{1,0:T(8,128)(2,1)S(1)}, u32[]{:S(2)}, u32[]{:S(2)}) collective-permute-start(bf16[80,768]{1,0:T(8,128)(2,1)S(1)} %get-tuple-element.125), channel_id=1, source_target_pairs={{0,2},{1,3},{2,0},{3,1},{4,6},{5,7},{6,4},{7,5},{8,10},{9,11},{10,... | collective-permute-start | bytes 368648 | tf_op jit(solution)/shard_map/ppermute | solution.py:660
  16.9 20.1 %collective-permute-start = (bf16[80,768]{1,0:T(8,128)(2,1)S(1)}, bf16[80,768]{1,0:T(8,128)(2,1)S(1)}, u32[]{:S(2)}, u32[]{:S(2)}) collective-permute-start(bf16[80,768]{1,0:T(8,128)(2,1)S(1)} %get-tuple-element.125), channel_id=1, source_target_pairs={{0,1},{1,0},{2,3},{3,2},{4,5},{5,4},{6,7},{7,6},{8,9},{9,8},{10,11... | collective-permute-start | bytes 368648 | tf_op jit(solution)/shard_map/ppermute | solution.py:660
  37.3 7.8 %collective-permute-start.3 = (bf16[1,1,1,4,80,384]{5,4,3,2,1,0:T(8,128)(2,1)S(1)}, bf16[1,1,1,4,80,384]{5,4,3,2,1,0:T(8,128)(2,1)S(1)}, u32[]{:S(2)}, u32[]{:S(2)}) collective-permute-start(bf16[1,1,1,4,80,384]{5,4,3,2,1,0:T(8,128)(2,1)S(1)} %get-tuple-element.114), channel_id=1, source_target_pairs={{0,8},{4,12},{8,0},{12,4},{16,24},{20,28},{24,16},{28,20},{1,9},{5... | collective-permute-start | bytes 737288 | tf_op jit(solution)/shard_map/ppermute | solution.py:660
  38.9 6.2 %collective-permute-start.6 = (bf16[1,1,1,4,80,384]{5,4,3,2,1,0:T(8,128)(2,1)S(1)}, bf16[1,1,1,4,80,384]{5,4,3,2,1,0:T(8,128)(2,1)S(1)}, u32[]{:S(2)}, u32[]{:S(2)}) collective-permute-start(bf16[1,1,1,4,80,384]{5,4,3,2,1,0:T(8,128)(2,1)S(1)} %get-tuple-element.115), channel_id=1, source_target_pairs={{0,16},{4,20},{8,24},{12,28},{16,0},{20,4},{24,8},{28,12},{1,17},{... | collective-permute-start | bytes 737288 | tf_op jit(solution)/shard_map/ppermute | solution.py:660
  45.3 9.4 %collective-permute-start.7 = (bf16[2,1,1,4,80,384]{5,4,3,2,1,0:T(8,128)(2,1)S(1)}, bf16[2,1,1,4,80,384]{5,4,3,2,1,0:T(8,128)(2,1)S(1)}, u32[]{:S(2)}, u32[]{:S(2)}) collective-permute-start(bf16[2,1,1,4,80,384]{5,4,3,2,1,0:T(8,128)(2,1)S(1)} %pad_maximum_fusion.19), channel_id=1, source_target_pairs={{0,8},{4,12},{8,0},{12,4},{16,24},{20,28},{24,16},{28,20},{1,9},{5... | collective-permute-start | bytes 1474568 | tf_op jit(solution)/shard_map/ppermute | solution.py:660
  50.8 8.9 %collective-permute-start.4 = (bf16[1,2,1,4,80,384]{5,4,3,2,1,0:T(8,128)(2,1)S(1)}, bf16[1,2,1,4,80,384]{5,4,3,2,1,0:T(8,128)(2,1)S(1)}, u32[]{:S(2)}, u32[]{:S(2)}) collective-permute-start(bf16[1,2,1,4,80,384]{5,4,3,2,1,0:T(8,128)(2,1)S(1)} %pad_maximum_fusion.18), channel_id=1, source_target_pairs={{0,16},{4,20},{8,24},{12,28},{16,0},{20,4},{24,8},{28,12},{1,17},{... | collective-permute-start | bytes 1474568 | tf_op jit(solution)/shard_map/ppermute | solution.py:660
  54.9 8.1 %collective-permute-start.8 = (bf16[2,2,1,4,80,384]{5,4,3,2,1,0:T(8,128)(2,1)S(1)}, bf16[2,2,1,4,80,384]{5,4,3,2,1,0:T(8,128)(2,1)S(1)}, u32[]{:S(2)}, u32[]{:S(2)}) collective-permute-start(bf16[2,2,1,4,80,384]{5,4,3,2,1,0:T(8,128)(2,1)S(1)} %pad_maximum_fusion.9), channel_id=1, source_target_pairs={{0,4},{4,0},{8,12},{12,8},{16,20},{20,16},{24,28},{28,24},{1,5},{5... | collective-permute-start | bytes 2949128 | tf_op jit(solution)/shard_map/ppermute | solution.py:660
  60.0 3.3 collective-permute-start.5
  66.0 18.8 %copy-start.34 = (bf16[1,3,64,768]{3,2,1,0:T(8,128)(2,1)}, bf16[1,3,64,768]{3,2,1,0:T(8,128)(2,1)S(1)}, u32[]{:S(2)}) copy-start(bf16[1,3,64,768]{3,2,1,0:T(8,128)(2,1)S(1)} %constant_dynamic-slice_fusion.12) | copy-start | bytes 884740
  66.1 18.8 %copy-start.28 = (bf16[3,2,64,768]{3,2,1,0:T(8,128)(2,1)}, bf16[3,2,64,768]{3,2,1,0:T(8,128)(2,1)S(1)}, u32[]{:S(2)}) copy-start(bf16[3,2,64,768]{3,2,1,0:T(8,128)(2,1)S(1)} %copy.128) | copy-start | bytes 1769476
  116.0 35.8 %all-to-all-start = ((bf16[4,720,128]{2,1,0:T(8,128)(2,1)}), bf16[4,720,128]{2,1,0:T(8,128)(2,1)S(1)}, u32[]{:S(2)}, u32[]{:S(2)}) async-start(bf16[4,720,128]{2,1,0:T(8,128)(2,1)} %maximum_maximum_fusion.5), calls=%async_computation | async-start | bytes 1474560 | tf_op jit(solution)/shard_map/all_to_all | solution.py:938
  172.3 30.1 %copy-start.4 = (f32[480,768]{1,0:T(8,128)}, f32[480,768]{1,0:T(8,128)S(1)}, u32[]{:S(2)}) copy-start(f32[480,768]{1,0:T(8,128)S(1)} %multiply_add_fusion) | copy-start | bytes 4423684
  175.4 32.6 %all-to-all-start.1 = ((bf16[4,720,128]{2,1,0:T(8,128)(2,1)}), bf16[4,720,128]{2,1,0:T(8,128)(2,1)}, u32[]{:S(2)}, u32[]{:S(2)}) async-start(bf16[4,720,128]{2,1,0:T(8,128)(2,1)} %copy.135), calls=%async_computation.1 | async-start | bytes 1474560 | tf_op jit(solution)/shard_map/all_to_all | solution.py:969
  179.6 263.2 %reduce-scatter.2.cloned.1.call-start = ((), (), s32[]{:S(2)}) async-start(), calls=%async_computation.5 | async-start | bytes 3686400 | tf_op jit(solution)/shard_map/reduce_scatter | solution.py:1061
  212.0 41.3 %copy-start.65 = (bf16[1920,768]{1,0:T(8,128)(2,1)S(1)}, bf16[1920,768]{1,0:T(8,128)(2,1)}, u32[]{:S(2)}) copy-start(bf16[1920,768]{1,0:T(8,128)(2,1)} %get-tuple-element.45) | copy-start | bytes 8847364
  257.3 7.4 %collective-permute-start.9 = (bf16[2,2,1,72,768]{4,3,2,1,0:T(8,128)(2,1)S(1)}, bf16[2,2,1,72,768]{4,3,2,1,0:T(8,128)(2,1)S(1)}, u32[]{:S(2)}, u32[]{:S(2)}) collective-permute-start(bf16[2,2,1,72,768]{4,3,2,1,0:T(8,128)(2,1)S(1)} %constant_dynamic-slice_fusion.11), channel_id=1, source_target_pairs={{0,4},{4,0},{8,12},{12,8},{16,20},{20,16},{24,28},{28,24},{1,5},{5... | collective-permute-start | bytes 1327112 | tf_op jit(solution)/shard_map/ppermute | solution.py:660
  264.2 32.5 %collective-permute-start.23 = (bf16[2,2,1,4,132,768]{5,3,4,2,1,0:T(4,128)(2,1)}, bf16[2,2,1,4,132,768]{5,3,4,2,1,0:T(4,128)(2,1)}, u32[]{:S(2)}, u32[]{:S(2)}) collective-permute-start(bf16[2,2,1,4,132,768]{5,3,4,2,1,0:T(4,128)(2,1)} %constant_dynamic-slice_fusion.6), channel_id=1, source_target_pairs={{0,4},{4,0},{8,12},{12,8},{16,20},{20,16},{24,28},{28,24},{1,5},{5... | collective-permute-start | bytes 9732104 | tf_op jit(solution)/shard_map/ppermute | solution.py:660
  264.9 5.1 %collective-permute-start.12 = (bf16[1,2,1,72,384]{4,3,2,1,0:T(8,128)(2,1)S(1)}, bf16[1,2,1,72,384]{4,3,2,1,0:T(8,128)(2,1)S(1)}, u32[]{:S(2)}, u32[]{:S(2)}) collective-permute-start(bf16[1,2,1,72,384]{4,3,2,1,0:T(8,128)(2,1)S(1)} %constant_dynamic-slice_fusion.8), channel_id=1, source_target_pairs={{0,16},{4,20},{8,24},{12,28},{16,0},{20,4},{24,8},{28,12},{1,17},{... | collective-permute-start | bytes 331784 | tf_op jit(solution)/shard_map/ppermute | solution.py:660
  265.0 5.1 %collective-permute-start.10 = (bf16[2,1,1,72,384]{4,3,2,1,0:T(8,128)(2,1)S(1)}, bf16[2,1,1,72,384]{4,3,2,1,0:T(8,128)(2,1)S(1)}, u32[]{:S(2)}, u32[]{:S(2)}) collective-permute-start(bf16[2,1,1,72,384]{4,3,2,1,0:T(8,128)(2,1)S(1)} %constant_dynamic-slice_fusion.10), channel_id=1, source_target_pairs={{0,8},{4,12},{8,0},{12,4},{16,24},{20,28},{24,16},{28,20},{1,9},{5... | collective-permute-start | bytes 331784 | tf_op jit(solution)/shard_map/ppermute | solution.py:660
  270.0 4.2 collective-permute-start.13
  270.2 4.2 collective-permute-start.11
  274.4 13.5 %collective-permute-start.16 = (bf16[72,768]{1,0:T(8,128)(2,1)S(1)}, bf16[72,768]{1,0:T(8,128)(2,1)S(1)}, u32[]{:S(2)}, u32[]{:S(2)}) collective-permute-start(bf16[72,768]{1,0:T(8,128)(2,1)S(1)} %get-tuple-element.127), channel_id=1, source_target_pairs={{0,3},{1,2},{2,1},{3,0},{4,7},{5,6},{6,5},{7,4},{8,11},{9,10},{10,... | collective-permute-start | bytes 331784 | tf_op jit(solution)/shard_map/ppermute | solution.py:660
  278.2 9.7 %collective-permute-start.15 = (bf16[72,768]{1,0:T(8,128)(2,1)S(1)}, bf16[72,768]{1,0:T(8,128)(2,1)S(1)}, u32[]{:S(2)}, u32[]{:S(2)}) collective-permute-start(bf16[72,768]{1,0:T(8,128)(2,1)S(1)} %get-tuple-element.127), channel_id=1, source_target_pairs={{0,2},{1,3},{2,0},{3,1},{4,6},{5,7},{6,4},{7,5},{8,10},{9,11},{10,... | collective-permute-start | bytes 331784 | tf_op jit(solution)/shard_map/ppermute | solution.py:660
  278.2 9.7 %collective-permute-start.14 = (bf16[72,768]{1,0:T(8,128)(2,1)S(1)}, bf16[72,768]{1,0:T(8,128)(2,1)S(1)}, u32[]{:S(2)}, u32[]{:S(2)}) collective-permute-start(bf16[72,768]{1,0:T(8,128)(2,1)S(1)} %get-tuple-element.127), channel_id=1, source_target_pairs={{0,1},{1,0},{2,3},{3,2},{4,5},{5,4},{6,7},{7,6},{8,9},{9,8},{10,11... | collective-permute-start | bytes 331784 | tf_op jit(solution)/shard_map/ppermute | solution.py:660
  288.3 8.0 %collective-permute-start.20 = (bf16[1,1,1,4,72,384]{5,4,2,1,0,3:T(8,128)(2,1)S(1)}, bf16[1,1,1,4,72,384]{5,4,2,1,0,3:T(8,128)(2,1)S(1)}, u32[]{:S(2)}, u32[]{:S(2)}) collective-permute-start(bf16[1,1,1,4,72,384]{5,4,2,1,0,3:T(8,128)(2,1)S(1)} %get-tuple-element.117), channel_id=1, source_target_pairs={{0,16},{4,20},{8,24},{12,28},{16,0},{20,4},{24,8},{28,12},{1,17},{... | collective-permute-start | bytes 663560 | tf_op jit(solution)/shard_map/ppermute | solution.py:660
  294.4 9.9 %collective-permute-start.17 = (bf16[1,1,1,4,72,384]{5,4,3,2,1,0:T(8,128)(2,1)S(1)}, bf16[1,1,1,4,72,384]{5,4,3,2,1,0:T(8,128)(2,1)S(1)}, u32[]{:S(2)}, u32[]{:S(2)}) collective-permute-start(bf16[1,1,1,4,72,384]{5,4,3,2,1,0:T(8,128)(2,1)S(1)} %get-tuple-element.116), channel_id=1, source_target_pairs={{0,8},{4,12},{8,0},{12,4},{16,24},{20,28},{24,16},{28,20},{1,9},{5... | collective-permute-start | bytes 663560 | tf_op jit(solution)/shard_map/ppermute | solution.py:660
  296.4 15.9 %collective-permute-start.21 = (bf16[2,1,1,4,72,384]{5,4,2,1,0,3:T(8,128)(2,1)S(1)}, bf16[2,1,1,4,72,384]{5,4,2,1,0,3:T(8,128)(2,1)S(1)}, u32[]{:S(2)}, u32[]{:S(2)}) collective-permute-start(bf16[2,1,1,4,72,384]{5,4,2,1,0,3:T(8,128)(2,1)S(1)} %pad_maximum_fusion.23), channel_id=1, source_target_pairs={{0,8},{4,12},{8,0},{12,4},{16,24},{20,28},{24,16},{28,20},{1,9},{5... | collective-permute-start | bytes 1327112 | tf_op jit(solution)/shard_map/ppermute | solution.py:660
  302.6 21.1 %collective-permute-start.26 = (bf16[1,2,1,4,132,384]{5,3,4,2,1,0:T(4,128)(2,1)S(1)}, bf16[1,2,1,4,132,384]{5,3,4,2,1,0:T(4,128)(2,1)S(1)}, u32[]{:S(2)}, u32[]{:S(2)}) collective-permute-start(bf16[1,2,1,4,132,384]{5,3,4,2,1,0:T(4,128)(2,1)S(1)} %constant_dynamic-slice_fusion.3), channel_id=1, source_target_pairs={{0,16},{4,20},{8,24},{12,28},{16,0},{20,4},{24,8},{28,12},{1,17},{... | collective-permute-start | bytes 2433032 | tf_op jit(solution)/shard_map/ppermute | solution.py:660
  304.7 25.0 %collective-permute-start.24 = (bf16[2,1,1,4,132,384]{5,3,4,2,1,0:T(4,128)(2,1)S(1)}, bf16[2,1,1,4,132,384]{5,3,4,2,1,0:T(4,128)(2,1)S(1)}, u32[]{:S(2)}, u32[]{:S(2)}) collective-permute-start(bf16[2,1,1,4,132,384]{5,3,4,2,1,0:T(4,128)(2,1)S(1)} %constant_dynamic-slice_fusion.5), channel_id=1, source_target_pairs={{0,8},{4,12},{8,0},{12,4},{16,24},{20,28},{24,16},{28,20},{1,9},{5... | collective-permute-start | bytes 2433032 | tf_op jit(solution)/shard_map/ppermute | solution.py:660
  305.5 26.6 %collective-permute-start.18 = (bf16[1,2,1,4,72,384]{5,4,3,2,1,0:T(8,128)(2,1)S(1)}, bf16[1,2,1,4,72,384]{5,4,3,2,1,0:T(8,128)(2,1)S(1)}, u32[]{:S(2)}, u32[]{:S(2)}) collective-permute-start(bf16[1,2,1,4,72,384]{5,4,3,2,1,0:T(8,128)(2,1)S(1)} %pad_maximum_fusion.22), channel_id=1, source_target_pairs={{0,16},{4,20},{8,24},{12,28},{16,0},{20,4},{24,8},{28,12},{1,17},{... | collective-permute-start | bytes 1327112 | tf_op jit(solution)/shard_map/ppermute | solution.py:660
  313.4 35.3 %collective-permute-start.22 = (bf16[2,2,1,4,72,384]{5,4,2,1,0,3:T(8,128)(2,1)}, bf16[2,2,1,4,72,384]{5,4,2,1,0,3:T(8,128)(2,1)}, u32[]{:S(2)}, u32[]{:S(2)}) collective-permute-start(bf16[2,2,1,4,72,384]{5,4,2,1,0,3:T(8,128)(2,1)} %pad_maximum_fusion.13), channel_id=1, source_target_pairs={{0,4},{4,0},{8,12},{12,8},{16,20},{20,16},{24,28},{28,24},{1,5},{5... | collective-permute-start | bytes 2654216 | tf_op jit(solution)/shard_map/ppermute | solution.py:660
  324.3 10.5 %collective-permute-start.27 = (bf16[1,1,1,4,132,384]{5,3,4,2,1,0:T(4,128)(2,1)S(1)}, bf16[1,1,1,4,132,384]{5,3,4,2,1,0:T(4,128)(2,1)S(1)}, u32[]{:S(2)}, u32[]{:S(2)}) collective-permute-start(bf16[1,1,1,4,132,384]{5,3,4,2,1,0:T(4,128)(2,1)S(1)} %constant_dynamic-slice_fusion.2), channel_id=1, source_target_pairs={{0,8},{4,12},{8,0},{12,4},{16,24},{20,28},{24,16},{28,20},{1,9},{5... | collective-permute-start | bytes 1216520 | tf_op jit(solution)/shard_map/ppermute | solution.py:660
  330.3 8.0 %collective-permute-start.25 = (bf16[1,1,1,4,132,384]{5,3,4,2,1,0:T(4,128)(2,1)S(1)}, bf16[1,1,1,4,132,384]{5,3,4,2,1,0:T(4,128)(2,1)S(1)}, u32[]{:S(2)}, u32[]{:S(2)}) collective-permute-start(bf16[1,1,1,4,132,384]{5,3,4,2,1,0:T(4,128)(2,1)S(1)} %constant_dynamic-slice_fusion.4), channel_id=1, source_target_pairs={{0,16},{4,20},{8,24},{12,28},{16,0},{20,4},{24,8},{28,12},{1,17},{... | collective-permute-start | bytes 1216520 | tf_op jit(solution)/shard_map/ppermute | solution.py:660
  333.2 16.9 %collective-permute-start.19 = (bf16[2,2,1,4,72,384]{5,4,3,2,1,0:T(8,128)(2,1)}, bf16[2,2,1,4,72,384]{5,4,3,2,1,0:T(8,128)(2,1)}, u32[]{:S(2)}, u32[]{:S(2)}) collective-permute-start(bf16[2,2,1,4,72,384]{5,4,3,2,1,0:T(8,128)(2,1)} %pad_maximum_fusion.12), channel_id=1, source_target_pairs={{0,4},{4,0},{8,12},{12,8},{16,20},{20,16},{24,28},{28,24},{1,5},{5... | collective-permute-start | bytes 2654216 | tf_op jit(solution)/shard_map/ppermute | solution.py:660
  339.9 29.8 %all-to-all-start.2 = ((bf16[4,132,768]{2,1,0:T(8,128)(2,1)}), bf16[4,132,768]{2,1,0:T(8,128)(2,1)}, u32[]{:S(2)}, u32[]{:S(2)}) async-start(bf16[4,132,768]{2,1,0:T(8,128)(2,1)} %copy.144), calls=%async_computation.3 | async-start | bytes 1671168 | tf_op jit(solution)/shard_map/all_to_all | solution.py:697
  371.0 10.1 %collective-permute-start.30 = (bf16[132,768]{1,0:T(8,128)(2,1)S(1)}, bf16[132,768]{1,0:T(8,128)(2,1)S(1)}, u32[]{:S(2)}, u32[]{:S(2)}) collective-permute-start(bf16[132,768]{1,0:T(8,128)(2,1)S(1)} %convert_element_type.307), channel_id=1, source_target_pairs={{0,3},{1,2},{2,1},{3,0},{4,7},{5,6},{6,5},{7,4},{8,11},{9,10},{10,... | collective-permute-start | bytes 608264 | tf_op jit(solution)/shard_map/ppermute | solution.py:660
  372.5 16.3 %collective-permute-start.29 = (bf16[132,768]{1,0:T(8,128)(2,1)S(1)}, bf16[132,768]{1,0:T(8,128)(2,1)S(1)}, u32[]{:S(2)}, u32[]{:S(2)}) collective-permute-start(bf16[132,768]{1,0:T(8,128)(2,1)S(1)} %convert_element_type.307), channel_id=1, source_target_pairs={{0,2},{1,3},{2,0},{3,1},{4,6},{5,7},{6,4},{7,5},{8,10},{9,11},{10,... | collective-permute-start | bytes 608264 | tf_op jit(solution)/shard_map/ppermute | solution.py:660
  372.5 16.3 %collective-permute-start.28 = (bf16[132,768]{1,0:T(8,128)(2,1)S(1)}, bf16[132,768]{1,0:T(8,128)(2,1)S(1)}, u32[]{:S(2)}, u32[]{:S(2)}) collective-permute-start(bf16[132,768]{1,0:T(8,128)(2,1)S(1)} %convert_element_type.307), channel_id=1, source_target_pairs={{0,1},{1,0},{2,3},{3,2},{4,5},{5,4},{6,7},{7,6},{8,9},{9,8},{10,11... | collective-permute-start | bytes 608264 | tf_op jit(solution)/shard_map/ppermute | solution.py:660
  391.7 11.8 %collective-permute-start.34 = (bf16[1,1,1,4,132,384]{5,3,4,2,1,0:T(4,128)(2,1)}, bf16[1,1,1,4,132,384]{5,3,4,2,1,0:T(4,128)(2,1)}, u32[]{:S(2)}, u32[]{:S(2)}) collective-permute-start(bf16[1,1,1,4,132,384]{5,3,4,2,1,0:T(4,128)(2,1)} %bitcast.211), channel_id=1, source_target_pairs={{0,16},{4,20},{8,24},{12,28},{16,0},{20,4},{24,8},{28,12},{1,17},{... | collective-permute-start | bytes 1216520 | tf_op jit(solution)/shard_map/ppermute | solution.py:660
  402.0 12.4 %collective-permute-start.31 = (bf16[1,1,1,4,132,384]{5,3,4,2,1,0:T(4,128)(2,1)S(1)}, bf16[1,1,1,4,132,384]{5,3,4,2,1,0:T(4,128)(2,1)S(1)}, u32[]{:S(2)}, u32[]{:S(2)}) collective-permute-start(bf16[1,1,1,4,132,384]{5,3,4,2,1,0:T(4,128)(2,1)S(1)} %bitcast.275), channel_id=1, source_target_pairs={{0,8},{4,12},{8,0},{12,4},{16,24},{20,28},{24,16},{28,20},{1,9},{5... | collective-permute-start | bytes 1216520 | tf_op jit(solution)/shard_map/ppermute | solution.py:660
  405.6 24.2 %collective-permute-start.35 = (bf16[2,1,1,4,132,384]{5,3,4,2,1,0:T(4,128)(2,1)S(1)}, bf16[2,1,1,4,132,384]{5,3,4,2,1,0:T(4,128)(2,1)S(1)}, u32[]{:S(2)}, u32[]{:S(2)}) collective-permute-start(bf16[2,1,1,4,132,384]{5,3,4,2,1,0:T(4,128)(2,1)S(1)} %pad_maximum_fusion.16), channel_id=1, source_target_pairs={{0,8},{4,12},{8,0},{12,4},{16,24},{20,28},{24,16},{28,20},{1,9},{5... | collective-permute-start | bytes 2433032 | tf_op jit(solution)/shard_map/ppermute | solution.py:660
  416.3 19.6 %collective-permute-start.32 = (bf16[1,2,1,4,132,384]{5,3,4,2,1,0:T(4,128)(2,1)}, bf16[1,2,1,4,132,384]{5,3,4,2,1,0:T(4,128)(2,1)}, u32[]{:S(2)}, u32[]{:S(2)}) collective-permute-start(bf16[1,2,1,4,132,384]{5,3,4,2,1,0:T(4,128)(2,1)} %pad_maximum_fusion.15), channel_id=1, source_target_pairs={{0,16},{4,20},{8,24},{12,28},{16,0},{20,4},{24,8},{28,12},{1,17},{... | collective-permute-start | bytes 2433032 | tf_op jit(solution)/shard_map/ppermute | solution.py:660
  433.2 13.1 %collective-permute-start.36 = (bf16[2,2,1,4,132,384]{5,3,4,2,1,0:T(4,128)(2,1)}, bf16[2,2,1,4,132,384]{5,3,4,2,1,0:T(4,128)(2,1)}, u32[]{:S(2)}, u32[]{:S(2)}) collective-permute-start(bf16[2,2,1,4,132,384]{5,3,4,2,1,0:T(4,128)(2,1)} %pad_maximum_fusion.4), channel_id=1, source_target_pairs={{0,4},{4,0},{8,12},{12,8},{16,20},{20,16},{24,28},{28,24},{1,5},{5... | collective-permute-start | bytes 4866056 | tf_op jit(solution)/shard_map/ppermute | solution.py:660
  441.5 8.0 %collective-permute-start.33 = (bf16[2,2,1,4,132,384]{5,3,4,2,1,0:T(4,128)(2,1)}, bf16[2,2,1,4,132,384]{5,3,4,2,1,0:T(4,128)(2,1)}, u32[]{:S(2)}, u32[]{:S(2)}) collective-permute-start(bf16[2,2,1,4,132,384]{5,3,4,2,1,0:T(4,128)(2,1)} %pad_maximum_fusion.3), channel_id=1, source_target_pairs={{0,4},{4,0},{8,12},{12,8},{16,20},{20,16},{24,28},{28,24},{1,5},{5... | collective-permute-start | bytes 4866056 | tf_op jit(solution)/shard_map/ppermute | solution.py:660
  (68 other events, 259.1 us)
Sparse Core Ops, SparseCore 0:
  9.6 65.7 all-gather.7
  78.8 77.3 all-gather.9
  159.1 77.4 all-gather.11
  294.5 64.1 reduce-scatter.1

commit v3 on v2

--- a/solution.py
+++ b/solution.py
@@ -1,3 +1,4 @@
+import functools
 import math
 
 import jax
@@ -404,11 +405,13 @@
     )
 
 
-QUERY_TILE = 384
-KEY_STEP = 256
+QUERY_TILE = 480
+ROW_ALIGN = 16
+KEY_STEP = 512
 KEY_ALIGN = 128
 PREP_TILE = 480
 LANES = 128
+REFRESH_ROWS = 384
 MASK_BIT = -(2.0**100)
 NO_MAX = -3e38
 BF16 = jnp.bfloat16
@@ -436,6 +439,13 @@
     first = column.astype(BF16).astype(F32)
     second = (column - first).astype(BF16).astype(F32)
     return first, second, column - first - second
+
+
+def with_pieces(values, column, lane, at):
+    one, two, three = three_pieces(column)
+    return jnp.where(
+        lane == at, one, jnp.where(lane == at + 1, two, jnp.where(lane == at + 2, three, values))
+    ).astype(BF16)
 
 
 def project_kernel(
@@ -489,7 +499,7 @@
 
 
 def attend_kernel(
-    start_at, step_count, pad_from, query, key, value, pair_out, extra_out, wide_out, query_out
+    start_at, step_count, pad_from, query, key, value, pair_out, extra_out, query_out
 ):
     tile = pl.program_id(0)
     own_heads, rows, _ = query.shape
@@ -497,7 +507,7 @@
     low_lanes = lane < HEAD_DIM
     place = tile * rows + lax.broadcasted_iota(jnp.int32, (rows, 1), 0)
     padded = place >= pad_from[0]
-    own_rows = pl.ds(pl.multiple_of(tile * rows, KEY_ALIGN), rows)
+    own_rows = pl.ds(pl.multiple_of(tile * rows, ROW_ALIGN), rows)
     maxima, totals = [], []
     for head in range(own_heads):
         products = query[head].astype(F32) * key[head, own_rows, :].astype(F32)
@@ -525,18 +535,10 @@
     outs = []
     for head in range(own_heads):
         row_sum = totals[head][:, HEAD_DIM : HEAD_DIM + 1]
-        attended = jnp.where(low_lanes, totals[head] / row_sum, 0.0)
-        wide_out[head] = attended
-        outs.append(attended)
-        one, two, three = three_pieces(-(maxima[head] + jnp.log(row_sum)))
-        at = HEAD_DIM + 8
-        query_out[head] = jnp.where(
-            lane == at,
-            one,
-            jnp.where(
-                lane == at + 1, two, jnp.where(lane == at + 2, three, query[head].astype(F32))
-            ),
-        ).astype(BF16)
+        outs.append(jnp.where(low_lanes, totals[head] * (1.0 / row_sum), 0.0))
+        query_out[head] = with_pieces(
+            query[head].astype(F32), -(maxima[head] + jnp.log(row_sum)), lane, HEAD_DIM + 8
+        )
     pair_out[...] = (outs[0] + pltpu.roll(outs[1], HEAD_DIM, 1)).astype(BF16)
     extra_out[...] = outs[2].astype(BF16)
 
@@ -546,7 +548,8 @@
     step_count,
     pad_from,
     query,
-    wide,
+    pair_out,
+    extra_out,
     grad_pair,
     grad_extra,
     key,
@@ -571,23 +574,22 @@
     def accumulate():
         lane = lane_index(rows)
         low_lanes = lane < HEAD_DIM
-        own_rows = pl.ds(pl.multiple_of(tile * rows, KEY_ALIGN), rows)
+        own_rows = pl.ds(pl.multiple_of(tile * rows, ROW_ALIGN), rows)
         first = start_at[tile] * KEY_ALIGN
         pair = grad_pair[...].astype(F32)
-        incoming = [pair, pltpu.roll(pair, HEAD_DIM, 1), grad_extra[...].astype(F32)]
+        extra = grad_extra[...].astype(F32)
+        pair_product = pair * pair_out[...].astype(F32)
+        products = [
+            jnp.where(low_lanes, pair_product, 0.0),
+            jnp.where(low_lanes, 0.0, pair_product),
+            extra * extra_out[...].astype(F32),
+        ]
+        incoming = [pair, pltpu.roll(pair, HEAD_DIM, 1), extra]
         grads_out = []
         for head in range(own_heads):
             own = jnp.where(low_lanes, incoming[head], 0.0)
-            one, two, three = three_pieces(-jnp.sum(own * wide[head], axis=1, keepdims=True))
-            grads_out.append(
-                jnp.where(
-                    lane == HEAD_DIM,
-                    one,
-                    jnp.where(
-                        lane == HEAD_DIM + 1, two, jnp.where(lane == HEAD_DIM + 2, three, own)
-                    ),
-                ).astype(BF16)
-            )
+            delta = jnp.sum(products[head], axis=1, keepdims=True)
+            grads_out.append(with_pieces(own, -delta, lane, HEAD_DIM))
 
         def step(index, carry):
             at = pl.ds(pl.multiple_of(first + index * KEY_STEP, KEY_ALIGN), KEY_STEP)
@@ -629,11 +631,11 @@
     @pl.when(tile >= tile_count)
     def finish():
         size = grads.shape[0]
-        at = pl.ds(pl.multiple_of((tile - tile_count) * size, 16), size)
+        at = pl.ds(pl.multiple_of((tile - tile_count) * size, ROW_ALIGN), size)
         lane = lane_index(size)
         low_lanes = lane < HEAD_DIM
         first_half = lane % HEAD_DIM < HEAD_DIM // 2
-        values = []
+        values, turns = [], []
         for head in range(own_heads):
             both = jnp.where(
                 low_lanes,
@@ -646,8 +648,12 @@
                 pltpu.roll(shifted, LANES - HEAD_DIM // 2, 1),
                 -pltpu.roll(shifted, HEAD_DIM // 2, 1),
             )
-            grads[:, head * LANES : (head + 1) * LANES] = (both * cosine[...] + turned).astype(BF16)
+            turns.append(both * cosine[...] + turned)
             values.append(jnp.where(low_lanes, grad_value[head, at, :], 0.0))
+        swapped = pltpu.roll(turns[1], HEAD_DIM, 1)
+        grads[:, :LANES] = jnp.where(low_lanes, turns[0], swapped).astype(BF16)
+        grads[:, LANES : 2 * LANES] = jnp.where(low_lanes, turns[2], turns[0]).astype(BF16)
+        grads[:, 2 * LANES : 3 * LANES] = jnp.where(low_lanes, swapped, turns[2]).astype(BF16)
         base = own_heads * LANES
         grads[:, base : base + LANES] = (values[0] + pltpu.roll(values[1], HEAD_DIM, 1)).astype(
             BF16
@@ -655,69 +661,247 @@
         grads[:, base + LANES : base + 2 * LANES] = values[2].astype(BF16)
 
 
+def refresh_kernel(
+    full, own, select, stat_left, stat_right, root_left, right_root, weight, *refs, kept
+):
+    new_left, new_right, new_weight, columns, total = refs[kept:]
+    step = pl.program_id(0)
+    chosen = select.shape[0]
+    count = new_right.shape[-2]
+    outer = dot_rows(jnp.concatenate([select[...], own[...]]), full[...])
+    columns[...] = outer[:chosen]
+    new_left[0] = 0.5 * stat_left[0] + 0.5 * outer[chosen:]
+    left = jnp.concatenate([outer[:chosen].astype(BF16), root_left[0].astype(BF16)])
+    product = dot_plain(left, full[...])
+
+    @pl.when(step == 0)
+    def begin():
+        total[...] = product
+
+    @pl.when(step > 0)
+    def add():
+        total[...] += product
+
+    @pl.when(step == pl.num_programs(0) - 1)
+    def finish():
+        new_right[0] = 0.5 * stat_right[0] + 0.5 * total[:count, :]
+        update = dot_plain(total[chosen:, :].astype(BF16), right_root[...])
+        new_weight[0] = weight[0] - SHAMPOO_RATE * update
+
+
+def refresh(at, full, own, select, stat_left, stat_right, root_left, right_root, weight, previous):
+    in_dim, out_dim = full.shape
+    chunk = REFRESH_ROWS
+    rows, count, chosen = own.shape[0], stat_right.shape[1], select.shape[0]
+
+    def by_chunk(rows):
+        return pl.BlockSpec((1, rows, chunk), lambda i: (at, 0, i))
+
+    def whole(*shape):
+        return pl.BlockSpec(shape, lambda i: (0,) * len(shape))
+
+    def stacked(array):
+        return pl.BlockSpec((1,) + array.shape[1:], lambda i: (at, 0, 0))
+
+    kept = [pl.BlockSpec(memory_space=pl.ANY)] * len(previous)
+    return pl.pallas_call(
+        functools.partial(refresh_kernel, kept=len(previous)),
+        grid=(in_dim // chunk,),
+        in_specs=[
+            pl.BlockSpec((chunk, out_dim), lambda i: (i, 0)),
+            whole(*own.shape),
+            whole(*select.shape),
+            by_chunk(rows),
+            stacked(stat_right),
+            by_chunk(rows),
+            whole(*right_root.shape),
+            stacked(weight),
+        ]
+        + kept,
+        out_specs=[
+            by_chunk(rows),
+            stacked(stat_right),
+            stacked(weight),
+            pl.BlockSpec((chosen, chunk), lambda i: (0, i)),
+        ],
+        out_shape=[
+            jax.ShapeDtypeStruct(stat_left.shape, F32),
+            jax.ShapeDtypeStruct(stat_right.shape, F32),
+            jax.ShapeDtypeStruct(weight.shape, F32),
+            jax.ShapeDtypeStruct((chosen, in_dim), F32),
+        ],
+        scratch_shapes=[pltpu.VMEM((chosen + rows, out_dim), F32)],
+        input_output_aliases={8 + i: i for i in range(len(previous))},
+        compiler_params=pltpu.CompilerParams(vmem_limit_bytes=VMEM_BYTES),
+        cost_estimate=pl.CostEstimate(
+            flops=4 * (chosen + rows) * in_dim * out_dim,
+            bytes_accessed=2 * in_dim * out_dim + 12 * rows * in_dim + 2 * out_dim * out_dim,
+            transcendentals=0,
+        ),
+        name="refresh",
+    )(
+        full,
+        own,
+        select,
+        stat_left,
+        stat_right,
+        root_left,
+        right_root,
+        weight,
+        *previous,
+    )
+
+
 def exchange(values, axis, offset):
     size = lax.axis_size(axis)
     return lax.ppermute(values, axis, [(i, i ^ offset) for i in range(size)])
 
 
-def bit_count(size):
-    return size.bit_length() - 1
-
-
-def gather_blocks(values):
-    seq_count, dp_count = lax.axis_size("seq"), lax.axis_size("dp")
-    seq_at, dp_at = lax.axis_index("seq"), lax.axis_index("dp")
-    parts = jnp.stack([values] + [exchange(values, "seq", k) for k in range(1, seq_count)])
-    for bit in range(bit_count(seq_count)):
-        split = parts.reshape((seq_count >> (bit + 1), 2, 1 << bit) + values.shape)
-        split = jnp.where(((seq_at >> bit) & 1) == 1, split[:, ::-1], split)
-        parts = split.reshape((seq_count,) + values.shape)
-    bits = bit_count(dp_count)
-    half = values.shape[1] // 2
-
-    def spread(block, order):
-        block = block.reshape((1,) * bits + block.shape)
-        for bit in order:
-            other = exchange(block, "dp", 1 << bit)
-            upper = ((dp_at >> bit) & 1) == 1
-            block = jnp.concatenate(
-                [jnp.where(upper, other, block), jnp.where(upper, block, other)], bits - 1 - bit
-            )
-        return block
-
-    ahead = list(range(1, bits))
-    left = spread(parts[..., :half], ahead + [0])
-    right = spread(parts[..., half:], ahead[::-1] + [0])
-    return jnp.concatenate([left, right], -1).reshape((dp_count, seq_count) + values.shape)
-
-
-def sum_to_owner(values):
-    seq_count, dp_count = lax.axis_size("seq"), lax.axis_size("dp")
-    part = sum_over_dp(values)
-    pieces = lax.all_to_all(part, "seq", 0, 0, tiled=True)
-    return jnp.sum(pieces.astype(F32), axis=0)
-
-
-def sum_over_dp(values):
-    dp_count = lax.axis_size("dp")
-    dp_at = lax.axis_index("dp")
-    bits = bit_count(dp_count)
-
-    def halve(block, bit):
-        at = bits - 1 - bit
-        upper = (dp_at >> bit) & 1
-        send = lax.dynamic_index_in_dim(block, 1 - upper, at, keepdims=True)
-        keep = lax.dynamic_index_in_dim(block, upper, at, keepdims=True)
-        other = exchange(send, "dp", 1 << bit)
-        return (keep.astype(F32) + other.astype(F32)).astype(BF16)
-
-    block = halve(values.reshape((2,) * bits + values.shape[1:]), 0)
-    half = values.shape[-1] // 2
-    left, right = block[..., :half], block[..., half:]
-    for bit in range(1, bits):
-        left = halve(left, bit)
-        right = halve(right, bits - bit)
-    return jnp.concatenate([left, right], -1).reshape(values.shape[1:])
+def arrange_kernel(own_at, *refs, count, moves):
+    blocks, outs, sems = refs[:count], refs[count:-1], refs[-1]
+    copies = []
+    for index, (number, offset, source, which, target) in enumerate(moves):
+        place = own_at[0] ^ offset
+        start = blocks[number].at[source] if source else blocks[number]
+        end = outs[which].at[tuple(place if at == "place" else at for at in target)]
+        copies.append(pltpu.make_async_copy(start, end, sems.at[index]))
+    for copy in copies:
+        copy.start()
+    for copy in copies:
+        copy.wait()
+
+
+def arrange(blocks, own_at, shapes, moves):
+    count = len(blocks)
+    return pl.pallas_call(
+        functools.partial(arrange_kernel, count=count, moves=moves),
+        in_specs=[pl.BlockSpec(memory_space=pltpu.SMEM)]
+        + [pl.BlockSpec(memory_space=pl.ANY)] * count,
+        out_specs=[pl.BlockSpec(memory_space=pltpu.VMEM)] * len(shapes),
+        scratch_shapes=[pltpu.SemaphoreType.DMA((len(moves),))],
+        out_shape=[jax.ShapeDtypeStruct(shape, blocks[0].dtype) for shape in shapes],
+        compiler_params=pltpu.CompilerParams(vmem_limit_bytes=VMEM_BYTES),
+        cost_estimate=pl.CostEstimate(
+            flops=0, bytes_accessed=2 * count * blocks[0].size * 2, transcendentals=0
+        ),
+        name="arrange",
+    )(own_at[None], *blocks)
+
+
+def terms_kernel(
+    core, grad_proj, ffn_in, grad_out, attended, cotangent, middle, send, keep
+):
+    step = pl.program_id(0)
+    groups, rows, _ = send.shape
+    width = ffn_in.shape[1]
+    chunk = 2 * groups * rows
+    pieces = [(grad_proj, part * width, ffn_in) for part in range(grad_proj.shape[1] // width)]
+    pieces += [(grad_out, 0, attended), (cotangent, 0, middle)]
+    first = 0
+    for left, offset, right in pieces:
+        columns = pl.ds(pl.multiple_of(offset + step * chunk, KEY_ALIGN), chunk)
+        term = dot_first(left[:, columns], right[...]).astype(BF16)
+        last = first + right.shape[1]
+        for own in range(2):
+
+            @pl.when(core[0] == own)
+            def store():
+                for group in range(groups):
+                    for side, out in ((own, keep), (1 - own, send)):
+                        at = (2 * group + side) * rows
+                        out[group, :, first:last] = term[at : at + rows]
+
+        first = last
+
+
+def gather_plane(values, by_steps=False):
+    far = exchange(values, "seq", 2)
+    last = exchange(far, "seq", 1) if by_steps else exchange(values, "seq", 3)
+    blocks = [values, exchange(values, "seq", 1), far, last]
+    shape = (len(blocks),) + values.shape
+    moves = [(k, k, (), 0, ("place",)) for k in range(len(blocks))]
+    return arrange(blocks, lax.axis_index("seq"), [shape], moves)[0]
+
+
+def gather_partners(plane):
+    half = plane.shape[0] // 2
+    left, right = plane[:half], plane[half:]
+    left_two, right_four = exchange(left, "dp", 2), exchange(right, "dp", 4)
+    left_four, right_two = exchange(left, "dp", 4), exchange(right, "dp", 2)
+    left_six, right_six = exchange(left_two, "dp", 4), exchange(right_four, "dp", 2)
+    return [left, right, left_two, right_two, left_four, right_four, left_six, right_six]
+
+
+def gather_cores(even):
+    blocks = []
+    for k in range(0, len(even), 2):
+        blocks += [*even[k : k + 2], *(exchange(block, "dp", 1) for block in even[k : k + 2])]
+    return blocks
+
+
+def half_moves(blocks, cuts):
+    half = blocks[0].shape[0]
+    moves = []
+    for number in range(len(blocks)):
+        rows = slice(number % 2 * half, (number % 2 + 1) * half)
+        for source, which, target in cuts:
+            end = tuple(rows if at == "half" else at for at in target)
+            moves.append((number, number // 2, source, which, end))
+    return moves
+
+
+def column_moves(blocks, widths):
+    shapes, cuts, first = [], [], 0
+    half, rows, _ = blocks[0].shape
+    for which, width in enumerate(widths):
+        shapes.append((len(blocks) // 2, 2 * half, rows, width))
+        source = (slice(None), slice(None), slice(first, first + width))
+        cuts.append((source, which, ("place", "half")))
+        first += width
+    return shapes, half_moves(blocks, cuts)
+
+
+def fence(*values):
+    return lax.optimization_barrier(values)
+
+
+def add_blocks(blocks):
+    total = blocks[0].astype(F32)
+    for block in blocks[1:]:
+        total = total + block.astype(F32)
+    return total
+
+
+def pair_sums(send, keep, axis=0):
+    came = exchange(send, "dp", 1)
+    own_at = lax.axis_index("dp") >> 1
+    return [
+        add_blocks(
+            [
+                lax.dynamic_index_in_dim(side, own_at ^ k, axis, keepdims=False)
+                for side in (keep, came)
+            ]
+        )
+        for k in range(keep.shape[axis])
+    ]
+
+
+def add_partners(blocks, axis, unit):
+    return add_blocks(
+        blocks[:1] + [exchange(block, axis, k * unit) for k, block in enumerate(blocks) if k]
+    )
+
+
+def lows(blocks):
+    return [block.astype(BF16) for block in blocks]
+
+
+def by_distance(values, axis):
+    own_at = lax.axis_index(axis)
+    return [
+        lax.dynamic_index_in_dim(values, own_at ^ k, 0, keepdims=False)
+        for k in range(values.shape[0])
+    ]
 
 
 def head_body(
@@ -755,44 +939,38 @@
     own_heads = head_count // seq_count
     own_width = own_heads * HEAD_DIM
     in_rows = w_in.shape[1]
-    ao_rows, fo_rows = w_ao.shape[0], w_fo.shape[0]
-    out_rows = fo_rows * hidden // width
+    ao_rows = w_ao.shape[0]
     gain_cols = norm_gains.shape[1]
 
+    gain_lanes = jnp.zeros((in_rows, LANES), BF16).at[:2, :gain_cols].set(norm_gains.astype(BF16))
+    up_parts = in_rows // ao_rows
     row_tokens = lax.all_gather(tokens, "seq", axis=0, tiled=True)
-    gain_tile = jnp.zeros((8, width), F32).at[:2, :gain_cols].set(norm_gains)
-    first_pack = gather_blocks(jnp.concatenate([w_in[0].astype(BF16), gain_tile.astype(BF16)]))
-    full_qkv = first_pack[:, :, :in_rows].reshape(all_count * in_rows, width)
+    qkv_blocks = gather_cores(
+        gather_partners(gather_plane(jnp.concatenate([w_in[0].astype(BF16), gain_lanes], axis=1)))
+    )
+    full_qkv, gain_blocks = arrange(
+        qkv_blocks, lax.axis_index("dp"), *column_moves(qkv_blocks, [width, LANES])
+    )
+    full_qkv = full_qkv.reshape(all_count * in_rows, width)
     gain_rows = (
-        jnp.transpose(first_pack[:, :, in_rows : in_rows + 2, :gain_cols], (2, 0, 1, 3))
-        .reshape(2, width)
-        .astype(F32)
-    )
-    rest = jnp.concatenate(
-        [
-            w_in[1].astype(BF16),
-            w_ao.astype(BF16),
-            w_fo.astype(BF16).reshape(out_rows, width),
-        ]
-    )
-    rest = lax.all_gather(rest, ("dp", "seq"), axis=0, tiled=False)
-    full_up = rest[:, :in_rows].reshape(all_count * in_rows, width)
-    full_ao = rest[:, in_rows : in_rows + ao_rows].reshape(width, width)
-    full_fo = rest[:, in_rows + ao_rows :].reshape(width, hidden)
+        jnp.transpose(gain_blocks[:, :, :2, :gain_cols], (2, 0, 1, 3)).reshape(2, width).astype(F32)
+    )
+    full_up = lax.all_gather(w_in[1].astype(BF16), ("dp", "seq"), axis=0, tiled=True)
+    out_weights = jnp.concatenate([w_ao.astype(BF16), w_fo.astype(BF16)], axis=1)
+    row_tokens, out_weights = fence(row_tokens, out_weights)
+    out_plane = gather_plane(out_weights)
     root_rows = stat_r_in.shape[1]
-    fo_root_rows = root_r_fo.shape[0] * hidden // width
+    fo_columns = root_r_fo.shape[0] * hidden // root_rows
     roots = jnp.concatenate(
         [
-            root_r_in.astype(BF16).reshape(2 * root_rows, width),
+            root_r_in[0].astype(BF16),
+            root_r_in[1].astype(BF16),
             root_r_ao.astype(BF16),
-            root_r_fo.astype(BF16).reshape(fo_root_rows, width),
-        ]
-    )
-    roots = lax.all_gather(roots, ("dp", "seq"), axis=0, tiled=False)
-    right_qkv = roots[:, :root_rows].reshape(width, width)
-    right_up = roots[:, root_rows : 2 * root_rows].reshape(width, width)
-    right_ao = roots[:, 2 * root_rows : 3 * root_rows].reshape(width, width)
-    right_fo = roots[:, 3 * root_rows :].reshape(hidden, hidden)
+            root_r_fo.astype(BF16).reshape(root_rows, fo_columns),
+        ],
+        axis=1,
+    )
+    roots = lax.all_gather(roots, ("dp", "seq"), axis=0, tiled=True)
 
     lengths = doc_lengths[0]
     segment, within, is_valid = doc_tables(lengths, pad_counts[0], row_length)
@@ -835,19 +1013,22 @@
             jnp.zeros((HEAD_DIM, width), BF16),
         ]
     )
+    back_weight = jnp.concatenate(
+        [qkv_heads.reshape(3 * own_width, width), jnp.zeros((HEAD_DIM, width), BF16)]
+    )
     own_columns = own_weight.shape[0]
     prep_count = row_length // PREP_TILE
     key_length = row_length + PREP_TILE
 
     def row_block(columns):
         return pl.BlockSpec(
-            (PREP_TILE, columns), lambda i: (jnp.minimum(i, prep_count - 1), 0)
+            (PREP_TILE, columns), lambda i, *_: (jnp.minimum(i, prep_count - 1), 0)
         )
 
     def fixed_block(*shape):
         return pl.BlockSpec(shape, lambda i, *_: (0,) * len(shape))
 
-    head_block = pl.BlockSpec((own_heads, PREP_TILE, LANES), lambda i: (0, i, 0))
+    head_block = pl.BlockSpec((own_heads, PREP_TILE, LANES), lambda i, *_: (0, i, 0))
     attn_in, query_ext, key_ext, value_ext = pl.pallas_call(
         project_kernel,
         grid=(prep_count + 1,),
@@ -891,6 +1072,9 @@
         key_mask,
     )
 
+    query_ext, key_ext, value_ext, out_plane = fence(query_ext, key_ext, value_ext, out_plane)
+    out_partners = gather_partners(out_plane)
+
     def tile_block(columns):
         return pl.BlockSpec(
             (QUERY_TILE, columns), lambda i, *_: (jnp.minimum(i, tile_count - 1), 0)
@@ -900,18 +1084,17 @@
         (own_heads, QUERY_TILE, LANES), lambda i, *_: (0, jnp.minimum(i, tile_count - 1), 0)
     )
     whole_keys = fixed_block(own_heads, key_length, LANES)
-    pair_out, extra_out, wide_out, query_low = pl.pallas_call(
+    pair_out, extra_out, query_low = pl.pallas_call(
         attend_kernel,
         grid_spec=pltpu.PrefetchScalarGridSpec(
             num_scalar_prefetch=3,
             grid=(tile_count,),
             in_specs=[head_tile, whole_keys, whole_keys],
-            out_specs=[tile_block(LANES), tile_block(LANES), head_tile, head_tile],
+            out_specs=[tile_block(LANES), tile_block(LANES), head_tile],
         ),
         out_shape=[
             jax.ShapeDtypeStruct((row_length, LANES), BF16),
             jax.ShapeDtypeStruct((row_length, LANES), BF16),
-            jax.ShapeDtypeStruct((own_heads, row_length, LANES), F32),
             jax.ShapeDtypeStruct((own_heads, row_length, LANES), BF16),
         ],
         compiler_params=pltpu.CompilerParams(vmem_limit_bytes=VMEM_BYTES),
@@ -922,6 +1105,15 @@
         ),
         name="attend",
     )(tile_starts, tile_steps, pad_at, query_ext, key_ext, value_ext)
+
+    fenced = fence(pair_out, extra_out, query_low, *out_partners)
+    pair_out, extra_out, query_low = fenced[:3]
+    out_blocks = gather_cores(fenced[3:])
+    full_ao, full_fo = arrange(
+        out_blocks, lax.axis_index("dp"), *column_moves(out_blocks, [width, hidden])
+    )
+    full_ao = full_ao.reshape(width, width)
+    full_fo = full_fo.reshape(width, hidden)
 
     half_tokens = token_count // 2
 
@@ -966,30 +1158,56 @@
     packed_back = jnp.concatenate(
         [grad_blocks[:, :, :LANES], jnp.concatenate([folded[:, 0], folded[:, 1]], axis=-1)], axis=1
     )
-    packed_back = lax.all_to_all(packed_back, "seq", 0, 0, tiled=True)
-    grad_pair = packed_back[:, :token_count].reshape(row_length, LANES)
-    grad_extra = unfold(packed_back[:, token_count:]).reshape(row_length, HEAD_DIM)
+    back_blocks = by_distance(packed_back, "seq")
+    back_blocks = [back_blocks[0]] + [
+        exchange(block, "seq", k) for k, block in enumerate(back_blocks) if k
+    ]
+
+    pack_width = up_parts * width + width + hidden
+    pair_count = dp_count // 2
+    block_rows = seq_count * ao_rows
+    core = lax.axis_index("dp") & 1
+    operands = (grad_proj, ffn_in, grad_out_attn, attn_low, cotangent, mid_low)
+    half_block = pl.BlockSpec((pair_count // 2, block_rows, pack_width), lambda i: (i, 0, 0))
+    send_terms, keep_terms = pl.pallas_call(
+        terms_kernel,
+        grid=(2,),
+        in_specs=[pl.BlockSpec(memory_space=pltpu.SMEM)]
+        + [pl.BlockSpec(operand.shape, lambda i: (0, 0)) for operand in operands],
+        out_specs=[half_block, half_block],
+        out_shape=[jax.ShapeDtypeStruct((pair_count, block_rows, pack_width), BF16)] * 2,
+        compiler_params=pltpu.CompilerParams(vmem_limit_bytes=VMEM_BYTES),
+        cost_estimate=pl.CostEstimate(
+            flops=2 * token_count * width * pack_width,
+            bytes_accessed=13_000_000,
+            transcendentals=0,
+        ),
+        name="terms",
+    )(core[None], *operands)
+    fenced = fence(send_terms, *back_blocks)
+    send_terms, back_blocks = fenced[0], fenced[1:]
+    pair_blocks = lows(pair_sums(send_terms, keep_terms))
+    folded_tokens = token_count + half_tokens
+    grad_pair, grad_extra = arrange(
+        back_blocks,
+        seq_at,
+        [(seq_count, token_count, LANES), (seq_count, half_tokens, LANES)],
+        [
+            (k, k, (rows,), which, ("place",))
+            for k in range(seq_count)
+            for which, rows in enumerate(
+                (slice(0, token_count), slice(token_count, folded_tokens))
+            )
+        ],
+    )
+    grad_pair = grad_pair.reshape(row_length, LANES)
+    grad_extra = unfold(grad_extra).reshape(row_length, HEAD_DIM)
     grad_extra = jnp.pad(grad_extra, ((0, 0), (0, LANES - HEAD_DIM)))
-
-    grad_up_term = outer_sum(grad_proj, ffn_in).astype(BF16).reshape(all_count, in_rows, width)
-    grad_ao_term = outer_sum(grad_out_attn, attn_low).astype(BF16)
-    grad_fo_term = outer_sum(cotangent, mid_low).astype(BF16)
-    terms = jnp.concatenate(
-        [
-            grad_up_term,
-            grad_ao_term.reshape(all_count, ao_rows, width),
-            grad_fo_term.reshape(all_count, out_rows, width),
-        ],
-        axis=1,
-    )
-    summed = sum_to_owner(terms.reshape((dp_count, seq_count) + terms.shape[1:]))
-    summed_up = summed[:in_rows]
-    summed_ao = summed[in_rows : in_rows + ao_rows]
-    summed_fo = summed[in_rows + ao_rows :].reshape(fo_rows, hidden)
-    whole = gather_blocks(summed.astype(BF16)).reshape(all_count, summed.shape[0], width)
-    whole_up = whole[:, :in_rows].reshape(all_count * in_rows, width)
-    whole_ao = whole[:, in_rows : in_rows + ao_rows].reshape(width, width)
-    whole_fo = whole[:, in_rows + ao_rows :].reshape(width, hidden)
+    fenced = fence(grad_pair, grad_extra, *pair_blocks)
+    grad_pair, grad_extra, pair_blocks = fenced[0], fenced[1], fenced[2:]
+    plane_blocks = [pair_blocks[0]] + [
+        exchange(block, "dp", 2 * k) for k, block in enumerate(pair_blocks) if k
+    ]
 
     finish_count = prep_count
 
@@ -1005,7 +1223,8 @@
             grid=(tile_count + finish_count,),
             in_specs=[
                 head_tile,
-                head_tile,
+                tile_block(LANES),
+                tile_block(LANES),
                 tile_block(LANES),
                 tile_block(LANES),
                 whole_keys,
@@ -1033,7 +1252,8 @@
         tile_steps,
         pad_at,
         query_low,
-        wide_out,
+        pair_out,
+        extra_out,
         grad_pair,
         grad_extra,
         key_ext,
@@ -1041,86 +1261,145 @@
         cos_table,
         sin_table,
     )
+    right_qkv = roots[:, :width]
+    right_up = roots[:, width : 2 * width]
+    right_ao = roots[:, 2 * width : 3 * width]
+    right_fo = roots[:, 3 * width :].reshape(hidden, hidden)
+    fenced = fence(grad_qkv, *plane_blocks)
+    grad_qkv = fenced[0]
+    plane_sum = add_blocks(fenced[1:]).astype(BF16).reshape(seq_count, ao_rows, pack_width)
+    summed = add_partners(by_distance(plane_sum, "seq"), "seq", 1)
+    low_sum = summed.astype(BF16)
+    term_plane = gather_plane(low_sum, by_steps=True)
+    low_ao = low_sum[:, up_parts * width : (up_parts + 1) * width]
+    low_fo = low_sum[:, (up_parts + 1) * width :]
+    summed_ao = summed[:, up_parts * width : (up_parts + 1) * width]
+    summed_fo = summed[:, (up_parts + 1) * width :]
+
     qkv_term = outer_sum(grad_qkv, attn_in)[: 3 * own_width].astype(BF16)
-    qkv_sum = sum_over_dp(qkv_term.reshape(dp_count, 3 * own_width // dp_count, width))
-    qkv_parts = jnp.transpose(gather_blocks(qkv_sum), (1, 0, 2, 3)).reshape(
-        seq_count, 3 * own_width, width
-    )
-    whole_query_key = qkv_parts[:, : 2 * own_width].reshape(
-        seq_count, own_heads, 2, HEAD_DIM, width
-    )
-    whole_qkv = jnp.concatenate(
-        [
-            jnp.transpose(whole_query_key, (2, 0, 1, 3, 4)),
-            qkv_parts[:, 2 * own_width :].reshape(1, seq_count, own_heads, HEAD_DIM, width),
-        ]
-    ).reshape(3 * width, width)
-    summed_qkv = lax.dynamic_slice_in_dim(whole_qkv, dev_at * in_rows, in_rows, 0).astype(F32)
-
-    input_term = jnp.dot(grad_qkv, own_weight, preferred_element_type=F32).astype(BF16)
+    qkv_rows = own_width // dp_count
+    qkv_term = qkv_term.reshape(3, pair_count, 2, qkv_rows, width)
+    qkv_halves = [
+        lax.dynamic_index_in_dim(qkv_term, side, 2, keepdims=False) for side in (1 - core, core)
+    ]
+    qkv_sum = add_partners(lows(pair_sums(*qkv_halves, axis=1)), "dp", 2).astype(BF16)
+    qkv_plane = gather_plane(qkv_sum, by_steps=True)
+    grad_qkv = fence(grad_qkv, qkv_plane, term_plane)[0]
+    fenced = fence(right_fo, *gather_partners(qkv_plane))
+    right_fo, qkv_blocks = fenced[0], gather_cores(fenced[1:])
+    [whole_qkv] = arrange(
+        qkv_blocks,
+        lax.axis_index("dp"),
+        [(3, seq_count, dp_count, qkv_rows, width)],
+        half_moves(qkv_blocks, [((slice(None), part), 0, (part, "half", "place")) for part in range(3)]),
+    )
+    whole_qkv = whole_qkv.reshape(3 * width, width)
+    low_qkv = lax.dynamic_slice_in_dim(whole_qkv, dev_at * in_rows, in_rows, 0)
+
+    input_term = jnp.dot(grad_qkv, back_weight, preferred_element_type=F32).astype(BF16)
     grad_attn_in = lax.psum_scatter(input_term, "seq", scatter_dimension=0, tiled=True).astype(F32)
     normed_one, spread_one = norm_forward(inputs)
     grad_norm_one, _ = norm_backward(grad_attn_in, normed_one, spread_one, gain_rows[0])
     grad_input = grad_resid + grad_norm_one
 
-    def own_columns_of(matrix, count):
-        return lax.dynamic_slice_in_dim(matrix, dev_at * count, count, 1)
-
-    def gain_gradient(weight, gradient, gain):
-        own_weight_columns = own_columns_of(weight, gain_cols).astype(F32)
-        products = own_weight_columns * own_columns_of(gradient, gain_cols).astype(F32)
+    def select(count, size):
+        places = jnp.arange(-(-count // 16) * 16, dtype=jnp.int32)[:, None]
+        wanted = jnp.where(places < count, dev_at * count + places, -1)
+        return (wanted == jnp.arange(size, dtype=jnp.int32)[None, :]).astype(BF16)
+
+    select_in = select(stat_r_in.shape[1], width)
+    select_fo = select(stat_r_fo.shape[0], hidden)
+    *stacked, qkv_columns = refresh(
+        0, whole_qkv, low_qkv, select_in, stat_l_in, stat_r_in, root_l_in, right_qkv, w_in, []
+    )
+    term_partners = gather_partners(term_plane)
+    fenced = fence(stacked, *term_partners)
+    stacked, term_blocks = fenced[0], gather_cores(fenced[1:])
+    whole_shape = (dp_count, seq_count, ao_rows)
+    cut = (slice(None), slice(None))
+    whole_up, whole_ao, whole_fo = arrange(
+        term_blocks,
+        lax.axis_index("dp"),
+        [(up_parts,) + whole_shape + (width,), whole_shape + (width,), whole_shape + (hidden,)],
+        half_moves(
+            term_blocks,
+            [
+                (cut + (slice(part * width, (part + 1) * width),), 0, (part, "place", "half"))
+                for part in range(up_parts)
+            ]
+            + [
+                (cut + (slice(up_parts * width, (up_parts + 1) * width),), 1, ("place", "half")),
+                (cut + (slice((up_parts + 1) * width, pack_width),), 2, ("place", "half")),
+            ],
+        ),
+    )
+    whole_up = whole_up.reshape(up_parts * width, width)
+    whole_ao = whole_ao.reshape(width, width)
+    whole_fo = whole_fo.reshape(width, hidden)
+    low_up = lax.dynamic_slice_in_dim(whole_up, dev_at * in_rows, in_rows, 0)
+    left_ao, right_stat_ao, new_ao, _ = refresh(
+        0,
+        whole_ao,
+        low_ao,
+        select_in,
+        stat_l_ao[None],
+        stat_r_ao[None],
+        root_l_ao[None],
+        right_ao,
+        w_ao[None],
+        [],
+    )
+    left_fo, right_stat_fo, new_fo, _ = refresh(
+        0,
+        whole_fo,
+        low_fo,
+        select_fo,
+        stat_l_fo[None],
+        stat_r_fo[None],
+        root_l_fo[None],
+        right_fo,
+        w_fo[None],
+        [],
+    )
+    *stacked, up_columns = refresh(
+        1, whole_up, low_up, select_in, stat_l_in, stat_r_in, root_l_in, right_up, w_in, stacked
+    )
+    new_left_in, new_right_in, new_in = stacked
+
+    def gain_gradient(weight, columns, gain):
+        own_weight_columns = lax.dynamic_slice_in_dim(weight, dev_at * gain_cols, gain_cols, 1)
+        products = jnp.transpose(own_weight_columns).astype(F32) * columns[:gain_cols]
         own_gain = lax.dynamic_slice_in_dim(gain, dev_at * gain_cols, gain_cols)
-        return jnp.sum(products, axis=0) / own_gain
+        return jnp.sum(products, axis=1) / own_gain
 
     summed_gains = jnp.stack(
         [
-            gain_gradient(full_qkv, whole_qkv, gain_rows[0]),
-            gain_gradient(full_up, whole_up, gain_rows[1]),
+            gain_gradient(full_qkv, qkv_columns, gain_rows[0]),
+            gain_gradient(full_up, up_columns, gain_rows[1]),
         ]
     )
     new_moment = 0.9 * gain_moment + 0.1 * summed_gains
     new_second = 0.999 * gain_second + 0.001 * summed_gains * summed_gains
     new_gains = norm_gains - ADAM_RATE * new_moment / (jnp.sqrt(new_second) + 1e-08)
-
-    def refresh(weight, own, full, stat_left, stat_right, root_left, right):
-        new_left = 0.5 * stat_left + 0.5 * apply_rows(own.astype(BF16), full)
-        columns = own_columns_of(full, stat_right.shape[0])
-        new_right = 0.5 * stat_right + 0.5 * outer_sum(columns, full)
-        left_product = jnp.dot(root_left.astype(BF16), full, preferred_element_type=F32)
-        update = jnp.dot(left_product.astype(BF16), right, preferred_element_type=F32)
-        return new_left, new_right, weight - SHAMPOO_RATE * update
-
-    left_up, right_stat_up, new_up = refresh(
-        w_in[1], summed_up, whole_up, stat_l_in[1], stat_r_in[1], root_l_in[1], right_up
-    )
-    left_ao, right_stat_ao, new_ao = refresh(
-        w_ao, summed_ao, whole_ao, stat_l_ao, stat_r_ao, root_l_ao, right_ao
-    )
-    left_fo, right_stat_fo, new_fo = refresh(
-        w_fo, summed_fo, whole_fo, stat_l_fo, stat_r_fo, root_l_fo, right_fo
-    )
-    left_qkv, right_stat_qkv, new_qkv = refresh(
-        w_in[0], summed_qkv, whole_qkv, stat_l_in[0], stat_r_in[0], root_l_in[0], right_qkv
-    )
     return (
         layer_out,
         grad_input,
-        jnp.stack([summed_qkv, summed_up]),
+        jnp.stack([low_qkv, low_up]).astype(F32),
         summed_ao,
         summed_fo,
         summed_gains,
         new_moment,
         new_second,
         new_gains,
-        jnp.stack([left_qkv, left_up]),
-        jnp.stack([right_stat_qkv, right_stat_up]),
-        left_ao,
-        right_stat_ao,
-        left_fo,
-        right_stat_fo,
-        jnp.stack([new_qkv, new_up]),
-        new_ao,
-        new_fo,
+        new_left_in,
+        new_right_in,
+        left_ao[0],
+        right_stat_ao[0],
+        left_fo[0],
+        right_stat_fo[0],
+        new_in,
+        new_ao[0],
+        new_fo[0],
     )
 
 
@@ -1133,7 +1412,10 @@
         and dp_count & (dp_count - 1) == 0
         and seq_count & (seq_count - 1) == 0
         and row_length % QUERY_TILE == 0
-        and row_length % PREP_TILE == 0
+        and token_count == PREP_TILE
+        and dp_count == 8
+        and seq_count == 4
+        and others[3].shape[1] == 3 * others[4].shape[0]
         and others[1].shape[1] == 8
     )
     return head_body(tokens, *others) if by_heads else sequence_body(tokens, *others)

time: 501 us -> 446 us (0.89)
  waiting for transfers between devices: 145 us -> 73.3 us
  Pallas kernels: 78.6 us -> 133 us
  other arithmetic: 72.8 us -> 39.8 us
  matrix products: 52.3 us -> 25.1 us
  starting transfers between devices: 54.6 us -> 78.5 us
    pallas_call x0 -> x14, Pallas kernels: none -> 65.3 us  [the longest x9 29.1 us: arrange(): pl.pallas_call(functools.partial(arrange_kernel, count=count, moves=moves...]
    ppermute x37 -> x82, starting transfers between devices: 41.1 us -> 74.9 us  [exchange(): return lax.ppermute(values, axis, [(i, i ^ offset) for i in range(size)])]
    ppermute x37 -> x82, waiting for transfers between devices: 86.4 us -> 60.7 us  [exchange(): return lax.ppermute(values, axis, [(i, i ^ offset) for i in range(size)])]
    all_to_all x1, waiting for transfers between devices: 29.9 us -> 7.02 us  [head_body(): packed = lax.all_to_all(packed, 'seq', 0, 0, tiled=True)]
    all_to_all x2 -> x0, waiting for transfers between devices: 16.7 us -> none  [the longest x1 16.7 us: sum_to_owner(): pieces = lax.all_to_all(part, 'seq', 0, 0, tiled=True)]
    select_n x20 -> x2, other arithmetic: 15.5 us -> 0.01 us  [select(): wanted = jnp.where(places < count, dev_at * count + places, -1)]
    convert_element_type x3 -> x1, local copies, waits for them, and re-layouts: 14.8 us -> 0.01 us  [head_body(): root_r_in[0].astype(BF16)]
    dot_general x8 -> x1, matrix products: 16.9 us -> 3.95 us  [outer_sum(): lax.dot_general(grad_rows, act_rows, (((0,), (0,)), ((), ())), preferred_...]
  transfers between devices with their start and end apart: 44 -> 87, of which waited for: 21 -> 22; matrix products, arithmetic and copies ran while one was open for 31% -> 29% of each run, Pallas kernels for 16% -> 30%
where the time goes in v3:
time: 446 us; the launch traced here: 444 us
  Pallas kernels  133 us (30%)
  starting transfers between devices  78.5 us (18%)
  local copies, waits for them, and re-layouts  78.1 us (18%)
  waiting for transfers between devices  73.3 us (16%)
  other arithmetic  39.8 us (9%)
  matrix products  25.1 us (6%)
  between operations  16.2 us (4%)
    ppermute x82, starting transfers between devices, exchange(): return lax.ppermute(values, axis, [(i, i ^ offset) for i in range(size)])  74.9 us
    ppermute x82, waiting for transfers between devices, exchange(): return lax.ppermute(values, axis, [(i, i ^ offset) for i in range(size)])  60.7 us
    pallas_call x1, Pallas kernels, head_body(): pl.pallas_call(attend_back_kernel, grid_spec=pltpu.PrefetchScalarGridSpec...  34.3 us
    pallas_call x9, Pallas kernels, arrange(): pl.pallas_call(functools.partial(arrange_kernel, count=count, moves=moves...  29.1 us
    pallas_call x4, Pallas kernels, refresh(): pl.pallas_call(functools.partial(refresh_kernel, kept=len(previous)), gri...  24.8 us
    pallas_call x1, Pallas kernels, head_body(): pl.pallas_call(attend_kernel, grid_spec=pltpu.PrefetchScalarGridSpec(num_...  23.8 us
    transpose x1, local copies, waits for them, and re-layouts, head_body(): attn_low = jnp.transpose(attn_low, (1, 0, 2)).reshape(token_count, width)  13.1 us
    pallas_call x1, Pallas kernels, head_body(): pl.pallas_call(terms_kernel, grid=(2,), in_specs=[pl.BlockSpec(memory_spa...  11.4 us
  transfers between devices with their start and end apart: 87, of which 22 were waited for; matrix products, arithmetic and copies ran while one was open for 29% of the time, Pallas kernels for 30%

profile of v3, /device:TPU:0, one launch (start us, length us, event | category | flops | bytes accessed | tf_op | source)
XLA Modules:
  0.0 443.9 jit_solution(2870843005320657695)
XLA Ops:
  10.4 3.1 collective-permute-start
  13.5 2.6 collective-permute-start.1
  16.5 3.5 multiply_sine_fusion
  20.7 10.9 %collective-permute-done.1.refs_2_ = bf16[72,896]{1,0:T(8,128)(2,1)S(1)} collective-permute-done((bf16[72,896]{1,0:T(8,128)(2,1)S(1)}, bf16[72,896]{1,0:T(8,128)(2,1)S(1)}, u32[]{:S(2)}, u32[]{:S(2)}) %collective-permute-start.1) | collective-permute-done | bytes 129056 | tf_op jit(solution)/shard_map/ppermute | solution.py:757
  38.8 2.6 select_convert_fusion.key_mask
  52.4 4.4 %collective-permute-done.13.refs_12_ = bf16[2,72,896]{2,1,0:T(8,128)(2,1)} collective-permute-done((bf16[2,72,896]{2,1,0:T(8,128)(2,1)S(1)}, bf16[2,72,896]{2,1,0:T(8,128)(2,1)}, u32[]{:S(2)}, u32[]{:S(2)}) %collective-permute-start.13) | collective-permute-done | bytes 258080 | tf_op jit(solution)/shard_map/ppermute | solution.py:757
  57.4 2.9 pad_maximum_fusion.1
  61.4 4.5 %arrange.10 = (bf16[8,4,72,768]{3,2,1,0:T(8,128)(2,1)}, bf16[8,4,72,128]{3,2,1,0:T(8,128)(2,1)}) custom-call(s32[1]{0:T(128)} %bitcast.4.own_at, bf16[2,72,896]{2,1,0:T(8,128)(2,1)} %copy-done.12, bf16[2,72,896]{2,1,0:T(8,128)(2,1)} %copy-done.11, bf16[2,72,896]{2,1,0:T(8,128)(2,1)} %copy-done.39, bf16[2,72,896]{2,1,0:T(8,128)(2,1)} %copy-done.41, ...), custom_call_target="tpu_custom_call" | custom-call | bytes 8257536 | tf_op jit(solution)/shard_map/arrange/pallas_call | solution.py:776
  70.9 4.8 %all-gather.5.cloned.1.call-done.tokens = bf16[1920,768]{1,0:T(8,128)(2,1)} async-done(((bf16[480,768]{1,0:T(8,128)(2,1)}), bf16[1920,768]{1,0:T(8,128)(2,1)}) %all-gather.5.cloned.1.call-update) | async-done | bytes 2949136 | tf_op jit(solution)/shard_map/all_gather | solution.py:947
  75.7 5.9 %collective-permute-start.17 = (bf16[24,1920]{1,0:T(8,128)(2,1)S(1)}, bf16[24,1920]{1,0:T(8,128)(2,1)S(1)}, u32[]{:S(2)}, u32[]{:S(2)}) collective-permute-start(bf16[24,1920]{1,0:T(8,128)(2,1)S(1)} %pad_maximum_fusion.5.refs_0_), channel_id=1, source_target_pairs={{0,1},{1,0},{2,3},{3,2},{4,5},{5,4},{6,7},{7,6},{8,9},{9,8},{10,11... | collective-permute-start | bytes 276488 | tf_op jit(solution)/shard_map/ppermute | solution.py:757
  85.0 9.5 %project.1 = (bf16[1920,768]{1,0:T(8,128)(2,1)}, bf16[3,1920,128]{2,1,0:T(8,128)(2,1)}, bf16[3,2400,128]{2,1,0:T(8,128)(2,1)}, bf16[3,2400,128]{2,1,0:T(8,128)(2,1)}) custom-call(bf16[1920,768]{1,0:T(8,128)(2,1)} %all-gather.5.cloned.1.call-done.tokens, bf16[640,768]{1,0:T(8,128)(2,1)} %maximum_maximum_fusion.weight, f32[1,768]{1,0:T(1,128)} %slice.179.gain, ...), custom_call_target="tpu_custom_call" | custom-call | flops 1887436800 | bytes 14000000 | tf_op jit(solution)/shard_map/project/pallas_call | solution.py:1032
  103.3 3.0 collective-permute-done.20.refs_4_
  108.6 23.8 %attend.1 = (bf16[1920,128]{1,0:T(8,128)(2,1)}, bf16[1920,128]{1,0:T(8,128)(2,1)}, bf16[3,1920,128]{2,1,0:T(8,128)(2,1)}) custom-call(s32[4]{0:T(128)} %get-tuple-element.219.start_at, s32[4]{0:T(128)} %get-tuple-element.218.step_count, s32[1]{0:T(128)} %sub.83.pad_from, bf16[3,1920,128]{2,1,0:T(8,128)(2,1)} %get-tuple-element.123.query, ...), custom_call_target="tpu_custom_call" | custom-call | flops 2831155200 | bytes 12000000 | tf_op jit(solution)/shard_map/attend/pallas_call | solution.py:1087
  133.9 2.1 maximum_maximum_fusion.2
  136.0 3.5 all-to-all-start
  144.7 3.8 arrange.12
  148.4 7.0 %all-to-all-done = bf16[4,720,128]{2,1,0:T(8,128)(2,1)S(1)} async-done(((bf16[4,720,128]{2,1,0:T(8,128)(2,1)}), bf16[4,720,128]{2,1,0:T(8,128)(2,1)S(1)}, u32[]{:S(2)}, u32[]{:S(2)}) %all-to-all-start) | async-done | bytes 737312 | tf_op jit(solution)/shard_map/all_to_all | solution.py:1130
  155.8 13.1 %copy.101 = bf16[480,4,192]{0,2,1:T(8,128)(2,1)S(1)} copy(bf16[480,4,192]{2,0,1:T(8,128)(2,1)S(1)} %maximum_bitcast_fusion) | data formatting | bytes 1474560 | tf_op jit(solution)/shard_map/transpose | solution.py:1132
  170.2 2.2 fusion.64
  173.9 4.3 fusion.2
  178.2 2.9 fusion.9
  199.9 2.7 collective-permute-start.36
  202.6 2.8 pad_maximum_fusion.grad_proj
  205.3 11.4 %terms.1 = (bf16[4,96,4224]{2,1,0:T(8,128)(2,1)}, bf16[4,96,4224]{2,1,0:T(8,128)(2,1)}) custom-call(s32[1]{0:T(128)} %bitcast.22.core, bf16[480,2304]{1,0:T(8,128)(2,1)} %pad_maximum_fusion.grad_proj, bf16[480,768]{1,0:T(8,128)(2,1)} %multiply_convert_fusion.2.ffn_in, bf16[480,768]{1,0:T(8,128)(2,1)} %copy-done.16, bf16[480,768]{1,0:T(8,128)(2,1)} %copy.102.attended, ...), custom_call_target="tpu_custom_call" | custom-call | flops 3114270720 | bytes 13000000 | tf_op jit(solution)/shard_map/terms/pallas_call | solution.py:1172
  216.8 6.5 %collective-permute-done.35.refs_2_ = bf16[720,128]{1,0:T(8,128)(2,1)} collective-permute-done((bf16[720,128]{1,0:T(8,128)(2,1)}, bf16[720,128]{1,0:T(8,128)(2,1)}, u32[]{:S(2)}, u32[]{:S(2)}) %collective-permute-start.35) | collective-permute-done | bytes 184352 | tf_op jit(solution)/shard_map/ppermute | solution.py:757
  224.0 2.2 arrange.13
  230.0 3.9 fusion.29
  237.3 34.3 %attend_back.1 = bf16[1920,640]{1,0:T(8,128)(2,1)} custom-call(s32[4]{0:T(128)} %get-tuple-element.219.start_at, s32[4]{0:T(128)} %get-tuple-element.218.step_count, s32[1]{0:T(128)} %sub.83.pad_from, bf16[3,1920,128]{2,1,0:T(8,128)(2,1)} %get-tuple-element.142.query, bf16[1920,128]{1,0:T(8,128)(2,1)} %get-tuple-element.130.pair_out, ...), custom_call_target="tpu_custom_call" | custom-call | flops 7077888000 | bytes 15000000 | tf_op jit(solution)/shard_map/attend_back/pallas_call | solution.py:1219
  275.4 4.2 collective-permute-start.49
  279.5 3.9 fusion.65
  284.5 10.8 %collective-permute-done.49 = bf16[24,4224]{1,0:T(8,128)(2,1)S(1)} collective-permute-done((bf16[24,4224]{1,0:T(8,128)(2,1)S(1)}, bf16[24,4224]{1,0:T(8,128)(2,1)S(1)}, u32[]{:S(2)}, u32[]{:S(2)}) %collective-permute-start.49) | collective-permute-done | bytes 202784 | tf_op jit(solution)/shard_map/ppermute | solution.py:757
  301.7 5.2 %collective-permute-done.52.refs_2_ = bf16[24,4224]{1,0:T(8,128)(2,1)S(1)} collective-permute-done((bf16[24,4224]{1,0:T(8,128)(2,1)S(1)}, bf16[24,4224]{1,0:T(8,128)(2,1)S(1)}, u32[]{:S(2)}, u32[]{:S(2)}) %collective-permute-start.52) | collective-permute-done | bytes 202784 | tf_op jit(solution)/shard_map/ppermute | solution.py:757
  307.1 3.3 collective-permute-start.46
  310.3 4.3 collective-permute-done.46.refs_2_
  314.7 3.7 collective-permute-start.47
  321.0 2.1 arrange.15
  326.3 4.1 convolution_convert_fusion
  339.1 6.7 %collective-permute-done.54.refs_4_ = bf16[2,3,24,768]{3,2,1,0:T(8,128)(2,1)} collective-permute-done((bf16[2,3,24,768]{3,2,1,0:T(8,128)(2,1)}, bf16[2,3,24,768]{3,2,1,0:T(8,128)(2,1)}, u32[]{:S(2)}, u32[]{:S(2)}) %collective-permute-start.54) | collective-permute-done | bytes 221216 | tf_op jit(solution)/shard_map/ppermute | solution.py:757
  349.9 3.5 slice.236
  353.4 6.9 %reshape.303.right_root = bf16[1152,1152]{1,0:T(8,128)(2,1)} reshape(bf16[768,1728]{1,0:T(8,128)(2,1)} %slice.236) | data formatting | bytes 5308416 | tf_op jit(solution)/shard_map/reshape | solution.py:1267
  368.6 3.8 fusion.55
  373.1 4.4 arrange.16
  379.1 8.0 %refresh.4 = (f32[2,72,2304]{2,1,0:T(8,128)}, f32[2,24,768]{2,1,0:T(8,128)}, f32[2,72,768]{2,1,0:T(8,128)}, f32[32,2304]{1,0:T(8,128)}) custom-call(bf16[2304,768]{1,0:T(8,128)(2,1)} %bitcast.178, bf16[72,768]{1,0:T(8,128)(2,1)} %constant_dynamic-slice_fusion.own, bf16[32,768]{1,0:T(8,128)(2,1)} %fusion.42.select, f32[2,72,2304]{2,1,0:T(8,128)} %stat_left.3, ...), custom_call_target="tpu_custom_call" | custom-call | flops 736100352 | bytes 6709248 | tf_op jit(solution)/shard_map/refresh/pallas_call | solution.py:707
  390.1 4.0 add_convert_fusion.5
  405.3 6.5 %arrange.17 = (bf16[3,8,4,24,768]{4,3,2,1,0:T(8,128)(2,1)}, bf16[8,4,24,768]{3,2,1,0:T(8,128)(2,1)}, bf16[8,4,24,1152]{3,2,1,0:T(8,128)(2,1)}) custom-call(s32[1]{0:T(128)} %bitcast.4.own_at, bf16[2,24,4224]{2,1,0:T(8,128)(2,1)} %get-tuple-element.176.refs_0_, bf16[2,24,4224]{2,1,0:T(8,128)(2,1)} %copy-done.6, ...), custom_call_target="tpu_custom_call" | custom-call | bytes 12976128 | tf_op jit(solution)/shard_map/arrange/pallas_call | solution.py:776
  411.8 3.8 refresh.6
  415.6 5.1 %refresh.7 = (f32[1,24,768]{2,1,0:T(8,128)}, f32[1,36,1152]{2,1,0:T(8,128)}, f32[1,24,1152]{2,1,0:T(8,128)}, f32[48,768]{1,0:T(8,128)}) custom-call(bf16[768,1152]{1,0:T(8,128)(2,1)} %bitcast.194, bf16[24,1152]{1,0:T(8,128)(2,1)} %slice.247.own, bf16[48,1152]{1,0:T(8,128)(2,1)} %fusion.40.select, f32[1,24,768]{2,1,0:T(8,128)} %bitcast.216, ...), custom_call_target="tpu_custom_call" | custom-call | flops 254803968 | bytes 4644864 | tf_op jit(solution)/shard_map/refresh/pallas_call | solution.py:707
  422.2 7.9 %refresh.5 = (f32[2,72,2304]{2,1,0:T(8,128)}, f32[2,24,768]{2,1,0:T(8,128)}, f32[2,72,768]{2,1,0:T(8,128)}, f32[32,2304]{1,0:T(8,128)}) custom-call(bf16[2304,768]{1,0:T(8,128)(2,1)} %bitcast.181, bf16[72,768]{1,0:T(8,128)(2,1)} %constant_dynamic-slice_fusion.12.own, ...), custom_call_target="tpu_custom_call", output_to_operand_aliasing={{0}: (8, {}), {1}: (9, {}), {2}: (10, {})} | custom-call | flops 736100352 | bytes 6709248 | tf_op jit(solution)/shard_map/refresh/pallas_call | solution.py:707
  (456 shorter events, 141.3 us)
Async XLA Ops:
  7.2 68.5 %all-gather.5.cloned.1.call-start = ((), (), s32[]{:S(2)}) async-start(), calls=%async_computation.2 | async-start | bytes 3686400 | tf_op jit(solution)/shard_map/all_gather | solution.py:947
  7.9 165.9 %all-gather.9.cloned.1.call-start = ((), (), s32[]{:S(2)}) async-start(), calls=%async_computation.5 | async-start | bytes 3649536 | tf_op jit(solution)/shard_map/all_gather | solution.py:958
  10.4 10.3 %collective-permute-start = (bf16[72,896]{1,0:T(8,128)(2,1)S(1)}, bf16[72,896]{1,0:T(8,128)(2,1)S(1)}, u32[]{:S(2)}, u32[]{:S(2)}) collective-permute-start(bf16[72,896]{1,0:T(8,128)(2,1)S(1)} %fusion.41.refs_0_), channel_id=1, source_target_pairs={{0,1},{1,0},{2,3},{3,2},{4,5},{5,4},{6,7},{7,6},{8,9},{9,8},{10,11... | collective-permute-start | bytes 387080 | tf_op jit(solution)/shard_map/ppermute | solution.py:757
  13.5 18.2 %collective-permute-start.1 = (bf16[72,896]{1,0:T(8,128)(2,1)S(1)}, bf16[72,896]{1,0:T(8,128)(2,1)S(1)}, u32[]{:S(2)}, u32[]{:S(2)}) collective-permute-start(bf16[72,896]{1,0:T(8,128)(2,1)S(1)} %fusion.41.refs_0_), channel_id=1, source_target_pairs={{0,2},{1,3},{2,0},{3,1},{4,6},{5,7},{6,4},{7,5},{8,10},{9,11},{10,... | collective-permute-start | bytes 387080 | tf_op jit(solution)/shard_map/ppermute | solution.py:757
  16.1 15.6 %collective-permute-start.2 = (bf16[72,896]{1,0:T(8,128)(2,1)S(1)}, bf16[72,896]{1,0:T(8,128)(2,1)S(1)}, u32[]{:S(2)}, u32[]{:S(2)}) collective-permute-start(bf16[72,896]{1,0:T(8,128)(2,1)S(1)} %fusion.41.refs_0_), channel_id=1, source_target_pairs={{0,3},{1,2},{2,1},{3,0},{4,7},{5,6},{6,5},{7,4},{8,11},{9,10},{10,... | collective-permute-start | bytes 387080 | tf_op jit(solution)/shard_map/ppermute | solution.py:757
  41.9 10.0 %collective-permute-start.9 = (bf16[2,72,896]{2,1,0:T(8,128)(2,1)S(1)}, bf16[2,72,896]{2,1,0:T(8,128)(2,1)}, u32[]{:S(2)}, u32[]{:S(2)}) collective-permute-start(bf16[2,72,896]{2,1,0:T(8,128)(2,1)S(1)} %get-tuple-element.245.refs_0_), channel_id=1, source_target_pairs={{0,16},{4,20},{8,24},{12,28},{16,0},{20,4},{24,8},{28,12},{1,17},{... | collective-permute-start | bytes 774152 | tf_op jit(solution)/shard_map/ppermute | solution.py:757
  44.3 12.6 %collective-permute-start.13 = (bf16[2,72,896]{2,1,0:T(8,128)(2,1)S(1)}, bf16[2,72,896]{2,1,0:T(8,128)(2,1)}, u32[]{:S(2)}, u32[]{:S(2)}) collective-permute-start(bf16[2,72,896]{2,1,0:T(8,128)(2,1)S(1)} %collective-permute-done.5.refs_4_), channel_id=1, source_target_pairs={{0,16},{4,20},{8,24},{12,28},{16,0},{20,4},{24,8},{28,12},{1,17},{... | collective-permute-start | bytes 774152 | tf_op jit(solution)/shard_map/ppermute | solution.py:757
  46.4 10.5 %collective-permute-start.14 = (bf16[2,72,896]{2,1,0:T(8,128)(2,1)}, bf16[2,72,896]{2,1,0:T(8,128)(2,1)}, u32[]{:S(2)}, u32[]{:S(2)}) collective-permute-start(bf16[2,72,896]{2,1,0:T(8,128)(2,1)} %collective-permute-done.10.refs_9_), channel_id=1, source_target_pairs={{0,8},{4,12},{8,0},{12,4},{16,24},{20,28},{24,16},{28,20},{1,9},{5... | collective-permute-start | bytes 774152 | tf_op jit(solution)/shard_map/ppermute | solution.py:757
  50.2 10.1 %collective-permute-start.12 = (bf16[2,72,896]{2,1,0:T(8,128)(2,1)}, bf16[2,72,896]{2,1,0:T(8,128)(2,1)S(1)}, u32[]{:S(2)}, u32[]{:S(2)}) collective-permute-start(bf16[2,72,896]{2,1,0:T(8,128)(2,1)} %collective-permute-done.10.refs_9_), channel_id=1, source_target_pairs={{0,4},{4,0},{8,12},{12,8},{16,20},{20,16},{24,28},{28,24},{1,5},{5... | collective-permute-start | bytes 774152 | tf_op jit(solution)/shard_map/ppermute | solution.py:757
  75.7 18.8 %collective-permute-start.17 = (bf16[24,1920]{1,0:T(8,128)(2,1)S(1)}, bf16[24,1920]{1,0:T(8,128)(2,1)S(1)}, u32[]{:S(2)}, u32[]{:S(2)}) collective-permute-start(bf16[24,1920]{1,0:T(8,128)(2,1)S(1)} %pad_maximum_fusion.5.refs_0_), channel_id=1, source_target_pairs={{0,1},{1,0},{2,3},{3,2},{4,5},{5,4},{6,7},{7,6},{8,9},{9,8},{10,11... | collective-permute-start | bytes 276488 | tf_op jit(solution)/shard_map/ppermute | solution.py:757
  81.6 12.9 %collective-permute-start.18 = (bf16[24,1920]{1,0:T(8,128)(2,1)S(1)}, bf16[24,1920]{1,0:T(8,128)(2,1)S(1)}, u32[]{:S(2)}, u32[]{:S(2)}) collective-permute-start(bf16[24,1920]{1,0:T(8,128)(2,1)S(1)} %pad_maximum_fusion.5.refs_0_), channel_id=1, source_target_pairs={{0,2},{1,3},{2,0},{3,1},{4,6},{5,7},{6,4},{7,5},{8,10},{9,11},{10,... | collective-permute-start | bytes 276488 | tf_op jit(solution)/shard_map/ppermute | solution.py:757
  83.5 11.0 %collective-permute-start.19 = (bf16[24,1920]{1,0:T(8,128)(2,1)S(1)}, bf16[24,1920]{1,0:T(8,128)(2,1)S(1)}, u32[]{:S(2)}, u32[]{:S(2)}) collective-permute-start(bf16[24,1920]{1,0:T(8,128)(2,1)S(1)} %pad_maximum_fusion.5.refs_0_), channel_id=1, source_target_pairs={{0,3},{1,2},{2,1},{3,0},{4,7},{5,6},{6,5},{7,4},{8,11},{9,10},{10,... | collective-permute-start | bytes 276488 | tf_op jit(solution)/shard_map/ppermute | solution.py:757
  101.3 31.1 %collective-permute-start.21 = (bf16[2,24,1920]{2,1,0:T(8,128)(2,1)S(1)}, bf16[2,24,1920]{2,1,0:T(8,128)(2,1)S(1)}, u32[]{:S(2)}, u32[]{:S(2)}) collective-permute-start(bf16[2,24,1920]{2,1,0:T(8,128)(2,1)S(1)} %get-tuple-element.133.refs_1_), channel_id=1, source_target_pairs={{0,8},{4,12},{8,0},{12,4},{16,24},{20,28},{24,16},{28,20},{1,9},{5... | collective-permute-start | bytes 552968 | tf_op jit(solution)/shard_map/ppermute | solution.py:757
  102.8 29.6 %collective-permute-start.22 = (bf16[2,24,1920]{2,1,0:T(8,128)(2,1)S(1)}, bf16[2,24,1920]{2,1,0:T(8,128)(2,1)S(1)}, u32[]{:S(2)}, u32[]{:S(2)}) collective-permute-start(bf16[2,24,1920]{2,1,0:T(8,128)(2,1)S(1)} %get-tuple-element.132.refs_0_), channel_id=1, source_target_pairs={{0,16},{4,20},{8,24},{12,28},{16,0},{20,4},{24,8},{28,12},{1,17},{... | collective-permute-start | bytes 552968 | tf_op jit(solution)/shard_map/ppermute | solution.py:757
  106.3 26.2 %collective-permute-start.24 = (bf16[2,24,1920]{2,1,0:T(8,128)(2,1)S(1)}, bf16[2,24,1920]{2,1,0:T(8,128)(2,1)S(1)}, u32[]{:S(2)}, u32[]{:S(2)}) collective-permute-start(bf16[2,24,1920]{2,1,0:T(8,128)(2,1)S(1)} %collective-permute-done.20.refs_4_), channel_id=1, source_target_pairs={{0,16},{4,20},{8,24},{12,28},{16,0},{20,4},{24,8},{28,12},{1,17},{... | collective-permute-start | bytes 552968 | tf_op jit(solution)/shard_map/ppermute | solution.py:757
  107.8 24.7 %collective-permute-start.25 = (bf16[2,24,1920]{2,1,0:T(8,128)(2,1)S(1)}, bf16[2,24,1920]{2,1,0:T(8,128)(2,1)S(1)}, u32[]{:S(2)}, u32[]{:S(2)}) collective-permute-start(bf16[2,24,1920]{2,1,0:T(8,128)(2,1)S(1)} %collective-permute-done.23.refs_9_), channel_id=1, source_target_pairs={{0,8},{4,12},{8,0},{12,4},{16,24},{20,28},{24,16},{28,20},{1,9},{5... | collective-permute-start | bytes 552968 | tf_op jit(solution)/shard_map/ppermute | solution.py:757
  136.0 19.5 %all-to-all-start = ((bf16[4,720,128]{2,1,0:T(8,128)(2,1)}), bf16[4,720,128]{2,1,0:T(8,128)(2,1)S(1)}, u32[]{:S(2)}, u32[]{:S(2)}) async-start(bf16[4,720,128]{2,1,0:T(8,128)(2,1)} %maximum_maximum_fusion.2), calls=%async_computation | async-start | bytes 1474560 | tf_op jit(solution)/shard_map/all_to_all | solution.py:1130
  139.5 210.4 %all-gather.7.cloned.1.call-start = ((), (), s32[]{:S(2)}) async-start(), calls=%async_computation.4 | async-start | bytes 6488064 | tf_op jit(solution)/shard_map/all_gather | solution.py:973
  142.9 290.8 %reduce-scatter.2.cloned.1.call-start = ((), (), s32[]{:S(2)}) async-start(), calls=%async_computation.3 | async-start | bytes 3686400 | tf_op jit(solution)/shard_map/reduce_scatter | solution.py:1300
  195.6 21.1 %collective-permute-start.34 = (bf16[720,128]{1,0:T(8,128)(2,1)}, bf16[720,128]{1,0:T(8,128)(2,1)}, u32[]{:S(2)}, u32[]{:S(2)}) collective-permute-start(bf16[720,128]{1,0:T(8,128)(2,1)} %bitcast.209), channel_id=1, source_target_pairs={{0,1},{1,0},{2,3},{3,2},{4,5},{5,4},{6,7},{7,6},{8,9},{9,8},{10,11... | collective-permute-start | bytes 552968 | tf_op jit(solution)/shard_map/ppermute | solution.py:757
  197.4 25.9 %collective-permute-start.35 = (bf16[720,128]{1,0:T(8,128)(2,1)}, bf16[720,128]{1,0:T(8,128)(2,1)}, u32[]{:S(2)}, u32[]{:S(2)}) collective-permute-start(bf16[720,128]{1,0:T(8,128)(2,1)} %bitcast.210), channel_id=1, source_target_pairs={{0,2},{1,3},{2,0},{3,1},{4,6},{5,7},{6,4},{7,5},{8,10},{9,11},{10,... | collective-permute-start | bytes 552968 | tf_op jit(solution)/shard_map/ppermute | solution.py:757
  199.9 23.4 %collective-permute-start.36 = (bf16[720,128]{1,0:T(8,128)(2,1)}, bf16[720,128]{1,0:T(8,128)(2,1)S(1)}, u32[]{:S(2)}, u32[]{:S(2)}) collective-permute-start(bf16[720,128]{1,0:T(8,128)(2,1)} %bitcast.211), channel_id=1, source_target_pairs={{0,3},{1,2},{2,1},{3,0},{4,7},{5,6},{6,5},{7,4},{8,11},{9,10},{10,... | collective-permute-start | bytes 552968 | tf_op jit(solution)/shard_map/ppermute | solution.py:757
  233.8 37.8 %collective-permute-start.38 = (bf16[96,4224]{1,0:T(8,128)(2,1)}, bf16[96,4224]{1,0:T(8,128)(2,1)}, u32[]{:S(2)}, u32[]{:S(2)}) collective-permute-start(bf16[96,4224]{1,0:T(8,128)(2,1)} %get-tuple-element.155), channel_id=1, source_target_pairs={{0,8},{4,12},{8,0},{12,4},{16,24},{20,28},{24,16},{28,20},{1,9},{5... | collective-permute-start | bytes 2433032 | tf_op jit(solution)/shard_map/ppermute | solution.py:757
  234.9 37.5 %collective-permute-start.39 = (bf16[96,4224]{1,0:T(8,128)(2,1)}, bf16[96,4224]{1,0:T(8,128)(2,1)}, u32[]{:S(2)}, u32[]{:S(2)}) collective-permute-start(bf16[96,4224]{1,0:T(8,128)(2,1)} %get-tuple-element.156), channel_id=1, source_target_pairs={{0,16},{4,20},{8,24},{12,28},{16,0},{20,4},{24,8},{28,12},{1,17},{... | collective-permute-start | bytes 2433032 | tf_op jit(solution)/shard_map/ppermute | solution.py:757
  236.4 36.0 %collective-permute-start.40 = (bf16[96,4224]{1,0:T(8,128)(2,1)}, bf16[96,4224]{1,0:T(8,128)(2,1)}, u32[]{:S(2)}, u32[]{:S(2)}) collective-permute-start(bf16[96,4224]{1,0:T(8,128)(2,1)} %get-tuple-element.157), channel_id=1, source_target_pairs={{0,24},{4,28},{8,16},{12,20},{16,8},{20,12},{24,0},{28,4},{1,25},{... | collective-permute-start | bytes 2433032 | tf_op jit(solution)/shard_map/ppermute | solution.py:757
  275.4 19.9 %collective-permute-start.49 = (bf16[24,4224]{1,0:T(8,128)(2,1)S(1)}, bf16[24,4224]{1,0:T(8,128)(2,1)S(1)}, u32[]{:S(2)}, u32[]{:S(2)}) collective-permute-start(bf16[24,4224]{1,0:T(8,128)(2,1)S(1)} %get-tuple-element.237), channel_id=1, source_target_pairs={{0,2},{1,3},{2,0},{3,1},{4,6},{5,7},{6,4},{7,5},{8,10},{9,11},{10,... | collective-permute-start | bytes 608264 | tf_op jit(solution)/shard_map/ppermute | solution.py:757
  279.5 15.8 %collective-permute-start.48 = (bf16[24,4224]{1,0:T(8,128)(2,1)S(1)}, bf16[24,4224]{1,0:T(8,128)(2,1)S(1)}, u32[]{:S(2)}, u32[]{:S(2)}) collective-permute-start(bf16[24,4224]{1,0:T(8,128)(2,1)S(1)} %get-tuple-element.235), channel_id=1, source_target_pairs={{0,1},{1,0},{2,3},{3,2},{4,5},{5,4},{6,7},{7,6},{8,9},{9,8},{10,11... | collective-permute-start | bytes 608264 | tf_op jit(solution)/shard_map/ppermute | solution.py:757
  283.6 12.6 %collective-permute-start.41 = (bf16[3,4,24,768]{3,2,0,1:T(8,128)(2,1)S(1)}, bf16[3,4,24,768]{3,2,0,1:T(8,128)(2,1)S(1)}, u32[]{:S(2)}, u32[]{:S(2)}) collective-permute-start(bf16[3,4,24,768]{3,2,0,1:T(8,128)(2,1)S(1)} %copy_bitcast_fusion), channel_id=1, source_target_pairs={{0,4},{4,0},{8,12},{12,8},{16,20},{20,16},{24,28},{28,24},{1,5},{5... | collective-permute-start | bytes 1327112 | tf_op jit(solution)/shard_map/ppermute | solution.py:757
  296.2 10.8 %collective-permute-start.52 = (bf16[24,4224]{1,0:T(8,128)(2,1)S(1)}, bf16[24,4224]{1,0:T(8,128)(2,1)S(1)}, u32[]{:S(2)}, u32[]{:S(2)}) collective-permute-start(bf16[24,4224]{1,0:T(8,128)(2,1)S(1)} %get-tuple-element.214.refs_0_), channel_id=1, source_target_pairs={{0,2},{1,3},{2,0},{3,1},{4,6},{5,7},{6,4},{7,5},{8,10},{9,11},{10,... | collective-permute-start | bytes 608264 | tf_op jit(solution)/shard_map/ppermute | solution.py:757
  296.3 10.6 %collective-permute-start.44 = (bf16[3,24,768]{2,1,0:T(8,128)(2,1)S(1)}, bf16[3,24,768]{2,1,0:T(8,128)(2,1)S(1)}, u32[]{:S(2)}, u32[]{:S(2)}) collective-permute-start(bf16[3,24,768]{2,1,0:T(8,128)(2,1)S(1)} %get-tuple-element.231), channel_id=1, source_target_pairs={{0,24},{4,28},{8,16},{12,20},{16,8},{20,12},{24,0},{28,4},{1,25},{... | collective-permute-start | bytes 331784 | tf_op jit(solution)/shard_map/ppermute | solution.py:757
  300.0 19.6 %collective-permute-start.51 = (bf16[24,4224]{1,0:T(8,128)(2,1)S(1)}, bf16[24,4224]{1,0:T(8,128)(2,1)S(1)}, u32[]{:S(2)}, u32[]{:S(2)}) collective-permute-start(bf16[24,4224]{1,0:T(8,128)(2,1)S(1)} %get-tuple-element.214.refs_0_), channel_id=1, source_target_pairs={{0,1},{1,0},{2,3},{3,2},{4,5},{5,4},{6,7},{7,6},{8,9},{9,8},{10,11... | collective-permute-start | bytes 608264 | tf_op jit(solution)/shard_map/ppermute | solution.py:757
  306.9 12.7 %collective-permute-start.53 = (bf16[24,4224]{1,0:T(8,128)(2,1)S(1)}, bf16[24,4224]{1,0:T(8,128)(2,1)S(1)}, u32[]{:S(2)}, u32[]{:S(2)}) collective-permute-start(bf16[24,4224]{1,0:T(8,128)(2,1)S(1)} %collective-permute-done.52.refs_2_), channel_id=1, source_target_pairs={{0,1},{1,0},{2,3},{3,2},{4,5},{5,4},{6,7},{7,6},{8,9},{9,8},{10,11... | collective-permute-start | bytes 608264 | tf_op jit(solution)/shard_map/ppermute | solution.py:757
  310.3 12.8 %collective-permute-start.45 = (bf16[3,24,768]{2,1,0:T(8,128)(2,1)S(1)}, bf16[3,24,768]{2,1,0:T(8,128)(2,1)S(1)}, u32[]{:S(2)}, u32[]{:S(2)}) collective-permute-start(bf16[3,24,768]{2,1,0:T(8,128)(2,1)S(1)} %add_convert_fusion.6.refs_0_), channel_id=1, source_target_pairs={{0,1},{1,0},{2,3},{3,2},{4,5},{5,4},{6,7},{7,6},{8,9},{9,8},{10,11... | collective-permute-start | bytes 331784 | tf_op jit(solution)/shard_map/ppermute | solution.py:757
  332.6 14.8 %collective-permute-start.55 = (bf16[2,3,24,768]{3,2,1,0:T(8,128)(2,1)S(1)}, bf16[2,3,24,768]{3,2,1,0:T(8,128)(2,1)S(1)}, u32[]{:S(2)}, u32[]{:S(2)}) collective-permute-start(bf16[2,3,24,768]{3,2,1,0:T(8,128)(2,1)S(1)} %get-tuple-element.166.refs_1_), channel_id=1, source_target_pairs={{0,8},{4,12},{8,0},{12,4},{16,24},{20,28},{24,16},{28,20},{1,9},{5... | collective-permute-start | bytes 663560 | tf_op jit(solution)/shard_map/ppermute | solution.py:757
  334.2 13.6 %collective-permute-start.57 = (bf16[2,3,24,768]{3,2,1,0:T(8,128)(2,1)S(1)}, bf16[2,3,24,768]{3,2,1,0:T(8,128)(2,1)}, u32[]{:S(2)}, u32[]{:S(2)}) collective-permute-start(bf16[2,3,24,768]{3,2,1,0:T(8,128)(2,1)S(1)} %get-tuple-element.166.refs_1_), channel_id=1, source_target_pairs={{0,16},{4,20},{8,24},{12,28},{16,0},{20,4},{24,8},{28,12},{1,17},{... | collective-permute-start | bytes 663560 | tf_op jit(solution)/shard_map/ppermute | solution.py:757
  334.3 11.5 %collective-permute-start.54 = (bf16[2,3,24,768]{3,2,1,0:T(8,128)(2,1)}, bf16[2,3,24,768]{3,2,1,0:T(8,128)(2,1)}, u32[]{:S(2)}, u32[]{:S(2)}) collective-permute-start(bf16[2,3,24,768]{3,2,1,0:T(8,128)(2,1)} %get-tuple-element.165.refs_0_), channel_id=1, source_target_pairs={{0,8},{4,12},{8,0},{12,4},{16,24},{20,28},{24,16},{28,20},{1,9},{5... | collective-permute-start | bytes 663560 | tf_op jit(solution)/shard_map/ppermute | solution.py:757
  337.1 24.2 %collective-permute-start.68 = (bf16[2,24,4224]{2,1,0:T(8,128)(2,1)}, bf16[2,24,4224]{2,1,0:T(8,128)(2,1)}, u32[]{:S(2)}, u32[]{:S(2)}) collective-permute-start(bf16[2,24,4224]{2,1,0:T(8,128)(2,1)} %get-tuple-element.176.refs_0_), channel_id=1, source_target_pairs={{0,8},{4,12},{8,0},{12,4},{16,24},{20,28},{24,16},{28,20},{1,9},{5... | collective-permute-start | bytes 1216520 | tf_op jit(solution)/shard_map/ppermute | solution.py:757
  337.1 24.6 %collective-permute-start.71 = (bf16[2,24,4224]{2,1,0:T(8,128)(2,1)S(1)}, bf16[2,24,4224]{2,1,0:T(8,128)(2,1)S(1)}, u32[]{:S(2)}, u32[]{:S(2)}) collective-permute-start(bf16[2,24,4224]{2,1,0:T(8,128)(2,1)S(1)} %get-tuple-element.177.refs_1_), channel_id=1, source_target_pairs={{0,16},{4,20},{8,24},{12,28},{16,0},{20,4},{24,8},{28,12},{1,17},{... | collective-permute-start | bytes 1216520 | tf_op jit(solution)/shard_map/ppermute | solution.py:757
  345.8 14.5 %collective-permute-start.56 = (bf16[2,3,24,768]{3,2,1,0:T(8,128)(2,1)}, bf16[2,3,24,768]{3,2,1,0:T(8,128)(2,1)}, u32[]{:S(2)}, u32[]{:S(2)}) collective-permute-start(bf16[2,3,24,768]{3,2,1,0:T(8,128)(2,1)} %get-tuple-element.165.refs_0_), channel_id=1, source_target_pairs={{0,16},{4,20},{8,24},{12,28},{16,0},{20,4},{24,8},{28,12},{1,17},{... | collective-permute-start | bytes 663560 | tf_op jit(solution)/shard_map/ppermute | solution.py:757
  347.4 12.9 %collective-permute-start.58 = (bf16[2,3,24,768]{3,2,1,0:T(8,128)(2,1)}, bf16[2,3,24,768]{3,2,1,0:T(8,128)(2,1)}, u32[]{:S(2)}, u32[]{:S(2)}) collective-permute-start(bf16[2,3,24,768]{3,2,1,0:T(8,128)(2,1)} %collective-permute-done.54.refs_4_), channel_id=1, source_target_pairs={{0,16},{4,20},{8,24},{12,28},{16,0},{20,4},{24,8},{28,12},{1,17},{... | collective-permute-start | bytes 663560 | tf_op jit(solution)/shard_map/ppermute | solution.py:757
  348.1 12.2 %collective-permute-start.59 = (bf16[2,3,24,768]{3,2,1,0:T(8,128)(2,1)}, bf16[2,3,24,768]{3,2,1,0:T(8,128)(2,1)}, u32[]{:S(2)}, u32[]{:S(2)}) collective-permute-start(bf16[2,3,24,768]{3,2,1,0:T(8,128)(2,1)} %collective-permute-done.57.refs_9_), channel_id=1, source_target_pairs={{0,8},{4,12},{8,0},{12,4},{16,24},{20,28},{24,16},{28,20},{1,9},{5... | collective-permute-start | bytes 663560 | tf_op jit(solution)/shard_map/ppermute | solution.py:757
  364.5 22.6 %collective-permute-start.69 = (bf16[2,24,4224]{2,1,0:T(8,128)(2,1)S(1)}, bf16[2,24,4224]{2,1,0:T(8,128)(2,1)S(1)}, u32[]{:S(2)}, u32[]{:S(2)}) collective-permute-start(bf16[2,24,4224]{2,1,0:T(8,128)(2,1)S(1)} %get-tuple-element.177.refs_1_), channel_id=1, source_target_pairs={{0,8},{4,12},{8,0},{12,4},{16,24},{20,28},{24,16},{28,20},{1,9},{5... | collective-permute-start | bytes 1216520 | tf_op jit(solution)/shard_map/ppermute | solution.py:757
  365.2 21.9 %collective-permute-start.70 = (bf16[2,24,4224]{2,1,0:T(8,128)(2,1)}, bf16[2,24,4224]{2,1,0:T(8,128)(2,1)S(1)}, u32[]{:S(2)}, u32[]{:S(2)}) collective-permute-start(bf16[2,24,4224]{2,1,0:T(8,128)(2,1)} %get-tuple-element.176.refs_0_), channel_id=1, source_target_pairs={{0,16},{4,20},{8,24},{12,28},{16,0},{20,4},{24,8},{28,12},{1,17},{... | collective-permute-start | bytes 1216520 | tf_op jit(solution)/shard_map/ppermute | solution.py:757
  366.5 20.6 %collective-permute-start.72 = (bf16[2,24,4224]{2,1,0:T(8,128)(2,1)}, bf16[2,24,4224]{2,1,0:T(8,128)(2,1)S(1)}, u32[]{:S(2)}, u32[]{:S(2)}) collective-permute-start(bf16[2,24,4224]{2,1,0:T(8,128)(2,1)} %collective-permute-done.68.refs_4_), channel_id=1, source_target_pairs={{0,16},{4,20},{8,24},{12,28},{16,0},{20,4},{24,8},{28,12},{1,17},{... | collective-permute-start | bytes 1216520 | tf_op jit(solution)/shard_map/ppermute | solution.py:757
  367.2 19.9 %collective-permute-start.73 = (bf16[2,24,4224]{2,1,0:T(8,128)(2,1)}, bf16[2,24,4224]{2,1,0:T(8,128)(2,1)S(1)}, u32[]{:S(2)}, u32[]{:S(2)}) collective-permute-start(bf16[2,24,4224]{2,1,0:T(8,128)(2,1)} %copy-done.22), channel_id=1, source_target_pairs={{0,8},{4,12},{8,0},{12,4},{16,24},{20,28},{24,16},{28,20},{1,9},{5... | collective-permute-start | bytes 1216520 | tf_op jit(solution)/shard_map/ppermute | solution.py:757
  387.2 13.4 %collective-permute-start.74 = (bf16[2,24,4224]{2,1,0:T(8,128)(2,1)}, bf16[2,24,4224]{2,1,0:T(8,128)(2,1)}, u32[]{:S(2)}, u32[]{:S(2)}) collective-permute-start(bf16[2,24,4224]{2,1,0:T(8,128)(2,1)} %get-tuple-element.176.refs_0_), channel_id=1, source_target_pairs={{0,4},{4,0},{8,12},{12,8},{16,20},{20,16},{24,28},{28,24},{1,5},{5... | collective-permute-start | bytes 1216520 | tf_op jit(solution)/shard_map/ppermute | solution.py:757
  387.7 13.3 %collective-permute-start.75 = (bf16[2,24,4224]{2,1,0:T(8,128)(2,1)S(1)}, bf16[2,24,4224]{2,1,0:T(8,128)(2,1)}, u32[]{:S(2)}, u32[]{:S(2)}) collective-permute-start(bf16[2,24,4224]{2,1,0:T(8,128)(2,1)S(1)} %get-tuple-element.177.refs_1_), channel_id=1, source_target_pairs={{0,4},{4,0},{8,12},{12,8},{16,20},{20,16},{24,28},{28,24},{1,5},{5... | collective-permute-start | bytes 1216520 | tf_op jit(solution)/shard_map/ppermute | solution.py:757
  387.9 13.2 %collective-permute-start.76 = (bf16[2,24,4224]{2,1,0:T(8,128)(2,1)}, bf16[2,24,4224]{2,1,0:T(8,128)(2,1)}, u32[]{:S(2)}, u32[]{:S(2)}) collective-permute-start(bf16[2,24,4224]{2,1,0:T(8,128)(2,1)} %collective-permute-done.68.refs_4_), channel_id=1, source_target_pairs={{0,4},{4,0},{8,12},{12,8},{16,20},{20,16},{24,28},{28,24},{1,5},{5... | collective-permute-start | bytes 1216520 | tf_op jit(solution)/shard_map/ppermute | solution.py:757
  (130 other events, 986.1 us)
Sparse Core Ops, SparseCore 0:
  9.6 66.0 all-gather.4
  79.1 64.6 all-gather.8
  146.7 82.8 all-gather.6
  330.6 55.2 reduce-scatter.1

commit v4 on v3

--- a/solution.py
+++ b/solution.py
@@ -411,7 +411,8 @@
 KEY_ALIGN = 128
 PREP_TILE = 480
 LANES = 128
-REFRESH_ROWS = 384
+REFRESH_ROWS = 768
+ROOT_SPLIT = 640
 MASK_BIT = -(2.0**100)
 NO_MAX = -3e38
 BF16 = jnp.bfloat16
@@ -662,13 +663,14 @@
 
 
 def refresh_kernel(
-    full, own, select, stat_left, stat_right, root_left, right_root, weight, *refs, kept
+    full, own, select, stat_left, stat_right, root_left, right_root, weight, *refs, kept, own_at, root_at
 ):
     new_left, new_right, new_weight, columns, total = refs[kept:]
     step = pl.program_id(0)
     chosen = select.shape[0]
     count = new_right.shape[-2]
-    outer = dot_rows(jnp.concatenate([select[...], own[...]]), full[...])
+    own_rows = own[:, own_at : own_at + full.shape[1]]
+    outer = dot_rows(jnp.concatenate([select[...], own_rows]), full[...])
     columns[...] = outer[:chosen]
     new_left[0] = 0.5 * stat_left[0] + 0.5 * outer[chosen:]
     left = jnp.concatenate([outer[:chosen].astype(BF16), root_left[0].astype(BF16)])
@@ -685,11 +687,24 @@
     @pl.when(step == pl.num_programs(0) - 1)
     def finish():
         new_right[0] = 0.5 * stat_right[0] + 0.5 * total[:count, :]
-        update = dot_plain(total[chosen:, :].astype(BF16), right_root[...])
-        new_weight[0] = weight[0] - SHAMPOO_RATE * update
-
-
-def refresh(at, full, own, select, stat_left, stat_right, root_left, right_root, weight, previous):
+        product = total[chosen:, :].astype(BF16)
+        if root_at is None:
+            new_weight[0] = weight[0] - SHAMPOO_RATE * dot_plain(product, right_root[...])
+        else:
+            size = product.shape[1]
+            rest = root_at + size
+            new_weight[0] = dot_rows(product, right_root[:, root_at:rest])
+            new_weight[1] = dot_rows(
+                product[:, :ROOT_SPLIT], right_root[:, rest : rest + ROOT_SPLIT]
+            )
+            new_weight[2] = dot_rows(
+                product[:, ROOT_SPLIT:], right_root[:, rest : rest + size - ROOT_SPLIT]
+            )
+
+
+def refresh(
+    at, full, own, own_at, select, stat_left, stat_right, root_left, roots, root_at, weight, previous
+):
     in_dim, out_dim = full.shape
     chunk = REFRESH_ROWS
     rows, count, chosen = own.shape[0], stat_right.shape[1], select.shape[0]
@@ -704,8 +719,21 @@
         return pl.BlockSpec((1,) + array.shape[1:], lambda i: (at, 0, 0))
 
     kept = [pl.BlockSpec(memory_space=pl.ANY)] * len(previous)
+    square = root_at >= 0
+    if square:
+        new_weight = stacked(weight), weight.shape
+        root_block = pl.BlockSpec((out_dim, out_dim), lambda i: (0, root_at))
+    else:
+        parts = (3, rows, roots.shape[0])
+        new_weight = whole(*parts), parts
+        root_block = whole(*roots.shape)
     return pl.pallas_call(
-        functools.partial(refresh_kernel, kept=len(previous)),
+        functools.partial(
+            refresh_kernel,
+            kept=len(previous),
+            own_at=own_at,
+            root_at=None if square else -root_at,
+        ),
         grid=(in_dim // chunk,),
         in_specs=[
             pl.BlockSpec((chunk, out_dim), lambda i: (i, 0)),
@@ -714,20 +742,20 @@
             by_chunk(rows),
             stacked(stat_right),
             by_chunk(rows),
-            whole(*right_root.shape),
+            root_block,
             stacked(weight),
         ]
         + kept,
         out_specs=[
             by_chunk(rows),
             stacked(stat_right),
-            stacked(weight),
+            new_weight[0],
             pl.BlockSpec((chosen, chunk), lambda i: (0, i)),
         ],
         out_shape=[
             jax.ShapeDtypeStruct(stat_left.shape, F32),
             jax.ShapeDtypeStruct(stat_right.shape, F32),
-            jax.ShapeDtypeStruct(weight.shape, F32),
+            jax.ShapeDtypeStruct(new_weight[1], F32),
             jax.ShapeDtypeStruct((chosen, in_dim), F32),
         ],
         scratch_shapes=[pltpu.VMEM((chosen + rows, out_dim), F32)],
@@ -746,7 +774,7 @@
         stat_left,
         stat_right,
         root_left,
-        right_root,
+        roots,
         weight,
         *previous,
     )
@@ -815,21 +843,28 @@
 
 
 def gather_plane(values, by_steps=False):
+    last = None if by_steps else exchange(values, "seq", 3)
     far = exchange(values, "seq", 2)
-    last = exchange(far, "seq", 1) if by_steps else exchange(values, "seq", 3)
+    last = exchange(far, "seq", 1) if by_steps else last
     blocks = [values, exchange(values, "seq", 1), far, last]
     shape = (len(blocks),) + values.shape
     moves = [(k, k, (), 0, ("place",)) for k in range(len(blocks))]
     return arrange(blocks, lax.axis_index("seq"), [shape], moves)[0]
 
 
-def gather_partners(plane):
+def gather_near(plane):
     half = plane.shape[0] // 2
     left, right = plane[:half], plane[half:]
     left_two, right_four = exchange(left, "dp", 2), exchange(right, "dp", 4)
-    left_four, right_two = exchange(left, "dp", 4), exchange(right, "dp", 2)
-    left_six, right_six = exchange(left_two, "dp", 4), exchange(right_four, "dp", 2)
-    return [left, right, left_two, right_two, left_four, right_four, left_six, right_six]
+    return [left, right, left_two, exchange(right, "dp", 2), exchange(left, "dp", 4), right_four]
+
+
+def gather_far(near):
+    return [*near, exchange(near[2], "dp", 4), exchange(near[5], "dp", 2)]
+
+
+def gather_partners(plane):
+    return gather_far(gather_near(plane))
 
 
 def gather_cores(even):
@@ -886,10 +921,13 @@
     ]
 
 
+def swap_blocks(blocks, axis, unit):
+    came = [exchange(blocks[k], axis, k * unit) for k in range(len(blocks) - 1, 0, -1)]
+    return [blocks[0]] + came[::-1]
+
+
 def add_partners(blocks, axis, unit):
-    return add_blocks(
-        blocks[:1] + [exchange(block, axis, k * unit) for k, block in enumerate(blocks) if k]
-    )
+    return add_blocks(swap_blocks(blocks, axis, unit))
 
 
 def lows(blocks):
@@ -960,17 +998,24 @@
     row_tokens, out_weights = fence(row_tokens, out_weights)
     out_plane = gather_plane(out_weights)
     root_rows = stat_r_in.shape[1]
-    fo_columns = root_r_fo.shape[0] * hidden // root_rows
+    fo_rest = root_r_fo.shape[0] - root_rows
+    rest_rows = root_r_fo[root_rows:].astype(BF16)
+    wrapped = jnp.concatenate(
+        [
+            rest_rows[:, :ROOT_SPLIT],
+            jnp.pad(rest_rows[:, ROOT_SPLIT:], ((0, 0), (0, 2 * ROOT_SPLIT - hidden))),
+        ]
+    )
     roots = jnp.concatenate(
         [
             root_r_in[0].astype(BF16),
             root_r_in[1].astype(BF16),
             root_r_ao.astype(BF16),
-            root_r_fo.astype(BF16).reshape(root_rows, fo_columns),
+            root_r_fo[:root_rows].astype(BF16),
+            wrapped,
         ],
         axis=1,
     )
-    roots = lax.all_gather(roots, ("dp", "seq"), axis=0, tiled=True)
 
     lengths = doc_lengths[0]
     segment, within, is_valid = doc_tables(lengths, pad_counts[0], row_length)
@@ -1158,10 +1203,7 @@
     packed_back = jnp.concatenate(
         [grad_blocks[:, :, :LANES], jnp.concatenate([folded[:, 0], folded[:, 1]], axis=-1)], axis=1
     )
-    back_blocks = by_distance(packed_back, "seq")
-    back_blocks = [back_blocks[0]] + [
-        exchange(block, "seq", k) for k, block in enumerate(back_blocks) if k
-    ]
+    packed_back = lax.all_to_all(packed_back, "seq", 0, 0, tiled=True)
 
     pack_width = up_parts * width + width + hidden
     pair_count = dp_count // 2
@@ -1184,22 +1226,11 @@
         ),
         name="terms",
     )(core[None], *operands)
-    fenced = fence(send_terms, *back_blocks)
-    send_terms, back_blocks = fenced[0], fenced[1:]
+    send_terms, packed_back, roots = fence(send_terms, packed_back, roots)
+    roots = lax.all_gather(roots, ("dp", "seq"), axis=0, tiled=True)
     pair_blocks = lows(pair_sums(send_terms, keep_terms))
-    folded_tokens = token_count + half_tokens
-    grad_pair, grad_extra = arrange(
-        back_blocks,
-        seq_at,
-        [(seq_count, token_count, LANES), (seq_count, half_tokens, LANES)],
-        [
-            (k, k, (rows,), which, ("place",))
-            for k in range(seq_count)
-            for which, rows in enumerate(
-                (slice(0, token_count), slice(token_count, folded_tokens))
-            )
-        ],
-    )
+    grad_pair = packed_back[:, :token_count]
+    grad_extra = packed_back[:, token_count:]
     grad_pair = grad_pair.reshape(row_length, LANES)
     grad_extra = unfold(grad_extra).reshape(row_length, HEAD_DIM)
     grad_extra = jnp.pad(grad_extra, ((0, 0), (0, LANES - HEAD_DIM)))
@@ -1261,18 +1292,15 @@
         cos_table,
         sin_table,
     )
-    right_qkv = roots[:, :width]
-    right_up = roots[:, width : 2 * width]
-    right_ao = roots[:, 2 * width : 3 * width]
-    right_fo = roots[:, 3 * width :].reshape(hidden, hidden)
     fenced = fence(grad_qkv, *plane_blocks)
     grad_qkv = fenced[0]
     plane_sum = add_blocks(fenced[1:]).astype(BF16).reshape(seq_count, ao_rows, pack_width)
-    summed = add_partners(by_distance(plane_sum, "seq"), "seq", 1)
+    seq_blocks = by_distance(plane_sum, "seq")
+    far_sum = add_blocks([seq_blocks[2], exchange(seq_blocks[3], "seq", 1)]).astype(BF16)
+    near_sum = add_blocks([seq_blocks[0], exchange(seq_blocks[1], "seq", 1)])
+    summed = add_blocks([near_sum, exchange(far_sum, "seq", 2)])
     low_sum = summed.astype(BF16)
     term_plane = gather_plane(low_sum, by_steps=True)
-    low_ao = low_sum[:, up_parts * width : (up_parts + 1) * width]
-    low_fo = low_sum[:, (up_parts + 1) * width :]
     summed_ao = summed[:, up_parts * width : (up_parts + 1) * width]
     summed_fo = summed[:, (up_parts + 1) * width :]
 
@@ -1284,9 +1312,22 @@
     ]
     qkv_sum = add_partners(lows(pair_sums(*qkv_halves, axis=1)), "dp", 2).astype(BF16)
     qkv_plane = gather_plane(qkv_sum, by_steps=True)
-    grad_qkv = fence(grad_qkv, qkv_plane, term_plane)[0]
-    fenced = fence(right_fo, *gather_partners(qkv_plane))
-    right_fo, qkv_blocks = fenced[0], gather_cores(fenced[1:])
+    input_term = jnp.dot(grad_qkv, back_weight, preferred_element_type=F32).astype(BF16)
+    input_term, roots = fence(input_term, roots, qkv_plane, term_plane)[:2]
+    qkv_blocks = gather_cores(gather_partners(qkv_plane))
+    term_partners = gather_partners(term_plane)
+    grad_attn_in = lax.psum_scatter(input_term, "seq", scatter_dimension=0, tiled=True).astype(F32)
+    normed_one, spread_one = norm_forward(inputs)
+    grad_norm_one, _ = norm_backward(grad_attn_in, normed_one, spread_one, gain_rows[0])
+    grad_input = grad_resid + grad_norm_one
+
+    def select(count, size):
+        places = jnp.arange(-(-count // 16) * 16, dtype=jnp.int32)[:, None]
+        wanted = jnp.where(places < count, dev_at * count + places, -1)
+        return (wanted == jnp.arange(size, dtype=jnp.int32)[None, :]).astype(BF16)
+
+    select_in = select(stat_r_in.shape[1], width)
+    select_fo = select(stat_r_fo.shape[0], hidden)
     [whole_qkv] = arrange(
         qkv_blocks,
         lax.axis_index("dp"),
@@ -1295,24 +1336,9 @@
     )
     whole_qkv = whole_qkv.reshape(3 * width, width)
     low_qkv = lax.dynamic_slice_in_dim(whole_qkv, dev_at * in_rows, in_rows, 0)
-
-    input_term = jnp.dot(grad_qkv, back_weight, preferred_element_type=F32).astype(BF16)
-    grad_attn_in = lax.psum_scatter(input_term, "seq", scatter_dimension=0, tiled=True).astype(F32)
-    normed_one, spread_one = norm_forward(inputs)
-    grad_norm_one, _ = norm_backward(grad_attn_in, normed_one, spread_one, gain_rows[0])
-    grad_input = grad_resid + grad_norm_one
-
-    def select(count, size):
-        places = jnp.arange(-(-count // 16) * 16, dtype=jnp.int32)[:, None]
-        wanted = jnp.where(places < count, dev_at * count + places, -1)
-        return (wanted == jnp.arange(size, dtype=jnp.int32)[None, :]).astype(BF16)
-
-    select_in = select(stat_r_in.shape[1], width)
-    select_fo = select(stat_r_fo.shape[0], hidden)
     *stacked, qkv_columns = refresh(
-        0, whole_qkv, low_qkv, select_in, stat_l_in, stat_r_in, root_l_in, right_qkv, w_in, []
-    )
-    term_partners = gather_partners(term_plane)
+        0, whole_qkv, low_qkv, 0, select_in, stat_l_in, stat_r_in, root_l_in, roots, 0, w_in, []
+    )
     fenced = fence(stacked, *term_partners)
     stacked, term_blocks = fenced[0], gather_cores(fenced[1:])
     whole_shape = (dp_count, seq_count, ao_rows)
@@ -1340,29 +1366,38 @@
     left_ao, right_stat_ao, new_ao, _ = refresh(
         0,
         whole_ao,
-        low_ao,
+        low_sum,
+        up_parts * width,
         select_in,
         stat_l_ao[None],
         stat_r_ao[None],
         root_l_ao[None],
-        right_ao,
+        roots,
+        2,
         w_ao[None],
         [],
     )
-    left_fo, right_stat_fo, new_fo, _ = refresh(
+    left_fo, right_stat_fo, fo_parts, _ = refresh(
         0,
         whole_fo,
-        low_fo,
+        low_sum,
+        (up_parts + 1) * width,
         select_fo,
         stat_l_fo[None],
         stat_r_fo[None],
         root_l_fo[None],
-        right_fo,
+        roots,
+        -3 * width,
         w_fo[None],
         [],
     )
+    update_first = fo_parts[0].reshape(ao_rows, all_count, root_rows)
+    update_rest = fo_parts[1].reshape(ao_rows, all_count, root_rows)[:, :, :fo_rest]
+    update_rest += fo_parts[2].reshape(ao_rows, all_count, root_rows)[:, :, fo_rest:]
+    update = jnp.concatenate([update_first, update_rest], axis=2).reshape(ao_rows, hidden)
+    new_fo = w_fo - SHAMPOO_RATE * update
     *stacked, up_columns = refresh(
-        1, whole_up, low_up, select_in, stat_l_in, stat_r_in, root_l_in, right_up, w_in, stacked
+        1, whole_up, low_up, 0, select_in, stat_l_in, stat_r_in, root_l_in, roots, 1, w_in, stacked
     )
     new_left_in, new_right_in, new_in = stacked
 
@@ -1399,7 +1434,7 @@
         right_stat_fo[0],
         new_in,
         new_ao[0],
-        new_fo[0],
+        new_fo,
     )
 
 
@@ -1416,6 +1451,7 @@
         and dp_count == 8
         and seq_count == 4
         and others[3].shape[1] == 3 * others[4].shape[0]
+        and others[5].shape[1] == 1152
         and others[1].shape[1] == 8
     )
     return head_body(tokens, *others) if by_heads else sequence_body(tokens, *others)

time: 446 us -> 426 us (0.955)
  local copies, waits for them, and re-layouts: 78.1 us -> 46.3 us
  waiting for transfers between devices: 73.3 us -> 96.3 us
  Pallas kernels: 133 us -> 118 us
    ppermute x82 -> x79, waiting for transfers between devices: 60.7 us -> 83.9 us  [exchange(): return lax.ppermute(values, axis, [(i, i ^ offset) for i in range(size)])]
    transpose x1, local copies, waits for them, and re-layouts: 13.1 us -> 0.5 us  [head_body(): attn_low = jnp.transpose(attn_low, (1, 0, 2)).reshape(token_count, width)]
    slice x8, local copies, waits for them, and re-layouts: 13.9 us -> 5.42 us  [the longest x4 3.01 us: gather_near(): left, right = (plane[:half], plane[half:])]
    ppermute x82 -> x79, starting transfers between devices: 74.9 us -> 67.1 us  [exchange(): return lax.ppermute(values, axis, [(i, i ^ offset) for i in range(size)])]
    dynamic_slice x5 -> x0, local copies, waits for them, and re-layouts: 6.85 us -> none  [by_distance(): lax.dynamic_index_in_dim(values, own_at ^ k, 0, keepdims=False)]
    reshape x2 -> x1, local copies, waits for them, and re-layouts: 7.06 us -> 0.23 us  [head_body(): jnp.concatenate([update_first, update_rest], axis=2)]
    pallas_call x1, Pallas kernels: 34.3 us -> 28 us  [head_body(): pl.pallas_call(attend_back_kernel, grid_spec=pltpu.PrefetchScalarGridSpec...]
    all_gather x1, waiting for transfers between devices: 4.79 us -> 0.01 us  [head_body(): row_tokens = lax.all_gather(tokens, 'seq', axis=0, tiled=True)]
  transfers between devices with their start and end apart: 87 -> 85, of which waited for: 22 -> 25; matrix products, arithmetic and copies ran while one was open for 29% -> 20% of each run, Pallas kernels for 30% -> 28%
where the time goes in v4:
time: 426 us; the launch traced here: 420 us
  Pallas kernels  118 us (28%)
  waiting for transfers between devices  96.3 us (23%)
  starting transfers between devices  76 us (18%)
  local copies, waits for them, and re-layouts  46.3 us (11%)
  other arithmetic  42.2 us (10%)
  matrix products  25.1 us (6%)
  between operations  16.1 us (4%)
    ppermute x79, waiting for transfers between devices, exchange(): return lax.ppermute(values, axis, [(i, i ^ offset) for i in range(size)])  83.9 us
    ppermute x79, starting transfers between devices, exchange(): return lax.ppermute(values, axis, [(i, i ^ offset) for i in range(size)])  67.1 us
    pallas_call x1, Pallas kernels, head_body(): pl.pallas_call(attend_back_kernel, grid_spec=pltpu.PrefetchScalarGridSpec...  28 us
    pallas_call x8, Pallas kernels, arrange(): pl.pallas_call(functools.partial(arrange_kernel, count=count, moves=moves...  26.7 us
    pallas_call x4, Pallas kernels, refresh(): pl.pallas_call(functools.partial(refresh_kernel, kept=len(previous), own_...  22.7 us
    pallas_call x1, Pallas kernels, head_body(): pl.pallas_call(attend_kernel, grid_spec=pltpu.PrefetchScalarGridSpec(num_...  19.4 us
    unnamed x181, local copies, waits for them, and re-layouts  12.7 us
    all_to_all x1, waiting for transfers between devices, head_body(): packed = lax.all_to_all(packed, 'seq', 0, 0, tiled=True)  11.6 us
  transfers between devices with their start and end apart: 85, of which 25 were waited for; matrix products, arithmetic and copies ran while one was open for 20% of the time, Pallas kernels for 28%

profile of v4, /device:TPU:0, one launch (start us, length us, event | category | flops | bytes accessed | tf_op | source)
XLA Modules:
  0.0 420.0 jit_solution(18247929526656833636)
XLA Ops:
  10.4 5.1 %collective-permute-start.2 = (bf16[72,896]{1,0:T(8,128)(2,1)S(1)}, bf16[72,896]{1,0:T(8,128)(2,1)S(1)}, u32[]{:S(2)}, u32[]{:S(2)}) collective-permute-start(bf16[72,896]{1,0:T(8,128)(2,1)S(1)} %fusion.41.refs_0_), channel_id=1, source_target_pairs={{0,3},{1,2},{2,1},{3,0},{4,7},{5,6},{6,5},{7,4},{8,11},{9,10},{10,... | collective-permute-start | bytes 387080 | tf_op jit(solution)/shard_map/ppermute | solution.py:785
  17.2 3.5 multiply_sine_fusion
  20.8 14.7 %collective-permute-done.1.refs_2_ = bf16[72,896]{1,0:T(8,128)(2,1)S(1)} collective-permute-done((bf16[72,896]{1,0:T(8,128)(2,1)S(1)}, bf16[72,896]{1,0:T(8,128)(2,1)S(1)}, u32[]{:S(2)}, u32[]{:S(2)}) %collective-permute-start.1) | collective-permute-done | bytes 129056 | tf_op jit(solution)/shard_map/ppermute | solution.py:785
  42.8 2.5 select_convert_fusion.key_mask
  45.8 3.1 collective-permute-done.6.refs_5_
  48.9 2.5 collective-permute-start.14
  51.4 3.1 collective-permute-done.5.refs_4_
  58.8 2.3 collective-permute-done.13.refs_12_
  61.1 2.9 pad_maximum_fusion.1
  65.1 4.5 %arrange.9 = (bf16[8,4,72,768]{3,2,1,0:T(8,128)(2,1)}, bf16[8,4,72,128]{3,2,1,0:T(8,128)(2,1)}) custom-call(s32[1]{0:T(128)} %bitcast.4.own_at, bf16[2,72,896]{2,1,0:T(8,128)(2,1)} %copy-done.12, bf16[2,72,896]{2,1,0:T(8,128)(2,1)} %copy-done.11, bf16[2,72,896]{2,1,0:T(8,128)(2,1)} %collective-permute-done.3.refs_2_, bf16[2,72,896]{2,1,0:T(8,128)(2,1)} %copy-done.33, ...), custom_call_target="tpu_custom_call" | custom-call | bytes 8257536 | tf_op jit(solution)/shard_map/arrange/pallas_call | solution.py:804
  75.2 3.4 collective-permute-start.19
  79.5 9.4 %project.1 = (bf16[1920,768]{1,0:T(8,128)(2,1)}, bf16[3,1920,128]{2,1,0:T(8,128)(2,1)}, bf16[3,2400,128]{2,1,0:T(8,128)(2,1)}, bf16[3,2400,128]{2,1,0:T(8,128)(2,1)}) custom-call(bf16[1920,768]{1,0:T(8,128)(2,1)} %all-gather.5.cloned.1.call-done.tokens, bf16[640,768]{1,0:T(8,128)(2,1)} %maximum_maximum_fusion.weight, f32[1,768]{1,0:T(1,128)} %slice.196.gain, ...), custom_call_target="tpu_custom_call" | custom-call | flops 1887436800 | bytes 14000000 | tf_op jit(solution)/shard_map/project/pallas_call | solution.py:1077
  100.5 2.9 collective-permute-start.25
  103.4 19.4 %attend.1 = (bf16[1920,128]{1,0:T(8,128)(2,1)}, bf16[1920,128]{1,0:T(8,128)(2,1)}, bf16[3,1920,128]{2,1,0:T(8,128)(2,1)}) custom-call(s32[4]{0:T(128)} %get-tuple-element.195.start_at, s32[4]{0:T(128)} %get-tuple-element.194.step_count, s32[1]{0:T(128)} %sub.86.pad_from, bf16[3,1920,128]{2,1,0:T(8,128)(2,1)} %get-tuple-element.111.query, ...), custom_call_target="tpu_custom_call" | custom-call | flops 2831155200 | bytes 12000000 | tf_op jit(solution)/shard_map/attend/pallas_call | solution.py:1132
  126.4 5.3 %all-to-all-start = ((bf16[4,720,128]{2,1,0:T(8,128)(2,1)}), bf16[4,720,128]{2,1,0:T(8,128)(2,1)S(1)}, u32[]{:S(2)}, u32[]{:S(2)}) async-start(bf16[4,720,128]{2,1,0:T(8,128)(2,1)} %maximum_maximum_fusion.2), calls=%async_computation | async-start | bytes 1474560 | tf_op jit(solution)/shard_map/all_to_all | solution.py:1175
  138.2 3.8 arrange.11
  142.0 11.6 %all-to-all-done = bf16[4,720,128]{2,1,0:T(8,128)(2,1)S(1)} async-done(((bf16[4,720,128]{2,1,0:T(8,128)(2,1)}), bf16[4,720,128]{2,1,0:T(8,128)(2,1)S(1)}, u32[]{:S(2)}, u32[]{:S(2)}) %all-to-all-start) | async-done | bytes 737312 | tf_op jit(solution)/shard_map/all_to_all | solution.py:1175
  154.9 2.2 fusion.69
  158.6 4.3 %fusion.2 = f32[480,2304]{1,0:T(8,128)S(1)} fusion(bf16[480,768]{1,0:T(8,128)(2,1)} %multiply_convert_fusion.2.ffn_in, bf16[1,2304,768]{2,1,0:T(8,128)(2,1)} %all-gather.9.cloned.1.call-done), kind=kOutput, calls=%fused_computation.2 | convolution fusion | flops 1698693120 | bytes 8699904 | tf_op jit(solution)/shard_map/dot_general | solution.py:84
  162.9 2.8 fusion.9
  177.2 3.5 all-to-all-start.1
  183.5 2.3 copy.97.attended
  185.8 3.1 pad_maximum_fusion.grad_proj
  188.9 11.6 %terms.1 = (bf16[4,96,4224]{2,1,0:T(8,128)(2,1)}, bf16[4,96,4224]{2,1,0:T(8,128)(2,1)}) custom-call(s32[1]{0:T(128)} %bitcast.22.core, bf16[480,2304]{1,0:T(8,128)(2,1)} %pad_maximum_fusion.grad_proj, bf16[480,768]{1,0:T(8,128)(2,1)} %multiply_convert_fusion.2.ffn_in, bf16[480,768]{1,0:T(8,128)(2,1)} %copy-done.18, bf16[480,768]{1,0:T(8,128)(2,1)} %copy.97.attended, ...), custom_call_target="tpu_custom_call" | custom-call | flops 3114270720 | bytes 13000000 | tf_op jit(solution)/shard_map/terms/pallas_call | solution.py:1214
  202.6 4.1 collective-permute-done.34
  206.8 3.8 fusion.29
  210.6 2.4 collective-permute-start.35
  214.4 28.0 %attend_back.1 = bf16[1920,640]{1,0:T(8,128)(2,1)} custom-call(s32[4]{0:T(128)} %get-tuple-element.195.start_at, s32[4]{0:T(128)} %get-tuple-element.194.step_count, s32[1]{0:T(128)} %sub.86.pad_from, bf16[3,1920,128]{2,1,0:T(8,128)(2,1)} %get-tuple-element.130.query, bf16[1920,128]{1,0:T(8,128)(2,1)} %get-tuple-element.118.pair_out, ...), custom_call_target="tpu_custom_call" | custom-call | flops 7077888000 | bytes 15000000 | tf_op jit(solution)/shard_map/attend_back/pallas_call | solution.py:1250
  242.5 14.1 %collective-permute-done.37 = bf16[96,4224]{1,0:T(8,128)(2,1)} collective-permute-done((bf16[96,4224]{1,0:T(8,128)(2,1)}, bf16[96,4224]{1,0:T(8,128)(2,1)}, u32[]{:S(2)}, u32[]{:S(2)}) %collective-permute-start.37) | collective-permute-done | bytes 811040 | tf_op jit(solution)/shard_map/ppermute | solution.py:785
  260.3 4.0 fusion.70
  265.0 5.7 %collective-permute-done.46 = bf16[24,4224]{1,0:T(8,128)(2,1)S(1)} collective-permute-done((bf16[24,4224]{1,0:T(8,128)(2,1)S(1)}, bf16[24,4224]{1,0:T(8,128)(2,1)S(1)}, u32[]{:S(2)}, u32[]{:S(2)}) %collective-permute-start.46) | collective-permute-done | bytes 202784 | tf_op jit(solution)/shard_map/ppermute | solution.py:785
  270.8 2.7 collective-permute-start.47
  275.0 5.1 %collective-permute-start.41 = (bf16[3,24,768]{2,1,0:T(8,128)(2,1)S(1)}, bf16[3,24,768]{2,1,0:T(8,128)(2,1)S(1)}, u32[]{:S(2)}, u32[]{:S(2)}) collective-permute-start(bf16[3,24,768]{2,1,0:T(8,128)(2,1)S(1)} %get-tuple-element.204), channel_id=1, source_target_pairs={{0,24},{4,28},{8,16},{12,20},{16,8},{20,12},{24,0},{28,4},{1,25},{... | collective-permute-start | bytes 331784 | tf_op jit(solution)/shard_map/ppermute | solution.py:785
  280.6 3.9 collective-permute-done.45
  289.7 2.5 collective-permute-start.48
  292.2 8.7 %collective-permute-done.49.refs_2_ = bf16[24,4224]{1,0:T(8,128)(2,1)S(1)} collective-permute-done((bf16[24,4224]{1,0:T(8,128)(2,1)S(1)}, bf16[24,4224]{1,0:T(8,128)(2,1)S(1)}, u32[]{:S(2)}, u32[]{:S(2)}) %collective-permute-start.49) | collective-permute-done | bytes 202784 | tf_op jit(solution)/shard_map/ppermute | solution.py:785
  303.0 4.1 convolution_convert_fusion
  307.1 3.3 collective-permute-done.44.refs_3_
  324.9 2.6 collective-permute-start.62
  330.9 4.0 collective-permute-done.62.refs_13_
  338.0 5.6 %collective-permute-done.61.refs_12_ = bf16[2,3,24,768]{3,2,1,0:T(8,128)(2,1)} collective-permute-done((bf16[2,3,24,768]{3,2,1,0:T(8,128)(2,1)}, bf16[2,3,24,768]{3,2,1,0:T(8,128)(2,1)}, u32[]{:S(2)}, u32[]{:S(2)}) %collective-permute-start.61) | collective-permute-done | bytes 221216 | tf_op jit(solution)/shard_map/ppermute | solution.py:785
  349.5 4.3 %arrange.14 = bf16[3,4,8,24,768]{4,3,2,1,0:T(8,128)(2,1)} custom-call(s32[1]{0:T(128)} %bitcast.4.own_at, bf16[2,3,24,768]{3,2,1,0:T(8,128)(2,1)} %copy-done.16, bf16[2,3,24,768]{3,2,1,0:T(8,128)(2,1)} %copy-done.15, bf16[2,3,24,768]{3,2,1,0:T(8,128)(2,1)} %copy-done.41, bf16[2,3,24,768]{3,2,1,0:T(8,128)(2,1)} %copy-done.39, ...), custom_call_target="tpu_custom_call" | custom-call | bytes 7077888 | tf_op jit(solution)/shard_map/arrange/pallas_call | solution.py:804
  355.3 6.5 %refresh.4 = (f32[2,72,2304]{2,1,0:T(8,128)}, f32[2,24,768]{2,1,0:T(8,128)}, f32[2,72,768]{2,1,0:T(8,128)}, f32[32,2304]{1,0:T(8,128)}) custom-call(bf16[2304,768]{1,0:T(8,128)(2,1)} %bitcast.178, bf16[72,768]{1,0:T(8,128)(2,1)} %constant_dynamic-slice_fusion.own, bf16[32,768]{1,0:T(8,128)(2,1)} %fusion.42.select, f32[2,72,2304]{2,1,0:T(8,128)} %stat_left.3, ...), custom_call_target="tpu_custom_call" | custom-call | flops 736100352 | bytes 6709248 | tf_op jit(solution)/shard_map/refresh/pallas_call | solution.py:730
  366.6 3.9 add_convert_fusion.5
  378.9 6.4 %arrange.15 = (bf16[3,8,4,24,768]{4,3,2,1,0:T(8,128)(2,1)}, bf16[8,4,24,768]{3,2,1,0:T(8,128)(2,1)}, bf16[8,4,24,1152]{3,2,1,0:T(8,128)(2,1)}) custom-call(s32[1]{0:T(128)} %bitcast.4.own_at, bf16[2,24,4224]{2,1,0:T(8,128)(2,1)} %get-tuple-element.153.refs_0_, bf16[2,24,4224]{2,1,0:T(8,128)(2,1)} %copy-done.8, ...), custom_call_target="tpu_custom_call" | custom-call | bytes 12976128 | tf_op jit(solution)/shard_map/arrange/pallas_call | solution.py:804
  385.4 6.3 %refresh.7 = (f32[1,24,768]{2,1,0:T(8,128)}, f32[1,36,1152]{2,1,0:T(8,128)}, f32[3,24,768]{2,1,0:T(8,128)}, f32[48,768]{1,0:T(8,128)}) custom-call(bf16[768,1152]{1,0:T(8,128)(2,1)} %bitcast.195, bf16[24,4224]{1,0:T(8,128)(2,1)} %copy-done.4, bf16[48,1152]{1,0:T(8,128)(2,1)} %fusion.40.select, f32[1,24,768]{2,1,0:T(8,128)} %bitcast.211, ...), custom_call_target="tpu_custom_call" | custom-call | flops 254803968 | bytes 4644864 | tf_op jit(solution)/shard_map/refresh/pallas_call | solution.py:730
  394.7 3.6 refresh.6
  399.9 6.3 %refresh.5 = (f32[2,72,2304]{2,1,0:T(8,128)}, f32[2,24,768]{2,1,0:T(8,128)}, f32[2,72,768]{2,1,0:T(8,128)}, f32[32,2304]{1,0:T(8,128)}) custom-call(bf16[2304,768]{1,0:T(8,128)(2,1)} %bitcast.181, bf16[72,768]{1,0:T(8,128)(2,1)} %constant_dynamic-slice_fusion.8.own, ...), custom_call_target="tpu_custom_call", output_to_operand_aliasing={{0}: (8, {}), {1}: (9, {}), {2}: (10, {})} | custom-call | flops 736100352 | bytes 6709248 | tf_op jit(solution)/shard_map/refresh/pallas_call | solution.py:730
  (447 shorter events, 131.9 us)
Async XLA Ops:
  7.2 68.0 %all-gather.5.cloned.1.call-start = ((), (), s32[]{:S(2)}) async-start(), calls=%async_computation.3 | async-start | bytes 3686400 | tf_op jit(solution)/shard_map/all_gather | solution.py:985
  7.9 150.6 %all-gather.9.cloned.1.call-start = ((), (), s32[]{:S(2)}) async-start(), calls=%async_computation.6 | async-start | bytes 3649536 | tf_op jit(solution)/shard_map/all_gather | solution.py:996
  10.4 10.3 %collective-permute-start.2 = (bf16[72,896]{1,0:T(8,128)(2,1)S(1)}, bf16[72,896]{1,0:T(8,128)(2,1)S(1)}, u32[]{:S(2)}, u32[]{:S(2)}) collective-permute-start(bf16[72,896]{1,0:T(8,128)(2,1)S(1)} %fusion.41.refs_0_), channel_id=1, source_target_pairs={{0,3},{1,2},{2,1},{3,0},{4,7},{5,6},{6,5},{7,4},{8,11},{9,10},{10,... | collective-permute-start | bytes 387080 | tf_op jit(solution)/shard_map/ppermute | solution.py:785
  15.5 19.9 %collective-permute-start.1 = (bf16[72,896]{1,0:T(8,128)(2,1)S(1)}, bf16[72,896]{1,0:T(8,128)(2,1)S(1)}, u32[]{:S(2)}, u32[]{:S(2)}) collective-permute-start(bf16[72,896]{1,0:T(8,128)(2,1)S(1)} %fusion.41.refs_0_), channel_id=1, source_target_pairs={{0,2},{1,3},{2,0},{3,1},{4,6},{5,7},{6,4},{7,5},{8,10},{9,11},{10,... | collective-permute-start | bytes 387080 | tf_op jit(solution)/shard_map/ppermute | solution.py:785
  15.5 19.9 %collective-permute-start = (bf16[72,896]{1,0:T(8,128)(2,1)S(1)}, bf16[72,896]{1,0:T(8,128)(2,1)S(1)}, u32[]{:S(2)}, u32[]{:S(2)}) collective-permute-start(bf16[72,896]{1,0:T(8,128)(2,1)S(1)} %fusion.41.refs_0_), channel_id=1, source_target_pairs={{0,1},{1,0},{2,3},{3,2},{4,5},{5,4},{6,7},{7,6},{8,9},{9,8},{10,11... | collective-permute-start | bytes 387080 | tf_op jit(solution)/shard_map/ppermute | solution.py:785
  42.3 9.0 %collective-permute-start.4 = (bf16[2,72,896]{2,1,0:T(8,128)(2,1)S(1)}, bf16[2,72,896]{2,1,0:T(8,128)(2,1)S(1)}, u32[]{:S(2)}, u32[]{:S(2)}) collective-permute-start(bf16[2,72,896]{2,1,0:T(8,128)(2,1)S(1)} %get-tuple-element.214.refs_1_), channel_id=1, source_target_pairs={{0,4},{4,0},{8,12},{12,8},{16,20},{20,16},{24,28},{28,24},{1,5},{5... | collective-permute-start | bytes 774152 | tf_op jit(solution)/shard_map/ppermute | solution.py:785
  42.3 12.1 %collective-permute-start.5 = (bf16[2,72,896]{2,1,0:T(8,128)(2,1)S(1)}, bf16[2,72,896]{2,1,0:T(8,128)(2,1)}, u32[]{:S(2)}, u32[]{:S(2)}) collective-permute-start(bf16[2,72,896]{2,1,0:T(8,128)(2,1)S(1)} %get-tuple-element.215.refs_0_), channel_id=1, source_target_pairs={{0,8},{4,12},{8,0},{12,4},{16,24},{20,28},{24,16},{28,20},{1,9},{5... | collective-permute-start | bytes 774152 | tf_op jit(solution)/shard_map/ppermute | solution.py:785
  45.4 11.0 %collective-permute-start.9 = (bf16[2,72,896]{2,1,0:T(8,128)(2,1)S(1)}, bf16[2,72,896]{2,1,0:T(8,128)(2,1)}, u32[]{:S(2)}, u32[]{:S(2)}) collective-permute-start(bf16[2,72,896]{2,1,0:T(8,128)(2,1)S(1)} %get-tuple-element.215.refs_0_), channel_id=1, source_target_pairs={{0,16},{4,20},{8,24},{12,28},{16,0},{20,4},{24,8},{28,12},{1,17},{... | collective-permute-start | bytes 774152 | tf_op jit(solution)/shard_map/ppermute | solution.py:785
  45.8 10.6 %collective-permute-start.3 = (bf16[2,72,896]{2,1,0:T(8,128)(2,1)S(1)}, bf16[2,72,896]{2,1,0:T(8,128)(2,1)}, u32[]{:S(2)}, u32[]{:S(2)}) collective-permute-start(bf16[2,72,896]{2,1,0:T(8,128)(2,1)S(1)} %get-tuple-element.215.refs_0_), channel_id=1, source_target_pairs={{0,4},{4,0},{8,12},{12,8},{16,20},{20,16},{24,28},{28,24},{1,5},{5... | collective-permute-start | bytes 774152 | tf_op jit(solution)/shard_map/ppermute | solution.py:785
  48.9 9.4 %collective-permute-start.14 = (bf16[2,72,896]{2,1,0:T(8,128)(2,1)S(1)}, bf16[2,72,896]{2,1,0:T(8,128)(2,1)}, u32[]{:S(2)}, u32[]{:S(2)}) collective-permute-start(bf16[2,72,896]{2,1,0:T(8,128)(2,1)S(1)} %collective-permute-done.10.refs_9_), channel_id=1, source_target_pairs={{0,8},{4,12},{8,0},{12,4},{16,24},{20,28},{24,16},{28,20},{1,9},{5... | collective-permute-start | bytes 774152 | tf_op jit(solution)/shard_map/ppermute | solution.py:785
  75.2 13.8 %collective-permute-start.19 = (bf16[24,1920]{1,0:T(8,128)(2,1)S(1)}, bf16[24,1920]{1,0:T(8,128)(2,1)S(1)}, u32[]{:S(2)}, u32[]{:S(2)}) collective-permute-start(bf16[24,1920]{1,0:T(8,128)(2,1)S(1)} %pad_maximum_fusion.5.refs_0_), channel_id=1, source_target_pairs={{0,3},{1,2},{2,1},{3,0},{4,7},{5,6},{6,5},{7,4},{8,11},{9,10},{10,... | collective-permute-start | bytes 276488 | tf_op jit(solution)/shard_map/ppermute | solution.py:785
  78.6 10.4 %collective-permute-start.18 = (bf16[24,1920]{1,0:T(8,128)(2,1)S(1)}, bf16[24,1920]{1,0:T(8,128)(2,1)S(1)}, u32[]{:S(2)}, u32[]{:S(2)}) collective-permute-start(bf16[24,1920]{1,0:T(8,128)(2,1)S(1)} %pad_maximum_fusion.5.refs_0_), channel_id=1, source_target_pairs={{0,2},{1,3},{2,0},{3,1},{4,6},{5,7},{6,4},{7,5},{8,10},{9,11},{10,... | collective-permute-start | bytes 276488 | tf_op jit(solution)/shard_map/ppermute | solution.py:785
  78.6 10.5 %collective-permute-start.17 = (bf16[24,1920]{1,0:T(8,128)(2,1)S(1)}, bf16[24,1920]{1,0:T(8,128)(2,1)S(1)}, u32[]{:S(2)}, u32[]{:S(2)}) collective-permute-start(bf16[24,1920]{1,0:T(8,128)(2,1)S(1)} %pad_maximum_fusion.5.refs_0_), channel_id=1, source_target_pairs={{0,1},{1,0},{2,3},{3,2},{4,5},{5,4},{6,7},{7,6},{8,9},{9,8},{10,11... | collective-permute-start | bytes 276488 | tf_op jit(solution)/shard_map/ppermute | solution.py:785
  94.3 9.1 %collective-permute-start.20 = (bf16[2,24,1920]{2,1,0:T(8,128)(2,1)S(1)}, bf16[2,24,1920]{2,1,0:T(8,128)(2,1)S(1)}, u32[]{:S(2)}, u32[]{:S(2)}) collective-permute-start(bf16[2,24,1920]{2,1,0:T(8,128)(2,1)S(1)} %get-tuple-element.120.refs_0_), channel_id=1, source_target_pairs={{0,8},{4,12},{8,0},{12,4},{16,24},{20,28},{24,16},{28,20},{1,9},{5... | collective-permute-start | bytes 552968 | tf_op jit(solution)/shard_map/ppermute | solution.py:785
  96.6 26.2 %collective-permute-start.21 = (bf16[2,24,1920]{2,1,0:T(8,128)(2,1)S(1)}, bf16[2,24,1920]{2,1,0:T(8,128)(2,1)S(1)}, u32[]{:S(2)}, u32[]{:S(2)}) collective-permute-start(bf16[2,24,1920]{2,1,0:T(8,128)(2,1)S(1)} %get-tuple-element.121.refs_1_), channel_id=1, source_target_pairs={{0,8},{4,12},{8,0},{12,4},{16,24},{20,28},{24,16},{28,20},{1,9},{5... | collective-permute-start | bytes 552968 | tf_op jit(solution)/shard_map/ppermute | solution.py:785
  96.8 26.0 %collective-permute-start.22 = (bf16[2,24,1920]{2,1,0:T(8,128)(2,1)S(1)}, bf16[2,24,1920]{2,1,0:T(8,128)(2,1)S(1)}, u32[]{:S(2)}, u32[]{:S(2)}) collective-permute-start(bf16[2,24,1920]{2,1,0:T(8,128)(2,1)S(1)} %get-tuple-element.120.refs_0_), channel_id=1, source_target_pairs={{0,16},{4,20},{8,24},{12,28},{16,0},{20,4},{24,8},{28,12},{1,17},{... | collective-permute-start | bytes 552968 | tf_op jit(solution)/shard_map/ppermute | solution.py:785
  100.5 22.4 %collective-permute-start.25 = (bf16[2,24,1920]{2,1,0:T(8,128)(2,1)S(1)}, bf16[2,24,1920]{2,1,0:T(8,128)(2,1)S(1)}, u32[]{:S(2)}, u32[]{:S(2)}) collective-permute-start(bf16[2,24,1920]{2,1,0:T(8,128)(2,1)S(1)} %collective-permute-done.23.refs_9_), channel_id=1, source_target_pairs={{0,8},{4,12},{8,0},{12,4},{16,24},{20,28},{24,16},{28,20},{1,9},{5... | collective-permute-start | bytes 552968 | tf_op jit(solution)/shard_map/ppermute | solution.py:785
  103.4 19.5 %collective-permute-start.24 = (bf16[2,24,1920]{2,1,0:T(8,128)(2,1)S(1)}, bf16[2,24,1920]{2,1,0:T(8,128)(2,1)S(1)}, u32[]{:S(2)}, u32[]{:S(2)}) collective-permute-start(bf16[2,24,1920]{2,1,0:T(8,128)(2,1)S(1)} %collective-permute-done.20.refs_4_), channel_id=1, source_target_pairs={{0,16},{4,20},{8,24},{12,28},{16,0},{20,4},{24,8},{28,12},{1,17},{... | collective-permute-start | bytes 552968 | tf_op jit(solution)/shard_map/ppermute | solution.py:785
  126.4 27.3 %all-to-all-start = ((bf16[4,720,128]{2,1,0:T(8,128)(2,1)}), bf16[4,720,128]{2,1,0:T(8,128)(2,1)S(1)}, u32[]{:S(2)}, u32[]{:S(2)}) async-start(bf16[4,720,128]{2,1,0:T(8,128)(2,1)} %maximum_maximum_fusion.2), calls=%async_computation | async-start | bytes 1474560 | tf_op jit(solution)/shard_map/all_to_all | solution.py:1175
  177.2 23.3 %all-to-all-start.1 = ((bf16[4,720,128]{2,1,0:T(8,128)(2,1)}), bf16[4,720,128]{2,1,0:T(8,128)(2,1)S(1)}, u32[]{:S(2)}, u32[]{:S(2)}) async-start(bf16[4,720,128]{2,1,0:T(8,128)(2,1)} %copy.101), calls=%async_computation.1 | async-start | bytes 1474560 | tf_op jit(solution)/shard_map/all_to_all | solution.py:1206
  180.7 135.9 %all-gather.7.cloned.1.call-start = ((), (), s32[]{:S(2)}) async-start(), calls=%async_computation.4 | async-start | bytes 6488064 | tf_op jit(solution)/shard_map/all_gather | solution.py:1230
  200.5 209.2 %reduce-scatter.2.cloned.1.call-start = ((), (), s32[]{:S(2)}) async-start(), calls=%async_computation.5 | async-start | bytes 3686400 | tf_op jit(solution)/shard_map/reduce_scatter | solution.py:1319
  210.6 31.9 %collective-permute-start.35 = (bf16[96,4224]{1,0:T(8,128)(2,1)}, bf16[96,4224]{1,0:T(8,128)(2,1)}, u32[]{:S(2)}, u32[]{:S(2)}) collective-permute-start(bf16[96,4224]{1,0:T(8,128)(2,1)} %get-tuple-element.138), channel_id=1, source_target_pairs={{0,8},{4,12},{8,0},{12,4},{16,24},{20,28},{24,16},{28,20},{1,9},{5... | collective-permute-start | bytes 2433032 | tf_op jit(solution)/shard_map/ppermute | solution.py:785
  213.0 29.5 %collective-permute-start.36 = (bf16[96,4224]{1,0:T(8,128)(2,1)}, bf16[96,4224]{1,0:T(8,128)(2,1)}, u32[]{:S(2)}, u32[]{:S(2)}) collective-permute-start(bf16[96,4224]{1,0:T(8,128)(2,1)} %get-tuple-element.139), channel_id=1, source_target_pairs={{0,16},{4,20},{8,24},{12,28},{16,0},{20,4},{24,8},{28,12},{1,17},{... | collective-permute-start | bytes 2433032 | tf_op jit(solution)/shard_map/ppermute | solution.py:785
  213.0 43.6 %collective-permute-start.37 = (bf16[96,4224]{1,0:T(8,128)(2,1)}, bf16[96,4224]{1,0:T(8,128)(2,1)}, u32[]{:S(2)}, u32[]{:S(2)}) collective-permute-start(bf16[96,4224]{1,0:T(8,128)(2,1)} %get-tuple-element.140), channel_id=1, source_target_pairs={{0,24},{4,28},{8,16},{12,20},{16,8},{20,12},{24,0},{28,4},{1,25},{... | collective-permute-start | bytes 2433032 | tf_op jit(solution)/shard_map/ppermute | solution.py:785
  258.7 12.1 %collective-permute-start.46 = (bf16[24,4224]{1,0:T(8,128)(2,1)S(1)}, bf16[24,4224]{1,0:T(8,128)(2,1)S(1)}, u32[]{:S(2)}, u32[]{:S(2)}) collective-permute-start(bf16[24,4224]{1,0:T(8,128)(2,1)S(1)} %get-tuple-element.209), channel_id=1, source_target_pairs={{0,1},{1,0},{2,3},{3,2},{4,5},{5,4},{6,7},{7,6},{8,9},{9,8},{10,11... | collective-permute-start | bytes 608264 | tf_op jit(solution)/shard_map/ppermute | solution.py:785
  264.4 20.1 %collective-permute-start.45 = (bf16[24,4224]{1,0:T(8,128)(2,1)S(1)}, bf16[24,4224]{1,0:T(8,128)(2,1)S(1)}, u32[]{:S(2)}, u32[]{:S(2)}) collective-permute-start(bf16[24,4224]{1,0:T(8,128)(2,1)S(1)} %get-tuple-element.208), channel_id=1, source_target_pairs={{0,1},{1,0},{2,3},{3,2},{4,5},{5,4},{6,7},{7,6},{8,9},{9,8},{10,11... | collective-permute-start | bytes 608264 | tf_op jit(solution)/shard_map/ppermute | solution.py:785
  264.9 8.6 %collective-permute-start.38 = (bf16[3,4,24,768]{3,2,0,1:T(8,128)(2,1)S(1)}, bf16[3,4,24,768]{3,2,0,1:T(8,128)(2,1)S(1)}, u32[]{:S(2)}, u32[]{:S(2)}) collective-permute-start(bf16[3,4,24,768]{3,2,0,1:T(8,128)(2,1)S(1)} %copy_bitcast_fusion), channel_id=1, source_target_pairs={{0,4},{4,0},{8,12},{12,8},{16,20},{20,16},{24,28},{28,24},{1,5},{5... | collective-permute-start | bytes 1327112 | tf_op jit(solution)/shard_map/ppermute | solution.py:785
  270.8 13.7 %collective-permute-start.47 = (bf16[24,4224]{1,0:T(8,128)(2,1)S(1)}, bf16[24,4224]{1,0:T(8,128)(2,1)S(1)}, u32[]{:S(2)}, u32[]{:S(2)}) collective-permute-start(bf16[24,4224]{1,0:T(8,128)(2,1)S(1)} %fusion.30), channel_id=1, source_target_pairs={{0,2},{1,3},{2,0},{3,1},{4,6},{5,7},{6,4},{7,5},{8,10},{9,11},{10,... | collective-permute-start | bytes 608264 | tf_op jit(solution)/shard_map/ppermute | solution.py:785
  273.6 13.0 %collective-permute-start.39 = (bf16[3,24,768]{2,1,0:T(8,128)(2,1)S(1)}, bf16[3,24,768]{2,1,0:T(8,128)(2,1)S(1)}, u32[]{:S(2)}, u32[]{:S(2)}) collective-permute-start(bf16[3,24,768]{2,1,0:T(8,128)(2,1)S(1)} %get-tuple-element.203), channel_id=1, source_target_pairs={{0,8},{4,12},{8,0},{12,4},{16,24},{20,28},{24,16},{28,20},{1,9},{5... | collective-permute-start | bytes 331784 | tf_op jit(solution)/shard_map/ppermute | solution.py:785
  275.0 11.7 %collective-permute-start.41 = (bf16[3,24,768]{2,1,0:T(8,128)(2,1)S(1)}, bf16[3,24,768]{2,1,0:T(8,128)(2,1)S(1)}, u32[]{:S(2)}, u32[]{:S(2)}) collective-permute-start(bf16[3,24,768]{2,1,0:T(8,128)(2,1)S(1)} %get-tuple-element.204), channel_id=1, source_target_pairs={{0,24},{4,28},{8,16},{12,20},{16,8},{20,12},{24,0},{28,4},{1,25},{... | collective-permute-start | bytes 331784 | tf_op jit(solution)/shard_map/ppermute | solution.py:785
  285.3 15.6 %collective-permute-start.49 = (bf16[24,4224]{1,0:T(8,128)(2,1)S(1)}, bf16[24,4224]{1,0:T(8,128)(2,1)S(1)}, u32[]{:S(2)}, u32[]{:S(2)}) collective-permute-start(bf16[24,4224]{1,0:T(8,128)(2,1)S(1)} %get-tuple-element.190.refs_0_.own), channel_id=1, source_target_pairs={{0,2},{1,3},{2,0},{3,1},{4,6},{5,7},{6,4},{7,5},{8,10},{9,11},{10,... | collective-permute-start | bytes 608264 | tf_op jit(solution)/shard_map/ppermute | solution.py:785
  286.8 15.4 %collective-permute-start.43 = (bf16[3,24,768]{2,1,0:T(8,128)(2,1)S(1)}, bf16[3,24,768]{2,1,0:T(8,128)(2,1)S(1)}, u32[]{:S(2)}, u32[]{:S(2)}) collective-permute-start(bf16[3,24,768]{2,1,0:T(8,128)(2,1)S(1)} %add_convert_fusion.6.refs_0_), channel_id=1, source_target_pairs={{0,2},{1,3},{2,0},{3,1},{4,6},{5,7},{6,4},{7,5},{8,10},{9,11},{10,... | collective-permute-start | bytes 331784 | tf_op jit(solution)/shard_map/ppermute | solution.py:785
  289.7 23.3 %collective-permute-start.48 = (bf16[24,4224]{1,0:T(8,128)(2,1)S(1)}, bf16[24,4224]{1,0:T(8,128)(2,1)S(1)}, u32[]{:S(2)}, u32[]{:S(2)}) collective-permute-start(bf16[24,4224]{1,0:T(8,128)(2,1)S(1)} %get-tuple-element.190.refs_0_.own), channel_id=1, source_target_pairs={{0,1},{1,0},{2,3},{3,2},{4,5},{5,4},{6,7},{7,6},{8,9},{9,8},{10,11... | collective-permute-start | bytes 608264 | tf_op jit(solution)/shard_map/ppermute | solution.py:785
  292.1 15.0 %collective-permute-start.42 = (bf16[3,24,768]{2,1,0:T(8,128)(2,1)S(1)}, bf16[3,24,768]{2,1,0:T(8,128)(2,1)S(1)}, u32[]{:S(2)}, u32[]{:S(2)}) collective-permute-start(bf16[3,24,768]{2,1,0:T(8,128)(2,1)S(1)} %add_convert_fusion.6.refs_0_), channel_id=1, source_target_pairs={{0,1},{1,0},{2,3},{3,2},{4,5},{5,4},{6,7},{7,6},{8,9},{9,8},{10,11... | collective-permute-start | bytes 331784 | tf_op jit(solution)/shard_map/ppermute | solution.py:785
  301.0 12.1 %collective-permute-start.50 = (bf16[24,4224]{1,0:T(8,128)(2,1)S(1)}, bf16[24,4224]{1,0:T(8,128)(2,1)S(1)}, u32[]{:S(2)}, u32[]{:S(2)}) collective-permute-start(bf16[24,4224]{1,0:T(8,128)(2,1)S(1)} %collective-permute-done.49.refs_2_), channel_id=1, source_target_pairs={{0,1},{1,0},{2,3},{3,2},{4,5},{5,4},{6,7},{7,6},{8,9},{9,8},{10,11... | collective-permute-start | bytes 608264 | tf_op jit(solution)/shard_map/ppermute | solution.py:785
  302.2 8.3 %collective-permute-start.44 = (bf16[3,24,768]{2,1,0:T(8,128)(2,1)S(1)}, bf16[3,24,768]{2,1,0:T(8,128)(2,1)S(1)}, u32[]{:S(2)}, u32[]{:S(2)}) collective-permute-start(bf16[3,24,768]{2,1,0:T(8,128)(2,1)S(1)} %collective-permute-done.43.refs_2_), channel_id=1, source_target_pairs={{0,1},{1,0},{2,3},{3,2},{4,5},{5,4},{6,7},{7,6},{8,9},{9,8},{10,11... | collective-permute-start | bytes 331784 | tf_op jit(solution)/shard_map/ppermute | solution.py:785
  324.9 10.1 %collective-permute-start.62 = (bf16[2,3,24,768]{3,2,1,0:T(8,128)(2,1)}, bf16[2,3,24,768]{3,2,1,0:T(8,128)(2,1)S(1)}, u32[]{:S(2)}, u32[]{:S(2)}) collective-permute-start(bf16[2,3,24,768]{3,2,1,0:T(8,128)(2,1)} %collective-permute-done.58.refs_9_), channel_id=1, source_target_pairs={{0,8},{4,12},{8,0},{12,4},{16,24},{20,28},{24,16},{28,20},{1,9},{5... | collective-permute-start | bytes 663560 | tf_op jit(solution)/shard_map/ppermute | solution.py:785
  328.3 18.0 %collective-permute-start.68 = (bf16[2,24,4224]{2,1,0:T(8,128)(2,1)S(1)}, bf16[2,24,4224]{2,1,0:T(8,128)(2,1)}, u32[]{:S(2)}, u32[]{:S(2)}) collective-permute-start(bf16[2,24,4224]{2,1,0:T(8,128)(2,1)S(1)} %get-tuple-element.154.refs_1_), channel_id=1, source_target_pairs={{0,16},{4,20},{8,24},{12,28},{16,0},{20,4},{24,8},{28,12},{1,17},{... | collective-permute-start | bytes 1216520 | tf_op jit(solution)/shard_map/ppermute | solution.py:785
  329.2 17.1 %collective-permute-start.65 = (bf16[2,24,4224]{2,1,0:T(8,128)(2,1)}, bf16[2,24,4224]{2,1,0:T(8,128)(2,1)}, u32[]{:S(2)}, u32[]{:S(2)}) collective-permute-start(bf16[2,24,4224]{2,1,0:T(8,128)(2,1)} %get-tuple-element.153.refs_0_), channel_id=1, source_target_pairs={{0,8},{4,12},{8,0},{12,4},{16,24},{20,28},{24,16},{28,20},{1,9},{5... | collective-permute-start | bytes 1216520 | tf_op jit(solution)/shard_map/ppermute | solution.py:785
  337.3 9.5 %collective-permute-start.64 = (bf16[2,3,24,768]{3,2,1,0:T(8,128)(2,1)}, bf16[2,3,24,768]{3,2,1,0:T(8,128)(2,1)}, u32[]{:S(2)}, u32[]{:S(2)}) collective-permute-start(bf16[2,3,24,768]{3,2,1,0:T(8,128)(2,1)} %copy-done.42), channel_id=1, source_target_pairs={{0,4},{4,0},{8,12},{12,8},{16,20},{20,16},{24,28},{28,24},{1,5},{5... | collective-permute-start | bytes 663560 | tf_op jit(solution)/shard_map/ppermute | solution.py:785
  343.6 18.2 %collective-permute-start.66 = (bf16[2,24,4224]{2,1,0:T(8,128)(2,1)S(1)}, bf16[2,24,4224]{2,1,0:T(8,128)(2,1)}, u32[]{:S(2)}, u32[]{:S(2)}) collective-permute-start(bf16[2,24,4224]{2,1,0:T(8,128)(2,1)S(1)} %get-tuple-element.154.refs_1_), channel_id=1, source_target_pairs={{0,8},{4,12},{8,0},{12,4},{16,24},{20,28},{24,16},{28,20},{1,9},{5... | collective-permute-start | bytes 1216520 | tf_op jit(solution)/shard_map/ppermute | solution.py:785
  345.4 16.4 %collective-permute-start.67 = (bf16[2,24,4224]{2,1,0:T(8,128)(2,1)}, bf16[2,24,4224]{2,1,0:T(8,128)(2,1)}, u32[]{:S(2)}, u32[]{:S(2)}) collective-permute-start(bf16[2,24,4224]{2,1,0:T(8,128)(2,1)} %get-tuple-element.153.refs_0_), channel_id=1, source_target_pairs={{0,16},{4,20},{8,24},{12,28},{16,0},{20,4},{24,8},{28,12},{1,17},{... | collective-permute-start | bytes 1216520 | tf_op jit(solution)/shard_map/ppermute | solution.py:785
  346.3 16.4 %collective-permute-start.70 = (bf16[2,24,4224]{2,1,0:T(8,128)(2,1)}, bf16[2,24,4224]{2,1,0:T(8,128)(2,1)}, u32[]{:S(2)}, u32[]{:S(2)}) collective-permute-start(bf16[2,24,4224]{2,1,0:T(8,128)(2,1)} %collective-permute-done.68.refs_9_), channel_id=1, source_target_pairs={{0,8},{4,12},{8,0},{12,4},{16,24},{20,28},{24,16},{28,20},{1,9},{5... | collective-permute-start | bytes 1216520 | tf_op jit(solution)/shard_map/ppermute | solution.py:785
  346.8 17.6 %collective-permute-start.69 = (bf16[2,24,4224]{2,1,0:T(8,128)(2,1)}, bf16[2,24,4224]{2,1,0:T(8,128)(2,1)}, u32[]{:S(2)}, u32[]{:S(2)}) collective-permute-start(bf16[2,24,4224]{2,1,0:T(8,128)(2,1)} %collective-permute-done.65.refs_4_), channel_id=1, source_target_pairs={{0,16},{4,20},{8,24},{12,28},{16,0},{20,4},{24,8},{28,12},{1,17},{... | collective-permute-start | bytes 1216520 | tf_op jit(solution)/shard_map/ppermute | solution.py:785
  364.4 9.8 %collective-permute-start.71 = (bf16[2,24,4224]{2,1,0:T(8,128)(2,1)}, bf16[2,24,4224]{2,1,0:T(8,128)(2,1)}, u32[]{:S(2)}, u32[]{:S(2)}) collective-permute-start(bf16[2,24,4224]{2,1,0:T(8,128)(2,1)} %get-tuple-element.153.refs_0_), channel_id=1, source_target_pairs={{0,4},{4,0},{8,12},{12,8},{16,20},{20,16},{24,28},{28,24},{1,5},{5... | collective-permute-start | bytes 1216520 | tf_op jit(solution)/shard_map/ppermute | solution.py:785
  364.4 10.2 %collective-permute-start.72 = (bf16[2,24,4224]{2,1,0:T(8,128)(2,1)S(1)}, bf16[2,24,4224]{2,1,0:T(8,128)(2,1)}, u32[]{:S(2)}, u32[]{:S(2)}) collective-permute-start(bf16[2,24,4224]{2,1,0:T(8,128)(2,1)S(1)} %get-tuple-element.154.refs_1_), channel_id=1, source_target_pairs={{0,4},{4,0},{8,12},{12,8},{16,20},{20,16},{24,28},{28,24},{1,5},{5... | collective-permute-start | bytes 1216520 | tf_op jit(solution)/shard_map/ppermute | solution.py:785
  364.9 9.8 %collective-permute-start.73 = (bf16[2,24,4224]{2,1,0:T(8,128)(2,1)}, bf16[2,24,4224]{2,1,0:T(8,128)(2,1)}, u32[]{:S(2)}, u32[]{:S(2)}) collective-permute-start(bf16[2,24,4224]{2,1,0:T(8,128)(2,1)} %collective-permute-done.65.refs_4_), channel_id=1, source_target_pairs={{0,4},{4,0},{8,12},{12,8},{16,20},{20,16},{24,28},{28,24},{1,5},{5... | collective-permute-start | bytes 1216520 | tf_op jit(solution)/shard_map/ppermute | solution.py:785
  (124 other events, 988.7 us)
Sparse Core Ops, SparseCore 0:
  9.6 65.0 all-gather.4
  78.0 67.8 all-gather.8
  200.6 84.2 all-gather.6
  316.7 59.0 reduce-scatter.1

commit v5 on v4

--- a/solution.py
+++ b/solution.py
@@ -1311,7 +1311,7 @@
         lax.dynamic_index_in_dim(qkv_term, side, 2, keepdims=False) for side in (1 - core, core)
     ]
     qkv_sum = add_partners(lows(pair_sums(*qkv_halves, axis=1)), "dp", 2).astype(BF16)
-    qkv_plane = gather_plane(qkv_sum, by_steps=True)
+    qkv_plane = gather_plane(qkv_sum)
     input_term = jnp.dot(grad_qkv, back_weight, preferred_element_type=F32).astype(BF16)
     input_term, roots = fence(input_term, roots, qkv_plane, term_plane)[:2]
     qkv_blocks = gather_cores(gather_partners(qkv_plane))

time: 426 us -> 421 us (0.988)
  waiting for transfers between devices: 96.3 us -> 82.1 us
  Pallas kernels: 118 us -> 125 us
    ppermute x79, waiting for transfers between devices: 83.9 us -> 71.7 us  [exchange(): return lax.ppermute(values, axis, [(i, i ^ offset) for i in range(size)])]
    pallas_call x1, Pallas kernels: 28 us -> 32.5 us  [head_body(): pl.pallas_call(attend_back_kernel, grid_spec=pltpu.PrefetchScalarGridSpec...]
  transfers between devices with their start and end apart: 85 -> 85, of which waited for: 25 -> 24; matrix products, arithmetic and copies ran while one was open for 20% -> 20% of each run, Pallas kernels for 28% -> 30%
where the time goes in v5:
time: 421 us; the launch traced here: 415 us
  Pallas kernels  125 us (30%)
  waiting for transfers between devices  82.1 us (20%)
  starting transfers between devices  77.3 us (18%)
  local copies, waits for them, and re-layouts  46.8 us (11%)
  other arithmetic  42.2 us (10%)
  matrix products  25.1 us (6%)
  between operations  16.2 us (4%)
    ppermute x79, waiting for transfers between devices, exchange(): return lax.ppermute(values, axis, [(i, i ^ offset) for i in range(size)])  71.7 us
    ppermute x79, starting transfers between devices, exchange(): return lax.ppermute(values, axis, [(i, i ^ offset) for i in range(size)])  68.5 us
    pallas_call x1, Pallas kernels, head_body(): pl.pallas_call(attend_back_kernel, grid_spec=pltpu.PrefetchScalarGridSpec...  32.5 us
    pallas_call x8, Pallas kernels, arrange(): pl.pallas_call(functools.partial(arrange_kernel, count=count, moves=moves...  26.8 us
    pallas_call x4, Pallas kernels, refresh(): pl.pallas_call(functools.partial(refresh_kernel, kept=len(previous), own_...  22.7 us
    pallas_call x1, Pallas kernels, head_body(): pl.pallas_call(attend_kernel, grid_spec=pltpu.PrefetchScalarGridSpec(num_...  22.4 us
    unnamed x181, local copies, waits for them, and re-layouts  13.2 us
    pallas_call x1, Pallas kernels, head_body(): pl.pallas_call(terms_kernel, grid=(2,), in_specs=[pl.BlockSpec(memory_spa...  11.6 us
  transfers between devices with their start and end apart: 85, of which 24 were waited for; matrix products, arithmetic and copies ran while one was open for 20% of the time, Pallas kernels for 30%

profile of v5, /device:TPU:0, one launch (start us, length us, event | category | flops | bytes accessed | tf_op | source)
XLA Modules:
  0.0 415.1 jit_solution(5021405267413412620)
XLA Ops:
  10.4 5.1 %collective-permute-start.2 = (bf16[72,896]{1,0:T(8,128)(2,1)S(1)}, bf16[72,896]{1,0:T(8,128)(2,1)S(1)}, u32[]{:S(2)}, u32[]{:S(2)}) collective-permute-start(bf16[72,896]{1,0:T(8,128)(2,1)S(1)} %fusion.41.refs_0_), channel_id=1, source_target_pairs={{0,3},{1,2},{2,1},{3,0},{4,7},{5,6},{6,5},{7,4},{8,11},{9,10},{10,... | collective-permute-start | bytes 387080 | tf_op jit(solution)/shard_map/ppermute | solution.py:785
  17.2 3.5 multiply_sine_fusion
  20.8 14.7 %collective-permute-done.1.refs_2_ = bf16[72,896]{1,0:T(8,128)(2,1)S(1)} collective-permute-done((bf16[72,896]{1,0:T(8,128)(2,1)S(1)}, bf16[72,896]{1,0:T(8,128)(2,1)S(1)}, u32[]{:S(2)}, u32[]{:S(2)}) %collective-permute-start.1) | collective-permute-done | bytes 129056 | tf_op jit(solution)/shard_map/ppermute | solution.py:785
  42.8 2.5 select_convert_fusion.key_mask
  45.8 3.1 collective-permute-done.6.refs_5_
  48.9 2.5 collective-permute-start.14
  51.4 3.1 collective-permute-done.5.refs_4_
  58.8 2.3 collective-permute-done.13.refs_12_
  61.1 2.9 pad_maximum_fusion.1
  65.1 4.5 %arrange.9 = (bf16[8,4,72,768]{3,2,1,0:T(8,128)(2,1)}, bf16[8,4,72,128]{3,2,1,0:T(8,128)(2,1)}) custom-call(s32[1]{0:T(128)} %bitcast.4.own_at, bf16[2,72,896]{2,1,0:T(8,128)(2,1)} %copy-done.12, bf16[2,72,896]{2,1,0:T(8,128)(2,1)} %copy-done.11, bf16[2,72,896]{2,1,0:T(8,128)(2,1)} %collective-permute-done.3.refs_2_, bf16[2,72,896]{2,1,0:T(8,128)(2,1)} %copy-done.33, ...), custom_call_target="tpu_custom_call" | custom-call | bytes 8257536 | tf_op jit(solution)/shard_map/arrange/pallas_call | solution.py:804
  75.2 3.4 collective-permute-start.19
  79.5 9.4 %project.1 = (bf16[1920,768]{1,0:T(8,128)(2,1)}, bf16[3,1920,128]{2,1,0:T(8,128)(2,1)}, bf16[3,2400,128]{2,1,0:T(8,128)(2,1)}, bf16[3,2400,128]{2,1,0:T(8,128)(2,1)}) custom-call(bf16[1920,768]{1,0:T(8,128)(2,1)} %all-gather.5.cloned.1.call-done.tokens, bf16[640,768]{1,0:T(8,128)(2,1)} %maximum_maximum_fusion.weight, f32[1,768]{1,0:T(1,128)} %slice.196.gain, ...), custom_call_target="tpu_custom_call" | custom-call | flops 1887436800 | bytes 14000000 | tf_op jit(solution)/shard_map/project/pallas_call | solution.py:1077
  100.5 2.9 collective-permute-start.25
  103.4 22.4 %attend.1 = (bf16[1920,128]{1,0:T(8,128)(2,1)}, bf16[1920,128]{1,0:T(8,128)(2,1)}, bf16[3,1920,128]{2,1,0:T(8,128)(2,1)}) custom-call(s32[4]{0:T(128)} %get-tuple-element.195.start_at, s32[4]{0:T(128)} %get-tuple-element.194.step_count, s32[1]{0:T(128)} %sub.86.pad_from, bf16[3,1920,128]{2,1,0:T(8,128)(2,1)} %get-tuple-element.111.query, ...), custom_call_target="tpu_custom_call" | custom-call | flops 2831155200 | bytes 12000000 | tf_op jit(solution)/shard_map/attend/pallas_call | solution.py:1132
  129.3 5.1 %all-to-all-start = ((bf16[4,720,128]{2,1,0:T(8,128)(2,1)}), bf16[4,720,128]{2,1,0:T(8,128)(2,1)S(1)}, u32[]{:S(2)}, u32[]{:S(2)}) async-start(bf16[4,720,128]{2,1,0:T(8,128)(2,1)} %maximum_maximum_fusion.2), calls=%async_computation | async-start | bytes 1474560 | tf_op jit(solution)/shard_map/all_to_all | solution.py:1175
  140.9 3.8 arrange.11
  144.7 9.7 %all-to-all-done = bf16[4,720,128]{2,1,0:T(8,128)(2,1)S(1)} async-done(((bf16[4,720,128]{2,1,0:T(8,128)(2,1)}), bf16[4,720,128]{2,1,0:T(8,128)(2,1)S(1)}, u32[]{:S(2)}, u32[]{:S(2)}) %all-to-all-start) | async-done | bytes 737312 | tf_op jit(solution)/shard_map/all_to_all | solution.py:1175
  155.7 2.2 fusion.69
  159.4 4.3 %fusion.2 = f32[480,2304]{1,0:T(8,128)S(1)} fusion(bf16[480,768]{1,0:T(8,128)(2,1)} %multiply_convert_fusion.2.ffn_in, bf16[1,2304,768]{2,1,0:T(8,128)(2,1)} %all-gather.9.cloned.1.call-done), kind=kOutput, calls=%fused_computation.2 | convolution fusion | flops 1698693120 | bytes 8699904 | tf_op jit(solution)/shard_map/dot_general | solution.py:84
  163.7 2.8 fusion.9
  178.0 3.5 all-to-all-start.1
  184.3 2.3 copy.97.attended
  186.6 3.1 pad_maximum_fusion.grad_proj
  189.7 11.6 %terms.1 = (bf16[4,96,4224]{2,1,0:T(8,128)(2,1)}, bf16[4,96,4224]{2,1,0:T(8,128)(2,1)}) custom-call(s32[1]{0:T(128)} %bitcast.22.core, bf16[480,2304]{1,0:T(8,128)(2,1)} %pad_maximum_fusion.grad_proj, bf16[480,768]{1,0:T(8,128)(2,1)} %multiply_convert_fusion.2.ffn_in, bf16[480,768]{1,0:T(8,128)(2,1)} %copy-done.18, bf16[480,768]{1,0:T(8,128)(2,1)} %copy.97.attended, ...), custom_call_target="tpu_custom_call" | custom-call | flops 3114270720 | bytes 13000000 | tf_op jit(solution)/shard_map/terms/pallas_call | solution.py:1214
  203.5 4.1 collective-permute-done.34
  207.6 3.8 fusion.29
  214.9 32.5 %attend_back.1 = bf16[1920,640]{1,0:T(8,128)(2,1)} custom-call(s32[4]{0:T(128)} %get-tuple-element.195.start_at, s32[4]{0:T(128)} %get-tuple-element.194.step_count, s32[1]{0:T(128)} %sub.86.pad_from, bf16[3,1920,128]{2,1,0:T(8,128)(2,1)} %get-tuple-element.130.query, bf16[1920,128]{1,0:T(8,128)(2,1)} %get-tuple-element.118.pair_out, ...), custom_call_target="tpu_custom_call" | custom-call | flops 7077888000 | bytes 15000000 | tf_op jit(solution)/shard_map/attend_back/pallas_call | solution.py:1250
  247.5 10.0 %collective-permute-done.37 = bf16[96,4224]{1,0:T(8,128)(2,1)} collective-permute-done((bf16[96,4224]{1,0:T(8,128)(2,1)}, bf16[96,4224]{1,0:T(8,128)(2,1)}, u32[]{:S(2)}, u32[]{:S(2)}) %collective-permute-start.37) | collective-permute-done | bytes 811040 | tf_op jit(solution)/shard_map/ppermute | solution.py:785
  259.6 2.3 collective-permute-start.46
  261.9 4.0 fusion.70
  266.2 6.2 %collective-permute-done.46 = bf16[24,4224]{1,0:T(8,128)(2,1)S(1)} collective-permute-done((bf16[24,4224]{1,0:T(8,128)(2,1)S(1)}, bf16[24,4224]{1,0:T(8,128)(2,1)S(1)}, u32[]{:S(2)}, u32[]{:S(2)}) %collective-permute-start.46) | collective-permute-done | bytes 202784 | tf_op jit(solution)/shard_map/ppermute | solution.py:785
  272.5 5.5 %collective-permute-start.47 = (bf16[24,4224]{1,0:T(8,128)(2,1)S(1)}, bf16[24,4224]{1,0:T(8,128)(2,1)S(1)}, u32[]{:S(2)}, u32[]{:S(2)}) collective-permute-start(bf16[24,4224]{1,0:T(8,128)(2,1)S(1)} %fusion.30), channel_id=1, source_target_pairs={{0,2},{1,3},{2,0},{3,1},{4,6},{5,7},{6,4},{7,5},{8,10},{9,11},{10,... | collective-permute-start | bytes 608264 | tf_op jit(solution)/shard_map/ppermute | solution.py:785
  283.6 2.3 collective-permute-done.47
  286.7 3.7 collective-permute-start.48
  292.1 2.9 collective-permute-start.42
  295.0 4.7 %collective-permute-done.49.refs_2_ = bf16[24,4224]{1,0:T(8,128)(2,1)S(1)} collective-permute-done((bf16[24,4224]{1,0:T(8,128)(2,1)S(1)}, bf16[24,4224]{1,0:T(8,128)(2,1)S(1)}, u32[]{:S(2)}, u32[]{:S(2)}) %collective-permute-start.49) | collective-permute-done | bytes 202784 | tf_op jit(solution)/shard_map/ppermute | solution.py:785
  300.3 4.1 convolution_convert_fusion
  312.2 2.8 collective-permute-start.58
  319.0 2.3 collective-permute-done.54.refs_5_
  326.8 4.0 collective-permute-done.62.refs_13_
  333.3 6.0 %collective-permute-done.61.refs_12_ = bf16[2,3,24,768]{3,2,1,0:T(8,128)(2,1)} collective-permute-done((bf16[2,3,24,768]{3,2,1,0:T(8,128)(2,1)}, bf16[2,3,24,768]{3,2,1,0:T(8,128)(2,1)}, u32[]{:S(2)}, u32[]{:S(2)}) %collective-permute-start.61) | collective-permute-done | bytes 221216 | tf_op jit(solution)/shard_map/ppermute | solution.py:785
  345.2 4.3 %arrange.14 = bf16[3,4,8,24,768]{4,3,2,1,0:T(8,128)(2,1)} custom-call(s32[1]{0:T(128)} %bitcast.4.own_at, bf16[2,3,24,768]{3,2,1,0:T(8,128)(2,1)} %copy-done.16, bf16[2,3,24,768]{3,2,1,0:T(8,128)(2,1)} %copy-done.15, bf16[2,3,24,768]{3,2,1,0:T(8,128)(2,1)} %copy-done.41, bf16[2,3,24,768]{3,2,1,0:T(8,128)(2,1)} %copy-done.39, ...), custom_call_target="tpu_custom_call" | custom-call | bytes 7077888 | tf_op jit(solution)/shard_map/arrange/pallas_call | solution.py:804
  351.1 6.5 %refresh.4 = (f32[2,72,2304]{2,1,0:T(8,128)}, f32[2,24,768]{2,1,0:T(8,128)}, f32[2,72,768]{2,1,0:T(8,128)}, f32[32,2304]{1,0:T(8,128)}) custom-call(bf16[2304,768]{1,0:T(8,128)(2,1)} %bitcast.178, bf16[72,768]{1,0:T(8,128)(2,1)} %constant_dynamic-slice_fusion.own, bf16[32,768]{1,0:T(8,128)(2,1)} %fusion.42.select, f32[2,72,2304]{2,1,0:T(8,128)} %stat_left.3, ...), custom_call_target="tpu_custom_call" | custom-call | flops 736100352 | bytes 6709248 | tf_op jit(solution)/shard_map/refresh/pallas_call | solution.py:730
  361.7 3.9 add_convert_fusion.5
  374.0 6.4 %arrange.15 = (bf16[3,8,4,24,768]{4,3,2,1,0:T(8,128)(2,1)}, bf16[8,4,24,768]{3,2,1,0:T(8,128)(2,1)}, bf16[8,4,24,1152]{3,2,1,0:T(8,128)(2,1)}) custom-call(s32[1]{0:T(128)} %bitcast.4.own_at, bf16[2,24,4224]{2,1,0:T(8,128)(2,1)} %get-tuple-element.153.refs_0_, bf16[2,24,4224]{2,1,0:T(8,128)(2,1)} %copy-done.8, ...), custom_call_target="tpu_custom_call" | custom-call | bytes 12976128 | tf_op jit(solution)/shard_map/arrange/pallas_call | solution.py:804
  380.5 6.3 %refresh.7 = (f32[1,24,768]{2,1,0:T(8,128)}, f32[1,36,1152]{2,1,0:T(8,128)}, f32[3,24,768]{2,1,0:T(8,128)}, f32[48,768]{1,0:T(8,128)}) custom-call(bf16[768,1152]{1,0:T(8,128)(2,1)} %bitcast.195, bf16[24,4224]{1,0:T(8,128)(2,1)} %copy-done.4, bf16[48,1152]{1,0:T(8,128)(2,1)} %fusion.40.select, f32[1,24,768]{2,1,0:T(8,128)} %bitcast.211, ...), custom_call_target="tpu_custom_call" | custom-call | flops 254803968 | bytes 4644864 | tf_op jit(solution)/shard_map/refresh/pallas_call | solution.py:730
  389.8 3.6 refresh.6
  395.0 6.3 %refresh.5 = (f32[2,72,2304]{2,1,0:T(8,128)}, f32[2,24,768]{2,1,0:T(8,128)}, f32[2,72,768]{2,1,0:T(8,128)}, f32[32,2304]{1,0:T(8,128)}) custom-call(bf16[2304,768]{1,0:T(8,128)(2,1)} %bitcast.181, bf16[72,768]{1,0:T(8,128)(2,1)} %constant_dynamic-slice_fusion.8.own, ...), custom_call_target="tpu_custom_call", output_to_operand_aliasing={{0}: (8, {}), {1}: (9, {}), {2}: (10, {})} | custom-call | flops 736100352 | bytes 6709248 | tf_op jit(solution)/shard_map/refresh/pallas_call | solution.py:730
  (447 shorter events, 129.5 us)
Async XLA Ops:
  7.2 68.0 %all-gather.5.cloned.1.call-start = ((), (), s32[]{:S(2)}) async-start(), calls=%async_computation.3 | async-start | bytes 3686400 | tf_op jit(solution)/shard_map/all_gather | solution.py:985
  7.9 151.4 %all-gather.9.cloned.1.call-start = ((), (), s32[]{:S(2)}) async-start(), calls=%async_computation.6 | async-start | bytes 3649536 | tf_op jit(solution)/shard_map/all_gather | solution.py:996
  10.4 10.3 %collective-permute-start.2 = (bf16[72,896]{1,0:T(8,128)(2,1)S(1)}, bf16[72,896]{1,0:T(8,128)(2,1)S(1)}, u32[]{:S(2)}, u32[]{:S(2)}) collective-permute-start(bf16[72,896]{1,0:T(8,128)(2,1)S(1)} %fusion.41.refs_0_), channel_id=1, source_target_pairs={{0,3},{1,2},{2,1},{3,0},{4,7},{5,6},{6,5},{7,4},{8,11},{9,10},{10,... | collective-permute-start | bytes 387080 | tf_op jit(solution)/shard_map/ppermute | solution.py:785
  15.5 19.9 %collective-permute-start.1 = (bf16[72,896]{1,0:T(8,128)(2,1)S(1)}, bf16[72,896]{1,0:T(8,128)(2,1)S(1)}, u32[]{:S(2)}, u32[]{:S(2)}) collective-permute-start(bf16[72,896]{1,0:T(8,128)(2,1)S(1)} %fusion.41.refs_0_), channel_id=1, source_target_pairs={{0,2},{1,3},{2,0},{3,1},{4,6},{5,7},{6,4},{7,5},{8,10},{9,11},{10,... | collective-permute-start | bytes 387080 | tf_op jit(solution)/shard_map/ppermute | solution.py:785
  15.5 19.9 %collective-permute-start = (bf16[72,896]{1,0:T(8,128)(2,1)S(1)}, bf16[72,896]{1,0:T(8,128)(2,1)S(1)}, u32[]{:S(2)}, u32[]{:S(2)}) collective-permute-start(bf16[72,896]{1,0:T(8,128)(2,1)S(1)} %fusion.41.refs_0_), channel_id=1, source_target_pairs={{0,1},{1,0},{2,3},{3,2},{4,5},{5,4},{6,7},{7,6},{8,9},{9,8},{10,11... | collective-permute-start | bytes 387080 | tf_op jit(solution)/shard_map/ppermute | solution.py:785
  42.3 9.0 %collective-permute-start.4 = (bf16[2,72,896]{2,1,0:T(8,128)(2,1)S(1)}, bf16[2,72,896]{2,1,0:T(8,128)(2,1)S(1)}, u32[]{:S(2)}, u32[]{:S(2)}) collective-permute-start(bf16[2,72,896]{2,1,0:T(8,128)(2,1)S(1)} %get-tuple-element.214.refs_1_), channel_id=1, source_target_pairs={{0,4},{4,0},{8,12},{12,8},{16,20},{20,16},{24,28},{28,24},{1,5},{5... | collective-permute-start | bytes 774152 | tf_op jit(solution)/shard_map/ppermute | solution.py:785
  42.3 12.1 %collective-permute-start.5 = (bf16[2,72,896]{2,1,0:T(8,128)(2,1)S(1)}, bf16[2,72,896]{2,1,0:T(8,128)(2,1)}, u32[]{:S(2)}, u32[]{:S(2)}) collective-permute-start(bf16[2,72,896]{2,1,0:T(8,128)(2,1)S(1)} %get-tuple-element.215.refs_0_), channel_id=1, source_target_pairs={{0,8},{4,12},{8,0},{12,4},{16,24},{20,28},{24,16},{28,20},{1,9},{5... | collective-permute-start | bytes 774152 | tf_op jit(solution)/shard_map/ppermute | solution.py:785
  45.4 11.0 %collective-permute-start.9 = (bf16[2,72,896]{2,1,0:T(8,128)(2,1)S(1)}, bf16[2,72,896]{2,1,0:T(8,128)(2,1)}, u32[]{:S(2)}, u32[]{:S(2)}) collective-permute-start(bf16[2,72,896]{2,1,0:T(8,128)(2,1)S(1)} %get-tuple-element.215.refs_0_), channel_id=1, source_target_pairs={{0,16},{4,20},{8,24},{12,28},{16,0},{20,4},{24,8},{28,12},{1,17},{... | collective-permute-start | bytes 774152 | tf_op jit(solution)/shard_map/ppermute | solution.py:785
  45.8 10.6 %collective-permute-start.3 = (bf16[2,72,896]{2,1,0:T(8,128)(2,1)S(1)}, bf16[2,72,896]{2,1,0:T(8,128)(2,1)}, u32[]{:S(2)}, u32[]{:S(2)}) collective-permute-start(bf16[2,72,896]{2,1,0:T(8,128)(2,1)S(1)} %get-tuple-element.215.refs_0_), channel_id=1, source_target_pairs={{0,4},{4,0},{8,12},{12,8},{16,20},{20,16},{24,28},{28,24},{1,5},{5... | collective-permute-start | bytes 774152 | tf_op jit(solution)/shard_map/ppermute | solution.py:785
  48.9 9.4 %collective-permute-start.14 = (bf16[2,72,896]{2,1,0:T(8,128)(2,1)S(1)}, bf16[2,72,896]{2,1,0:T(8,128)(2,1)}, u32[]{:S(2)}, u32[]{:S(2)}) collective-permute-start(bf16[2,72,896]{2,1,0:T(8,128)(2,1)S(1)} %collective-permute-done.10.refs_9_), channel_id=1, source_target_pairs={{0,8},{4,12},{8,0},{12,4},{16,24},{20,28},{24,16},{28,20},{1,9},{5... | collective-permute-start | bytes 774152 | tf_op jit(solution)/shard_map/ppermute | solution.py:785
  75.2 13.8 %collective-permute-start.19 = (bf16[24,1920]{1,0:T(8,128)(2,1)S(1)}, bf16[24,1920]{1,0:T(8,128)(2,1)S(1)}, u32[]{:S(2)}, u32[]{:S(2)}) collective-permute-start(bf16[24,1920]{1,0:T(8,128)(2,1)S(1)} %pad_maximum_fusion.5.refs_0_), channel_id=1, source_target_pairs={{0,3},{1,2},{2,1},{3,0},{4,7},{5,6},{6,5},{7,4},{8,11},{9,10},{10,... | collective-permute-start | bytes 276488 | tf_op jit(solution)/shard_map/ppermute | solution.py:785
  78.6 10.4 %collective-permute-start.18 = (bf16[24,1920]{1,0:T(8,128)(2,1)S(1)}, bf16[24,1920]{1,0:T(8,128)(2,1)S(1)}, u32[]{:S(2)}, u32[]{:S(2)}) collective-permute-start(bf16[24,1920]{1,0:T(8,128)(2,1)S(1)} %pad_maximum_fusion.5.refs_0_), channel_id=1, source_target_pairs={{0,2},{1,3},{2,0},{3,1},{4,6},{5,7},{6,4},{7,5},{8,10},{9,11},{10,... | collective-permute-start | bytes 276488 | tf_op jit(solution)/shard_map/ppermute | solution.py:785
  78.6 10.5 %collective-permute-start.17 = (bf16[24,1920]{1,0:T(8,128)(2,1)S(1)}, bf16[24,1920]{1,0:T(8,128)(2,1)S(1)}, u32[]{:S(2)}, u32[]{:S(2)}) collective-permute-start(bf16[24,1920]{1,0:T(8,128)(2,1)S(1)} %pad_maximum_fusion.5.refs_0_), channel_id=1, source_target_pairs={{0,1},{1,0},{2,3},{3,2},{4,5},{5,4},{6,7},{7,6},{8,9},{9,8},{10,11... | collective-permute-start | bytes 276488 | tf_op jit(solution)/shard_map/ppermute | solution.py:785
  94.3 9.1 %collective-permute-start.20 = (bf16[2,24,1920]{2,1,0:T(8,128)(2,1)S(1)}, bf16[2,24,1920]{2,1,0:T(8,128)(2,1)S(1)}, u32[]{:S(2)}, u32[]{:S(2)}) collective-permute-start(bf16[2,24,1920]{2,1,0:T(8,128)(2,1)S(1)} %get-tuple-element.120.refs_0_), channel_id=1, source_target_pairs={{0,8},{4,12},{8,0},{12,4},{16,24},{20,28},{24,16},{28,20},{1,9},{5... | collective-permute-start | bytes 552968 | tf_op jit(solution)/shard_map/ppermute | solution.py:785
  96.6 29.1 %collective-permute-start.21 = (bf16[2,24,1920]{2,1,0:T(8,128)(2,1)S(1)}, bf16[2,24,1920]{2,1,0:T(8,128)(2,1)S(1)}, u32[]{:S(2)}, u32[]{:S(2)}) collective-permute-start(bf16[2,24,1920]{2,1,0:T(8,128)(2,1)S(1)} %get-tuple-element.121.refs_1_), channel_id=1, source_target_pairs={{0,8},{4,12},{8,0},{12,4},{16,24},{20,28},{24,16},{28,20},{1,9},{5... | collective-permute-start | bytes 552968 | tf_op jit(solution)/shard_map/ppermute | solution.py:785
  96.8 28.9 %collective-permute-start.22 = (bf16[2,24,1920]{2,1,0:T(8,128)(2,1)S(1)}, bf16[2,24,1920]{2,1,0:T(8,128)(2,1)S(1)}, u32[]{:S(2)}, u32[]{:S(2)}) collective-permute-start(bf16[2,24,1920]{2,1,0:T(8,128)(2,1)S(1)} %get-tuple-element.120.refs_0_), channel_id=1, source_target_pairs={{0,16},{4,20},{8,24},{12,28},{16,0},{20,4},{24,8},{28,12},{1,17},{... | collective-permute-start | bytes 552968 | tf_op jit(solution)/shard_map/ppermute | solution.py:785
  100.5 25.3 %collective-permute-start.25 = (bf16[2,24,1920]{2,1,0:T(8,128)(2,1)S(1)}, bf16[2,24,1920]{2,1,0:T(8,128)(2,1)S(1)}, u32[]{:S(2)}, u32[]{:S(2)}) collective-permute-start(bf16[2,24,1920]{2,1,0:T(8,128)(2,1)S(1)} %collective-permute-done.23.refs_9_), channel_id=1, source_target_pairs={{0,8},{4,12},{8,0},{12,4},{16,24},{20,28},{24,16},{28,20},{1,9},{5... | collective-permute-start | bytes 552968 | tf_op jit(solution)/shard_map/ppermute | solution.py:785
  103.4 22.4 %collective-permute-start.24 = (bf16[2,24,1920]{2,1,0:T(8,128)(2,1)S(1)}, bf16[2,24,1920]{2,1,0:T(8,128)(2,1)S(1)}, u32[]{:S(2)}, u32[]{:S(2)}) collective-permute-start(bf16[2,24,1920]{2,1,0:T(8,128)(2,1)S(1)} %collective-permute-done.20.refs_4_), channel_id=1, source_target_pairs={{0,16},{4,20},{8,24},{12,28},{16,0},{20,4},{24,8},{28,12},{1,17},{... | collective-permute-start | bytes 552968 | tf_op jit(solution)/shard_map/ppermute | solution.py:785
  129.3 25.2 %all-to-all-start = ((bf16[4,720,128]{2,1,0:T(8,128)(2,1)}), bf16[4,720,128]{2,1,0:T(8,128)(2,1)S(1)}, u32[]{:S(2)}, u32[]{:S(2)}) async-start(bf16[4,720,128]{2,1,0:T(8,128)(2,1)} %maximum_maximum_fusion.2), calls=%async_computation | async-start | bytes 1474560 | tf_op jit(solution)/shard_map/all_to_all | solution.py:1175
  178.0 23.3 %all-to-all-start.1 = ((bf16[4,720,128]{2,1,0:T(8,128)(2,1)}), bf16[4,720,128]{2,1,0:T(8,128)(2,1)S(1)}, u32[]{:S(2)}, u32[]{:S(2)}) async-start(bf16[4,720,128]{2,1,0:T(8,128)(2,1)} %copy.101), calls=%async_computation.1 | async-start | bytes 1474560 | tf_op jit(solution)/shard_map/all_to_all | solution.py:1206
  181.5 129.7 %all-gather.7.cloned.1.call-start = ((), (), s32[]{:S(2)}) async-start(), calls=%async_computation.4 | async-start | bytes 6488064 | tf_op jit(solution)/shard_map/all_gather | solution.py:1230
  201.3 203.5 %reduce-scatter.2.cloned.1.call-start = ((), (), s32[]{:S(2)}) async-start(), calls=%async_computation.5 | async-start | bytes 3686400 | tf_op jit(solution)/shard_map/reduce_scatter | solution.py:1319
  211.4 36.0 %collective-permute-start.35 = (bf16[96,4224]{1,0:T(8,128)(2,1)}, bf16[96,4224]{1,0:T(8,128)(2,1)}, u32[]{:S(2)}, u32[]{:S(2)}) collective-permute-start(bf16[96,4224]{1,0:T(8,128)(2,1)} %get-tuple-element.138), channel_id=1, source_target_pairs={{0,8},{4,12},{8,0},{12,4},{16,24},{20,28},{24,16},{28,20},{1,9},{5... | collective-permute-start | bytes 2433032 | tf_op jit(solution)/shard_map/ppermute | solution.py:785
  212.8 34.7 %collective-permute-start.36 = (bf16[96,4224]{1,0:T(8,128)(2,1)}, bf16[96,4224]{1,0:T(8,128)(2,1)}, u32[]{:S(2)}, u32[]{:S(2)}) collective-permute-start(bf16[96,4224]{1,0:T(8,128)(2,1)} %get-tuple-element.139), channel_id=1, source_target_pairs={{0,16},{4,20},{8,24},{12,28},{16,0},{20,4},{24,8},{28,12},{1,17},{... | collective-permute-start | bytes 2433032 | tf_op jit(solution)/shard_map/ppermute | solution.py:785
  213.5 44.0 %collective-permute-start.37 = (bf16[96,4224]{1,0:T(8,128)(2,1)}, bf16[96,4224]{1,0:T(8,128)(2,1)}, u32[]{:S(2)}, u32[]{:S(2)}) collective-permute-start(bf16[96,4224]{1,0:T(8,128)(2,1)} %get-tuple-element.140), channel_id=1, source_target_pairs={{0,24},{4,28},{8,16},{12,20},{16,8},{20,12},{24,0},{28,4},{1,25},{... | collective-permute-start | bytes 2433032 | tf_op jit(solution)/shard_map/ppermute | solution.py:785
  259.6 12.8 %collective-permute-start.46 = (bf16[24,4224]{1,0:T(8,128)(2,1)S(1)}, bf16[24,4224]{1,0:T(8,128)(2,1)S(1)}, u32[]{:S(2)}, u32[]{:S(2)}) collective-permute-start(bf16[24,4224]{1,0:T(8,128)(2,1)S(1)} %get-tuple-element.209), channel_id=1, source_target_pairs={{0,1},{1,0},{2,3},{3,2},{4,5},{5,4},{6,7},{7,6},{8,9},{9,8},{10,11... | collective-permute-start | bytes 608264 | tf_op jit(solution)/shard_map/ppermute | solution.py:785
  266.0 17.6 %collective-permute-start.45 = (bf16[24,4224]{1,0:T(8,128)(2,1)S(1)}, bf16[24,4224]{1,0:T(8,128)(2,1)S(1)}, u32[]{:S(2)}, u32[]{:S(2)}) collective-permute-start(bf16[24,4224]{1,0:T(8,128)(2,1)S(1)} %get-tuple-element.208), channel_id=1, source_target_pairs={{0,1},{1,0},{2,3},{3,2},{4,5},{5,4},{6,7},{7,6},{8,9},{9,8},{10,11... | collective-permute-start | bytes 608264 | tf_op jit(solution)/shard_map/ppermute | solution.py:785
  266.1 13.1 %collective-permute-start.38 = (bf16[3,4,24,768]{3,2,0,1:T(8,128)(2,1)S(1)}, bf16[3,4,24,768]{3,2,0,1:T(8,128)(2,1)S(1)}, u32[]{:S(2)}, u32[]{:S(2)}) collective-permute-start(bf16[3,4,24,768]{3,2,0,1:T(8,128)(2,1)S(1)} %copy_bitcast_fusion), channel_id=1, source_target_pairs={{0,4},{4,0},{8,12},{12,8},{16,20},{20,16},{24,28},{28,24},{1,5},{5... | collective-permute-start | bytes 1327112 | tf_op jit(solution)/shard_map/ppermute | solution.py:785
  272.5 13.4 %collective-permute-start.47 = (bf16[24,4224]{1,0:T(8,128)(2,1)S(1)}, bf16[24,4224]{1,0:T(8,128)(2,1)S(1)}, u32[]{:S(2)}, u32[]{:S(2)}) collective-permute-start(bf16[24,4224]{1,0:T(8,128)(2,1)S(1)} %fusion.30), channel_id=1, source_target_pairs={{0,2},{1,3},{2,0},{3,1},{4,6},{5,7},{6,4},{7,5},{8,10},{9,11},{10,... | collective-permute-start | bytes 608264 | tf_op jit(solution)/shard_map/ppermute | solution.py:785
  279.3 11.1 %collective-permute-start.39 = (bf16[3,24,768]{2,1,0:T(8,128)(2,1)S(1)}, bf16[3,24,768]{2,1,0:T(8,128)(2,1)S(1)}, u32[]{:S(2)}, u32[]{:S(2)}) collective-permute-start(bf16[3,24,768]{2,1,0:T(8,128)(2,1)S(1)} %get-tuple-element.203), channel_id=1, source_target_pairs={{0,8},{4,12},{8,0},{12,4},{16,24},{20,28},{24,16},{28,20},{1,9},{5... | collective-permute-start | bytes 331784 | tf_op jit(solution)/shard_map/ppermute | solution.py:785
  280.4 10.1 %collective-permute-start.41 = (bf16[3,24,768]{2,1,0:T(8,128)(2,1)S(1)}, bf16[3,24,768]{2,1,0:T(8,128)(2,1)S(1)}, u32[]{:S(2)}, u32[]{:S(2)}) collective-permute-start(bf16[3,24,768]{2,1,0:T(8,128)(2,1)S(1)} %get-tuple-element.204), channel_id=1, source_target_pairs={{0,24},{4,28},{8,16},{12,20},{16,8},{20,12},{24,0},{28,4},{1,25},{... | collective-permute-start | bytes 331784 | tf_op jit(solution)/shard_map/ppermute | solution.py:785
  281.9 8.6 %collective-permute-start.40 = (bf16[3,24,768]{2,1,0:T(8,128)(2,1)S(1)}, bf16[3,24,768]{2,1,0:T(8,128)(2,1)S(1)}, u32[]{:S(2)}, u32[]{:S(2)}) collective-permute-start(bf16[3,24,768]{2,1,0:T(8,128)(2,1)S(1)} %get-tuple-element.205), channel_id=1, source_target_pairs={{0,16},{4,20},{8,24},{12,28},{16,0},{20,4},{24,8},{28,12},{1,17},{... | collective-permute-start | bytes 331784 | tf_op jit(solution)/shard_map/ppermute | solution.py:785
  286.7 13.1 %collective-permute-start.49 = (bf16[24,4224]{1,0:T(8,128)(2,1)S(1)}, bf16[24,4224]{1,0:T(8,128)(2,1)S(1)}, u32[]{:S(2)}, u32[]{:S(2)}) collective-permute-start(bf16[24,4224]{1,0:T(8,128)(2,1)S(1)} %get-tuple-element.190.refs_0_.own), channel_id=1, source_target_pairs={{0,2},{1,3},{2,0},{3,1},{4,6},{5,7},{6,4},{7,5},{8,10},{9,11},{10,... | collective-permute-start | bytes 608264 | tf_op jit(solution)/shard_map/ppermute | solution.py:785
  286.7 20.9 %collective-permute-start.48 = (bf16[24,4224]{1,0:T(8,128)(2,1)S(1)}, bf16[24,4224]{1,0:T(8,128)(2,1)S(1)}, u32[]{:S(2)}, u32[]{:S(2)}) collective-permute-start(bf16[24,4224]{1,0:T(8,128)(2,1)S(1)} %get-tuple-element.190.refs_0_.own), channel_id=1, source_target_pairs={{0,1},{1,0},{2,3},{3,2},{4,5},{5,4},{6,7},{7,6},{8,9},{9,8},{10,11... | collective-permute-start | bytes 608264 | tf_op jit(solution)/shard_map/ppermute | solution.py:785
  290.6 13.8 %collective-permute-start.44 = (bf16[3,24,768]{2,1,0:T(8,128)(2,1)S(1)}, bf16[3,24,768]{2,1,0:T(8,128)(2,1)S(1)}, u32[]{:S(2)}, u32[]{:S(2)}) collective-permute-start(bf16[3,24,768]{2,1,0:T(8,128)(2,1)S(1)} %add_convert_fusion.6.refs_0_), channel_id=1, source_target_pairs={{0,3},{1,2},{2,1},{3,0},{4,7},{5,6},{6,5},{7,4},{8,11},{9,10},{10,... | collective-permute-start | bytes 331784 | tf_op jit(solution)/shard_map/ppermute | solution.py:785
  291.3 13.1 %collective-permute-start.43 = (bf16[3,24,768]{2,1,0:T(8,128)(2,1)S(1)}, bf16[3,24,768]{2,1,0:T(8,128)(2,1)S(1)}, u32[]{:S(2)}, u32[]{:S(2)}) collective-permute-start(bf16[3,24,768]{2,1,0:T(8,128)(2,1)S(1)} %add_convert_fusion.6.refs_0_), channel_id=1, source_target_pairs={{0,2},{1,3},{2,0},{3,1},{4,6},{5,7},{6,4},{7,5},{8,10},{9,11},{10,... | collective-permute-start | bytes 331784 | tf_op jit(solution)/shard_map/ppermute | solution.py:785
  292.1 12.3 %collective-permute-start.42 = (bf16[3,24,768]{2,1,0:T(8,128)(2,1)S(1)}, bf16[3,24,768]{2,1,0:T(8,128)(2,1)S(1)}, u32[]{:S(2)}, u32[]{:S(2)}) collective-permute-start(bf16[3,24,768]{2,1,0:T(8,128)(2,1)S(1)} %add_convert_fusion.6.refs_0_), channel_id=1, source_target_pairs={{0,1},{1,0},{2,3},{3,2},{4,5},{5,4},{6,7},{7,6},{8,9},{9,8},{10,11... | collective-permute-start | bytes 331784 | tf_op jit(solution)/shard_map/ppermute | solution.py:785
  321.4 9.4 %collective-permute-start.62 = (bf16[2,3,24,768]{3,2,1,0:T(8,128)(2,1)}, bf16[2,3,24,768]{3,2,1,0:T(8,128)(2,1)S(1)}, u32[]{:S(2)}, u32[]{:S(2)}) collective-permute-start(bf16[2,3,24,768]{3,2,1,0:T(8,128)(2,1)} %collective-permute-done.58.refs_9_), channel_id=1, source_target_pairs={{0,8},{4,12},{8,0},{12,4},{16,24},{20,28},{24,16},{28,20},{1,9},{5... | collective-permute-start | bytes 663560 | tf_op jit(solution)/shard_map/ppermute | solution.py:785
  323.4 18.0 %collective-permute-start.68 = (bf16[2,24,4224]{2,1,0:T(8,128)(2,1)S(1)}, bf16[2,24,4224]{2,1,0:T(8,128)(2,1)}, u32[]{:S(2)}, u32[]{:S(2)}) collective-permute-start(bf16[2,24,4224]{2,1,0:T(8,128)(2,1)S(1)} %get-tuple-element.154.refs_1_), channel_id=1, source_target_pairs={{0,16},{4,20},{8,24},{12,28},{16,0},{20,4},{24,8},{28,12},{1,17},{... | collective-permute-start | bytes 1216520 | tf_op jit(solution)/shard_map/ppermute | solution.py:785
  324.4 17.0 %collective-permute-start.65 = (bf16[2,24,4224]{2,1,0:T(8,128)(2,1)}, bf16[2,24,4224]{2,1,0:T(8,128)(2,1)}, u32[]{:S(2)}, u32[]{:S(2)}) collective-permute-start(bf16[2,24,4224]{2,1,0:T(8,128)(2,1)} %get-tuple-element.153.refs_0_), channel_id=1, source_target_pairs={{0,8},{4,12},{8,0},{12,4},{16,24},{20,28},{24,16},{28,20},{1,9},{5... | collective-permute-start | bytes 1216520 | tf_op jit(solution)/shard_map/ppermute | solution.py:785
  332.6 9.5 %collective-permute-start.64 = (bf16[2,3,24,768]{3,2,1,0:T(8,128)(2,1)}, bf16[2,3,24,768]{3,2,1,0:T(8,128)(2,1)}, u32[]{:S(2)}, u32[]{:S(2)}) collective-permute-start(bf16[2,3,24,768]{3,2,1,0:T(8,128)(2,1)} %copy-done.42), channel_id=1, source_target_pairs={{0,4},{4,0},{8,12},{12,8},{16,20},{20,16},{24,28},{28,24},{1,5},{5... | collective-permute-start | bytes 663560 | tf_op jit(solution)/shard_map/ppermute | solution.py:785
  339.3 18.3 %collective-permute-start.66 = (bf16[2,24,4224]{2,1,0:T(8,128)(2,1)S(1)}, bf16[2,24,4224]{2,1,0:T(8,128)(2,1)}, u32[]{:S(2)}, u32[]{:S(2)}) collective-permute-start(bf16[2,24,4224]{2,1,0:T(8,128)(2,1)S(1)} %get-tuple-element.154.refs_1_), channel_id=1, source_target_pairs={{0,8},{4,12},{8,0},{12,4},{16,24},{20,28},{24,16},{28,20},{1,9},{5... | collective-permute-start | bytes 1216520 | tf_op jit(solution)/shard_map/ppermute | solution.py:785
  340.5 17.1 %collective-permute-start.67 = (bf16[2,24,4224]{2,1,0:T(8,128)(2,1)}, bf16[2,24,4224]{2,1,0:T(8,128)(2,1)}, u32[]{:S(2)}, u32[]{:S(2)}) collective-permute-start(bf16[2,24,4224]{2,1,0:T(8,128)(2,1)} %get-tuple-element.153.refs_0_), channel_id=1, source_target_pairs={{0,16},{4,20},{8,24},{12,28},{16,0},{20,4},{24,8},{28,12},{1,17},{... | collective-permute-start | bytes 1216520 | tf_op jit(solution)/shard_map/ppermute | solution.py:785
  341.4 17.0 %collective-permute-start.70 = (bf16[2,24,4224]{2,1,0:T(8,128)(2,1)}, bf16[2,24,4224]{2,1,0:T(8,128)(2,1)}, u32[]{:S(2)}, u32[]{:S(2)}) collective-permute-start(bf16[2,24,4224]{2,1,0:T(8,128)(2,1)} %collective-permute-done.68.refs_9_), channel_id=1, source_target_pairs={{0,8},{4,12},{8,0},{12,4},{16,24},{20,28},{24,16},{28,20},{1,9},{5... | collective-permute-start | bytes 1216520 | tf_op jit(solution)/shard_map/ppermute | solution.py:785
  342.2 17.3 %collective-permute-start.69 = (bf16[2,24,4224]{2,1,0:T(8,128)(2,1)}, bf16[2,24,4224]{2,1,0:T(8,128)(2,1)}, u32[]{:S(2)}, u32[]{:S(2)}) collective-permute-start(bf16[2,24,4224]{2,1,0:T(8,128)(2,1)} %collective-permute-done.65.refs_4_), channel_id=1, source_target_pairs={{0,16},{4,20},{8,24},{12,28},{16,0},{20,4},{24,8},{28,12},{1,17},{... | collective-permute-start | bytes 1216520 | tf_op jit(solution)/shard_map/ppermute | solution.py:785
  359.5 9.7 %collective-permute-start.71 = (bf16[2,24,4224]{2,1,0:T(8,128)(2,1)}, bf16[2,24,4224]{2,1,0:T(8,128)(2,1)}, u32[]{:S(2)}, u32[]{:S(2)}) collective-permute-start(bf16[2,24,4224]{2,1,0:T(8,128)(2,1)} %get-tuple-element.153.refs_0_), channel_id=1, source_target_pairs={{0,4},{4,0},{8,12},{12,8},{16,20},{20,16},{24,28},{28,24},{1,5},{5... | collective-permute-start | bytes 1216520 | tf_op jit(solution)/shard_map/ppermute | solution.py:785
  359.5 10.2 %collective-permute-start.72 = (bf16[2,24,4224]{2,1,0:T(8,128)(2,1)S(1)}, bf16[2,24,4224]{2,1,0:T(8,128)(2,1)}, u32[]{:S(2)}, u32[]{:S(2)}) collective-permute-start(bf16[2,24,4224]{2,1,0:T(8,128)(2,1)S(1)} %get-tuple-element.154.refs_1_), channel_id=1, source_target_pairs={{0,4},{4,0},{8,12},{12,8},{16,20},{20,16},{24,28},{28,24},{1,5},{5... | collective-permute-start | bytes 1216520 | tf_op jit(solution)/shard_map/ppermute | solution.py:785
  360.0 9.8 %collective-permute-start.73 = (bf16[2,24,4224]{2,1,0:T(8,128)(2,1)}, bf16[2,24,4224]{2,1,0:T(8,128)(2,1)}, u32[]{:S(2)}, u32[]{:S(2)}) collective-permute-start(bf16[2,24,4224]{2,1,0:T(8,128)(2,1)} %collective-permute-done.65.refs_4_), channel_id=1, source_target_pairs={{0,4},{4,0},{8,12},{12,8},{16,20},{20,16},{24,28},{28,24},{1,5},{5... | collective-permute-start | bytes 1216520 | tf_op jit(solution)/shard_map/ppermute | solution.py:785
  (124 other events, 980.5 us)
Sparse Core Ops, SparseCore 0:
  9.6 65.0 all-gather.4
  78.0 66.4 all-gather.8
  201.5 82.2 all-gather.6
  311.3 57.9 reduce-scatter.1

commit v6 on v5

--- a/solution.py
+++ b/solution.py
@@ -1341,6 +1341,8 @@
     )
     fenced = fence(stacked, *term_partners)
     stacked, term_blocks = fenced[0], gather_cores(fenced[1:])
+    fenced = fence(grad_input, *term_blocks)
+    grad_input, term_blocks = fenced[0], fenced[1:]
     whole_shape = (dp_count, seq_count, ao_rows)
     cut = (slice(None), slice(None))
     whole_up, whole_ao, whole_fo = arrange(

time: 421 us -> 420 us (level)
  Pallas kernels: 125 us -> 118 us
    pallas_call x1, Pallas kernels: 32.5 us -> 28 us  [head_body(): pl.pallas_call(attend_back_kernel, grid_spec=pltpu.PrefetchScalarGridSpec...]
    unnamed x181 -> x175, local copies, waits for them, and re-layouts: 13.2 us -> 13.5 us
  transfers between devices with their start and end apart: 85 -> 85, of which waited for: 24 -> 22; matrix products, arithmetic and copies ran while one was open for 20% -> 19% of each run, Pallas kernels for 30% -> 23%
where the time goes in v6:
time: 420 us; the launch traced here: 413 us
  Pallas kernels  118 us (28%)
  waiting for transfers between devices  85.1 us (20%)
  starting transfers between devices  78 us (19%)
  local copies, waits for them, and re-layouts  47.2 us (11%)
  other arithmetic  44.2 us (11%)
  matrix products  25 us (6%)
  between operations  16.2 us (4%)
    ppermute x79, waiting for transfers between devices, exchange(): return lax.ppermute(values, axis, [(i, i ^ offset) for i in range(size)])  71.5 us
    ppermute x79, starting transfers between devices, exchange(): return lax.ppermute(values, axis, [(i, i ^ offset) for i in range(size)])  69 us
    pallas_call x1, Pallas kernels, head_body(): pl.pallas_call(attend_back_kernel, grid_spec=pltpu.PrefetchScalarGridSpec...  28 us
    pallas_call x8, Pallas kernels, arrange(): pl.pallas_call(functools.partial(arrange_kernel, count=count, moves=moves...  26.7 us
    pallas_call x4, Pallas kernels, refresh(): pl.pallas_call(functools.partial(refresh_kernel, kept=len(previous), own_...  22.7 us
    pallas_call x1, Pallas kernels, head_body(): pl.pallas_call(attend_kernel, grid_spec=pltpu.PrefetchScalarGridSpec(num_...  19.4 us
    unnamed x175, local copies, waits for them, and re-layouts  13.5 us
    all_to_all x1, waiting for transfers between devices, head_body(): packed = lax.all_to_all(packed, 'seq', 0, 0, tiled=True)  12.4 us
  transfers between devices with their start and end apart: 85, of which 22 were waited for; matrix products, arithmetic and copies ran while one was open for 19% of the time, Pallas kernels for 23%

profile of v6, /device:TPU:0, one launch (start us, length us, event | category | flops | bytes accessed | tf_op | source)
XLA Modules:
  0.0 413.4 jit_solution(12056244817831602323)
XLA Ops:
  10.4 5.1 %collective-permute-start.2 = (bf16[72,896]{1,0:T(8,128)(2,1)S(1)}, bf16[72,896]{1,0:T(8,128)(2,1)S(1)}, u32[]{:S(2)}, u32[]{:S(2)}) collective-permute-start(bf16[72,896]{1,0:T(8,128)(2,1)S(1)} %fusion.41.refs_0_), channel_id=1, source_target_pairs={{0,3},{1,2},{2,1},{3,0},{4,7},{5,6},{6,5},{7,4},{8,11},{9,10},{10,... | collective-permute-start | bytes 387080 | tf_op jit(solution)/shard_map/ppermute | solution.py:785
  17.2 3.5 multiply_sine_fusion
  20.8 14.7 %collective-permute-done.1.refs_2_ = bf16[72,896]{1,0:T(8,128)(2,1)S(1)} collective-permute-done((bf16[72,896]{1,0:T(8,128)(2,1)S(1)}, bf16[72,896]{1,0:T(8,128)(2,1)S(1)}, u32[]{:S(2)}, u32[]{:S(2)}) %collective-permute-start.1) | collective-permute-done | bytes 129056 | tf_op jit(solution)/shard_map/ppermute | solution.py:785
  42.8 2.5 select_convert_fusion.key_mask
  45.8 3.0 collective-permute-done.6.refs_5_
  48.9 2.5 collective-permute-start.14
  51.4 3.1 collective-permute-done.5.refs_4_
  58.8 2.3 collective-permute-done.13.refs_12_
  61.1 2.9 pad_maximum_fusion.1
  65.1 4.5 %arrange.9 = (bf16[8,4,72,768]{3,2,1,0:T(8,128)(2,1)}, bf16[8,4,72,128]{3,2,1,0:T(8,128)(2,1)}) custom-call(s32[1]{0:T(128)} %bitcast.4.own_at, bf16[2,72,896]{2,1,0:T(8,128)(2,1)} %copy-done.11, bf16[2,72,896]{2,1,0:T(8,128)(2,1)} %copy-done.10, bf16[2,72,896]{2,1,0:T(8,128)(2,1)} %collective-permute-done.3.refs_2_, bf16[2,72,896]{2,1,0:T(8,128)(2,1)} %copy-done.30, ...), custom_call_target="tpu_custom_call" | custom-call | bytes 8257536 | tf_op jit(solution)/shard_map/arrange/pallas_call | solution.py:804
  75.2 3.4 collective-permute-start.19
  79.6 9.4 %project.1 = (bf16[1920,768]{1,0:T(8,128)(2,1)}, bf16[3,1920,128]{2,1,0:T(8,128)(2,1)}, bf16[3,2400,128]{2,1,0:T(8,128)(2,1)}, bf16[3,2400,128]{2,1,0:T(8,128)(2,1)}) custom-call(bf16[1920,768]{1,0:T(8,128)(2,1)} %all-gather.5.cloned.1.call-done.tokens, bf16[640,768]{1,0:T(8,128)(2,1)} %maximum_maximum_fusion.weight, f32[1,768]{1,0:T(1,128)} %slice.196.gain, ...), custom_call_target="tpu_custom_call" | custom-call | flops 1887436800 | bytes 14000000 | tf_op jit(solution)/shard_map/project/pallas_call | solution.py:1077
  100.4 2.9 collective-permute-start.25
  103.4 19.4 %attend.1 = (bf16[1920,128]{1,0:T(8,128)(2,1)}, bf16[1920,128]{1,0:T(8,128)(2,1)}, bf16[3,1920,128]{2,1,0:T(8,128)(2,1)}) custom-call(s32[4]{0:T(128)} %get-tuple-element.229.start_at, s32[4]{0:T(128)} %get-tuple-element.228.step_count, s32[1]{0:T(128)} %sub.86.pad_from, bf16[3,1920,128]{2,1,0:T(8,128)(2,1)} %get-tuple-element.128.query, ...), custom_call_target="tpu_custom_call" | custom-call | flops 2831155200 | bytes 12000000 | tf_op jit(solution)/shard_map/attend/pallas_call | solution.py:1132
  126.4 5.3 %all-to-all-start = ((bf16[4,720,128]{2,1,0:T(8,128)(2,1)}), bf16[4,720,128]{2,1,0:T(8,128)(2,1)S(1)}, u32[]{:S(2)}, u32[]{:S(2)}) async-start(bf16[4,720,128]{2,1,0:T(8,128)(2,1)} %maximum_maximum_fusion.2), calls=%async_computation | async-start | bytes 1474560 | tf_op jit(solution)/shard_map/all_to_all | solution.py:1175
  138.1 3.8 arrange.11
  142.0 12.4 %all-to-all-done = bf16[4,720,128]{2,1,0:T(8,128)(2,1)S(1)} async-done(((bf16[4,720,128]{2,1,0:T(8,128)(2,1)}), bf16[4,720,128]{2,1,0:T(8,128)(2,1)S(1)}, u32[]{:S(2)}, u32[]{:S(2)}) %all-to-all-start) | async-done | bytes 737312 | tf_op jit(solution)/shard_map/all_to_all | solution.py:1175
  155.7 2.2 fusion.69
  159.4 4.3 %fusion.2 = f32[480,2304]{1,0:T(8,128)S(1)} fusion(bf16[480,768]{1,0:T(8,128)(2,1)} %multiply_convert_fusion.2.ffn_in, bf16[1,2304,768]{2,1,0:T(8,128)(2,1)} %all-gather.9.cloned.1.call-done), kind=kOutput, calls=%fused_computation.2 | convolution fusion | flops 1698693120 | bytes 8699904 | tf_op jit(solution)/shard_map/dot_general | solution.py:84
  163.7 2.9 fusion.9
  177.9 3.5 all-to-all-start.1
  184.3 2.3 copy.97.attended
  186.5 3.1 pad_maximum_fusion.grad_proj
  189.6 11.6 %terms.1 = (bf16[4,96,4224]{2,1,0:T(8,128)(2,1)}, bf16[4,96,4224]{2,1,0:T(8,128)(2,1)}) custom-call(s32[1]{0:T(128)} %bitcast.22.core, bf16[480,2304]{1,0:T(8,128)(2,1)} %pad_maximum_fusion.grad_proj, bf16[480,768]{1,0:T(8,128)(2,1)} %multiply_convert_fusion.2.ffn_in, bf16[480,768]{1,0:T(8,128)(2,1)} %copy-done.17, bf16[480,768]{1,0:T(8,128)(2,1)} %copy.97.attended, ...), custom_call_target="tpu_custom_call" | custom-call | flops 3114270720 | bytes 13000000 | tf_op jit(solution)/shard_map/terms/pallas_call | solution.py:1214
  203.4 4.2 %collective-permute-done.34 = bf16[4,96,4224]{2,1,0:T(8,128)(2,1)} collective-permute-done((bf16[4,96,4224]{2,1,0:T(8,128)(2,1)}, bf16[4,96,4224]{2,1,0:T(8,128)(2,1)}, u32[]{:S(2)}, u32[]{:S(2)}) %collective-permute-start.34) | collective-permute-done | bytes 3244064 | tf_op jit(solution)/shard_map/ppermute | solution.py:785
  207.5 3.8 fusion.29
  214.8 28.0 %attend_back.1 = bf16[1920,640]{1,0:T(8,128)(2,1)} custom-call(s32[4]{0:T(128)} %get-tuple-element.229.start_at, s32[4]{0:T(128)} %get-tuple-element.228.step_count, s32[1]{0:T(128)} %sub.86.pad_from, bf16[3,1920,128]{2,1,0:T(8,128)(2,1)} %get-tuple-element.147.query, bf16[1920,128]{1,0:T(8,128)(2,1)} %get-tuple-element.135.pair_out, ...), custom_call_target="tpu_custom_call" | custom-call | flops 7077888000 | bytes 15000000 | tf_op jit(solution)/shard_map/attend_back/pallas_call | solution.py:1250
  242.9 14.3 %collective-permute-done.37 = bf16[96,4224]{1,0:T(8,128)(2,1)} collective-permute-done((bf16[96,4224]{1,0:T(8,128)(2,1)}, bf16[96,4224]{1,0:T(8,128)(2,1)}, u32[]{:S(2)}, u32[]{:S(2)}) %collective-permute-start.37) | collective-permute-done | bytes 811040 | tf_op jit(solution)/shard_map/ppermute | solution.py:785
  260.9 4.0 fusion.70
  265.6 5.0 %collective-permute-done.46 = bf16[24,4224]{1,0:T(8,128)(2,1)S(1)} collective-permute-done((bf16[24,4224]{1,0:T(8,128)(2,1)S(1)}, bf16[24,4224]{1,0:T(8,128)(2,1)S(1)}, u32[]{:S(2)}, u32[]{:S(2)}) %collective-permute-start.46) | collective-permute-done | bytes 202784 | tf_op jit(solution)/shard_map/ppermute | solution.py:785
  270.7 5.9 %collective-permute-start.47 = (bf16[24,4224]{1,0:T(8,128)(2,1)S(1)}, bf16[24,4224]{1,0:T(8,128)(2,1)S(1)}, u32[]{:S(2)}, u32[]{:S(2)}) collective-permute-start(bf16[24,4224]{1,0:T(8,128)(2,1)S(1)} %fusion.30), channel_id=1, source_target_pairs={{0,2},{1,3},{2,0},{3,1},{4,6},{5,7},{6,4},{7,5},{8,10},{9,11},{10,... | collective-permute-start | bytes 608264 | tf_op jit(solution)/shard_map/ppermute | solution.py:785
  277.9 2.4 collective-permute-start.39
  281.9 2.2 collective-permute-done.45
  286.6 3.6 collective-permute-start.48
  291.9 2.9 collective-permute-start.42
  294.9 5.0 %collective-permute-done.49.refs_2_ = bf16[24,4224]{1,0:T(8,128)(2,1)S(1)} collective-permute-done((bf16[24,4224]{1,0:T(8,128)(2,1)S(1)}, bf16[24,4224]{1,0:T(8,128)(2,1)S(1)}, u32[]{:S(2)}, u32[]{:S(2)}) %collective-permute-start.49) | collective-permute-done | bytes 202784 | tf_op jit(solution)/shard_map/ppermute | solution.py:785
  300.2 4.1 convolution_convert_fusion
  319.1 3.0 collective-permute-done.58.refs_9_
  328.6 4.2 %collective-permute-done.62.refs_13_ = bf16[2,3,24,768]{3,2,1,0:T(8,128)(2,1)S(1)} collective-permute-done((bf16[2,3,24,768]{3,2,1,0:T(8,128)(2,1)}, bf16[2,3,24,768]{3,2,1,0:T(8,128)(2,1)S(1)}, u32[]{:S(2)}, u32[]{:S(2)}) %collective-permute-start.62) | collective-permute-done | bytes 221216 | tf_op jit(solution)/shard_map/ppermute | solution.py:785
  336.5 3.8 add_convert_fusion.5
  340.3 2.6 collective-permute-done.61.refs_12_
  352.5 4.2 %arrange.14 = bf16[3,4,8,24,768]{4,3,2,1,0:T(8,128)(2,1)} custom-call(s32[1]{0:T(128)} %bitcast.4.own_at, bf16[2,3,24,768]{3,2,1,0:T(8,128)(2,1)} %copy-done.15, bf16[2,3,24,768]{3,2,1,0:T(8,128)(2,1)} %copy-done.14, bf16[2,3,24,768]{3,2,1,0:T(8,128)(2,1)} %copy-done.38, bf16[2,3,24,768]{3,2,1,0:T(8,128)(2,1)} %copy-done.36, ...), custom_call_target="tpu_custom_call" | custom-call | bytes 7077888 | tf_op jit(solution)/shard_map/arrange/pallas_call | solution.py:804
  359.2 6.5 %refresh.4 = (f32[2,72,2304]{2,1,0:T(8,128)}, f32[2,24,768]{2,1,0:T(8,128)}, f32[2,72,768]{2,1,0:T(8,128)}, f32[32,2304]{1,0:T(8,128)}) custom-call(bf16[2304,768]{1,0:T(8,128)(2,1)} %bitcast.179, bf16[72,768]{1,0:T(8,128)(2,1)} %constant_dynamic-slice_fusion.own, bf16[32,768]{1,0:T(8,128)(2,1)} %fusion.42.select, f32[2,72,2304]{2,1,0:T(8,128)} %stat_left.3, ...), custom_call_target="tpu_custom_call" | custom-call | flops 736100352 | bytes 6709248 | tf_op jit(solution)/shard_map/refresh/pallas_call | solution.py:730
  371.5 2.8 fusion.17
  375.9 6.4 %arrange.15 = (bf16[3,8,4,24,768]{4,3,2,1,0:T(8,128)(2,1)}, bf16[8,4,24,768]{3,2,1,0:T(8,128)(2,1)}, bf16[8,4,24,1152]{3,2,1,0:T(8,128)(2,1)}) custom-call(s32[1]{0:T(128)} %bitcast.4.own_at, bf16[2,24,4224]{2,1,0:T(8,128)(2,1)} %get-tuple-element.179.refs_0_, bf16[2,24,4224]{2,1,0:T(8,128)(2,1)} %copy-done.7, ...), custom_call_target="tpu_custom_call" | custom-call | bytes 12976128 | tf_op jit(solution)/shard_map/arrange/pallas_call | solution.py:804
  384.8 6.3 %refresh.7 = (f32[1,24,768]{2,1,0:T(8,128)}, f32[1,36,1152]{2,1,0:T(8,128)}, f32[3,24,768]{2,1,0:T(8,128)}, f32[48,768]{1,0:T(8,128)}) custom-call(bf16[768,1152]{1,0:T(8,128)(2,1)} %bitcast.195, bf16[24,4224]{1,0:T(8,128)(2,1)} %copy-done.4, bf16[48,1152]{1,0:T(8,128)(2,1)} %fusion.40.select, f32[1,24,768]{2,1,0:T(8,128)} %bitcast.211, ...), custom_call_target="tpu_custom_call" | custom-call | flops 254803968 | bytes 4644864 | tf_op jit(solution)/shard_map/refresh/pallas_call | solution.py:730
  394.2 6.3 %refresh.5 = (f32[2,72,2304]{2,1,0:T(8,128)}, f32[2,24,768]{2,1,0:T(8,128)}, f32[2,72,768]{2,1,0:T(8,128)}, f32[32,2304]{1,0:T(8,128)}) custom-call(bf16[2304,768]{1,0:T(8,128)(2,1)} %bitcast.182, bf16[72,768]{1,0:T(8,128)(2,1)} %constant_dynamic-slice_fusion.8.own, ...), custom_call_target="tpu_custom_call", output_to_operand_aliasing={{0}: (8, {}), {1}: (9, {}), {2}: (10, {})} | custom-call | flops 736100352 | bytes 6709248 | tf_op jit(solution)/shard_map/refresh/pallas_call | solution.py:730
  403.0 3.6 refresh.6
  (441 shorter events, 131.3 us)
Async XLA Ops:
  7.2 68.0 %all-gather.5.cloned.1.call-start = ((), (), s32[]{:S(2)}) async-start(), calls=%async_computation.3 | async-start | bytes 3686400 | tf_op jit(solution)/shard_map/all_gather | solution.py:985
  7.9 151.4 %all-gather.9.cloned.1.call-start = ((), (), s32[]{:S(2)}) async-start(), calls=%async_computation.6 | async-start | bytes 3649536 | tf_op jit(solution)/shard_map/all_gather | solution.py:996
  10.4 10.3 %collective-permute-start.2 = (bf16[72,896]{1,0:T(8,128)(2,1)S(1)}, bf16[72,896]{1,0:T(8,128)(2,1)S(1)}, u32[]{:S(2)}, u32[]{:S(2)}) collective-permute-start(bf16[72,896]{1,0:T(8,128)(2,1)S(1)} %fusion.41.refs_0_), channel_id=1, source_target_pairs={{0,3},{1,2},{2,1},{3,0},{4,7},{5,6},{6,5},{7,4},{8,11},{9,10},{10,... | collective-permute-start | bytes 387080 | tf_op jit(solution)/shard_map/ppermute | solution.py:785
  15.5 19.9 %collective-permute-start.1 = (bf16[72,896]{1,0:T(8,128)(2,1)S(1)}, bf16[72,896]{1,0:T(8,128)(2,1)S(1)}, u32[]{:S(2)}, u32[]{:S(2)}) collective-permute-start(bf16[72,896]{1,0:T(8,128)(2,1)S(1)} %fusion.41.refs_0_), channel_id=1, source_target_pairs={{0,2},{1,3},{2,0},{3,1},{4,6},{5,7},{6,4},{7,5},{8,10},{9,11},{10,... | collective-permute-start | bytes 387080 | tf_op jit(solution)/shard_map/ppermute | solution.py:785
  15.5 19.9 %collective-permute-start = (bf16[72,896]{1,0:T(8,128)(2,1)S(1)}, bf16[72,896]{1,0:T(8,128)(2,1)S(1)}, u32[]{:S(2)}, u32[]{:S(2)}) collective-permute-start(bf16[72,896]{1,0:T(8,128)(2,1)S(1)} %fusion.41.refs_0_), channel_id=1, source_target_pairs={{0,1},{1,0},{2,3},{3,2},{4,5},{5,4},{6,7},{7,6},{8,9},{9,8},{10,11... | collective-permute-start | bytes 387080 | tf_op jit(solution)/shard_map/ppermute | solution.py:785
  42.3 9.0 %collective-permute-start.4 = (bf16[2,72,896]{2,1,0:T(8,128)(2,1)S(1)}, bf16[2,72,896]{2,1,0:T(8,128)(2,1)S(1)}, u32[]{:S(2)}, u32[]{:S(2)}) collective-permute-start(bf16[2,72,896]{2,1,0:T(8,128)(2,1)S(1)} %get-tuple-element.248.refs_1_), channel_id=1, source_target_pairs={{0,4},{4,0},{8,12},{12,8},{16,20},{20,16},{24,28},{28,24},{1,5},{5... | collective-permute-start | bytes 774152 | tf_op jit(solution)/shard_map/ppermute | solution.py:785
  42.3 12.1 %collective-permute-start.5 = (bf16[2,72,896]{2,1,0:T(8,128)(2,1)S(1)}, bf16[2,72,896]{2,1,0:T(8,128)(2,1)}, u32[]{:S(2)}, u32[]{:S(2)}) collective-permute-start(bf16[2,72,896]{2,1,0:T(8,128)(2,1)S(1)} %get-tuple-element.249.refs_0_), channel_id=1, source_target_pairs={{0,8},{4,12},{8,0},{12,4},{16,24},{20,28},{24,16},{28,20},{1,9},{5... | collective-permute-start | bytes 774152 | tf_op jit(solution)/shard_map/ppermute | solution.py:785
  45.4 11.0 %collective-permute-start.9 = (bf16[2,72,896]{2,1,0:T(8,128)(2,1)S(1)}, bf16[2,72,896]{2,1,0:T(8,128)(2,1)}, u32[]{:S(2)}, u32[]{:S(2)}) collective-permute-start(bf16[2,72,896]{2,1,0:T(8,128)(2,1)S(1)} %get-tuple-element.249.refs_0_), channel_id=1, source_target_pairs={{0,16},{4,20},{8,24},{12,28},{16,0},{20,4},{24,8},{28,12},{1,17},{... | collective-permute-start | bytes 774152 | tf_op jit(solution)/shard_map/ppermute | solution.py:785
  45.8 10.6 %collective-permute-start.3 = (bf16[2,72,896]{2,1,0:T(8,128)(2,1)S(1)}, bf16[2,72,896]{2,1,0:T(8,128)(2,1)}, u32[]{:S(2)}, u32[]{:S(2)}) collective-permute-start(bf16[2,72,896]{2,1,0:T(8,128)(2,1)S(1)} %get-tuple-element.249.refs_0_), channel_id=1, source_target_pairs={{0,4},{4,0},{8,12},{12,8},{16,20},{20,16},{24,28},{28,24},{1,5},{5... | collective-permute-start | bytes 774152 | tf_op jit(solution)/shard_map/ppermute | solution.py:785
  48.9 9.4 %collective-permute-start.14 = (bf16[2,72,896]{2,1,0:T(8,128)(2,1)S(1)}, bf16[2,72,896]{2,1,0:T(8,128)(2,1)}, u32[]{:S(2)}, u32[]{:S(2)}) collective-permute-start(bf16[2,72,896]{2,1,0:T(8,128)(2,1)S(1)} %collective-permute-done.10.refs_9_), channel_id=1, source_target_pairs={{0,8},{4,12},{8,0},{12,4},{16,24},{20,28},{24,16},{28,20},{1,9},{5... | collective-permute-start | bytes 774152 | tf_op jit(solution)/shard_map/ppermute | solution.py:785
  75.2 13.8 %collective-permute-start.19 = (bf16[24,1920]{1,0:T(8,128)(2,1)S(1)}, bf16[24,1920]{1,0:T(8,128)(2,1)S(1)}, u32[]{:S(2)}, u32[]{:S(2)}) collective-permute-start(bf16[24,1920]{1,0:T(8,128)(2,1)S(1)} %pad_maximum_fusion.5.refs_0_), channel_id=1, source_target_pairs={{0,3},{1,2},{2,1},{3,0},{4,7},{5,6},{6,5},{7,4},{8,11},{9,10},{10,... | collective-permute-start | bytes 276488 | tf_op jit(solution)/shard_map/ppermute | solution.py:785
  78.6 10.4 %collective-permute-start.18 = (bf16[24,1920]{1,0:T(8,128)(2,1)S(1)}, bf16[24,1920]{1,0:T(8,128)(2,1)S(1)}, u32[]{:S(2)}, u32[]{:S(2)}) collective-permute-start(bf16[24,1920]{1,0:T(8,128)(2,1)S(1)} %pad_maximum_fusion.5.refs_0_), channel_id=1, source_target_pairs={{0,2},{1,3},{2,0},{3,1},{4,6},{5,7},{6,4},{7,5},{8,10},{9,11},{10,... | collective-permute-start | bytes 276488 | tf_op jit(solution)/shard_map/ppermute | solution.py:785
  78.6 10.4 %collective-permute-start.17 = (bf16[24,1920]{1,0:T(8,128)(2,1)S(1)}, bf16[24,1920]{1,0:T(8,128)(2,1)S(1)}, u32[]{:S(2)}, u32[]{:S(2)}) collective-permute-start(bf16[24,1920]{1,0:T(8,128)(2,1)S(1)} %pad_maximum_fusion.5.refs_0_), channel_id=1, source_target_pairs={{0,1},{1,0},{2,3},{3,2},{4,5},{5,4},{6,7},{7,6},{8,9},{9,8},{10,11... | collective-permute-start | bytes 276488 | tf_op jit(solution)/shard_map/ppermute | solution.py:785
  94.2 9.1 %collective-permute-start.20 = (bf16[2,24,1920]{2,1,0:T(8,128)(2,1)S(1)}, bf16[2,24,1920]{2,1,0:T(8,128)(2,1)S(1)}, u32[]{:S(2)}, u32[]{:S(2)}) collective-permute-start(bf16[2,24,1920]{2,1,0:T(8,128)(2,1)S(1)} %get-tuple-element.137.refs_0_), channel_id=1, source_target_pairs={{0,8},{4,12},{8,0},{12,4},{16,24},{20,28},{24,16},{28,20},{1,9},{5... | collective-permute-start | bytes 552968 | tf_op jit(solution)/shard_map/ppermute | solution.py:785
  96.6 26.2 %collective-permute-start.21 = (bf16[2,24,1920]{2,1,0:T(8,128)(2,1)S(1)}, bf16[2,24,1920]{2,1,0:T(8,128)(2,1)S(1)}, u32[]{:S(2)}, u32[]{:S(2)}) collective-permute-start(bf16[2,24,1920]{2,1,0:T(8,128)(2,1)S(1)} %get-tuple-element.138.refs_1_), channel_id=1, source_target_pairs={{0,8},{4,12},{8,0},{12,4},{16,24},{20,28},{24,16},{28,20},{1,9},{5... | collective-permute-start | bytes 552968 | tf_op jit(solution)/shard_map/ppermute | solution.py:785
  96.8 26.0 %collective-permute-start.22 = (bf16[2,24,1920]{2,1,0:T(8,128)(2,1)S(1)}, bf16[2,24,1920]{2,1,0:T(8,128)(2,1)S(1)}, u32[]{:S(2)}, u32[]{:S(2)}) collective-permute-start(bf16[2,24,1920]{2,1,0:T(8,128)(2,1)S(1)} %get-tuple-element.137.refs_0_), channel_id=1, source_target_pairs={{0,16},{4,20},{8,24},{12,28},{16,0},{20,4},{24,8},{28,12},{1,17},{... | collective-permute-start | bytes 552968 | tf_op jit(solution)/shard_map/ppermute | solution.py:785
  100.4 22.4 %collective-permute-start.25 = (bf16[2,24,1920]{2,1,0:T(8,128)(2,1)S(1)}, bf16[2,24,1920]{2,1,0:T(8,128)(2,1)S(1)}, u32[]{:S(2)}, u32[]{:S(2)}) collective-permute-start(bf16[2,24,1920]{2,1,0:T(8,128)(2,1)S(1)} %collective-permute-done.23.refs_9_), channel_id=1, source_target_pairs={{0,8},{4,12},{8,0},{12,4},{16,24},{20,28},{24,16},{28,20},{1,9},{5... | collective-permute-start | bytes 552968 | tf_op jit(solution)/shard_map/ppermute | solution.py:785
  103.4 19.5 %collective-permute-start.24 = (bf16[2,24,1920]{2,1,0:T(8,128)(2,1)S(1)}, bf16[2,24,1920]{2,1,0:T(8,128)(2,1)S(1)}, u32[]{:S(2)}, u32[]{:S(2)}) collective-permute-start(bf16[2,24,1920]{2,1,0:T(8,128)(2,1)S(1)} %collective-permute-done.20.refs_4_), channel_id=1, source_target_pairs={{0,16},{4,20},{8,24},{12,28},{16,0},{20,4},{24,8},{28,12},{1,17},{... | collective-permute-start | bytes 552968 | tf_op jit(solution)/shard_map/ppermute | solution.py:785
  126.4 28.0 %all-to-all-start = ((bf16[4,720,128]{2,1,0:T(8,128)(2,1)}), bf16[4,720,128]{2,1,0:T(8,128)(2,1)S(1)}, u32[]{:S(2)}, u32[]{:S(2)}) async-start(bf16[4,720,128]{2,1,0:T(8,128)(2,1)} %maximum_maximum_fusion.2), calls=%async_computation | async-start | bytes 1474560 | tf_op jit(solution)/shard_map/all_to_all | solution.py:1175
  177.9 23.3 %all-to-all-start.1 = ((bf16[4,720,128]{2,1,0:T(8,128)(2,1)}), bf16[4,720,128]{2,1,0:T(8,128)(2,1)S(1)}, u32[]{:S(2)}, u32[]{:S(2)}) async-start(bf16[4,720,128]{2,1,0:T(8,128)(2,1)} %copy.101), calls=%async_computation.1 | async-start | bytes 1474560 | tf_op jit(solution)/shard_map/all_to_all | solution.py:1206
  181.4 131.4 %all-gather.7.cloned.1.call-start = ((), (), s32[]{:S(2)}) async-start(), calls=%async_computation.4 | async-start | bytes 6488064 | tf_op jit(solution)/shard_map/all_gather | solution.py:1230
  201.3 167.9 %reduce-scatter.2.cloned.1.call-start = ((), (), s32[]{:S(2)}) async-start(), calls=%async_computation.5 | async-start | bytes 3686400 | tf_op jit(solution)/shard_map/reduce_scatter | solution.py:1319
  211.4 31.5 %collective-permute-start.35 = (bf16[96,4224]{1,0:T(8,128)(2,1)}, bf16[96,4224]{1,0:T(8,128)(2,1)}, u32[]{:S(2)}, u32[]{:S(2)}) collective-permute-start(bf16[96,4224]{1,0:T(8,128)(2,1)} %get-tuple-element.155), channel_id=1, source_target_pairs={{0,8},{4,12},{8,0},{12,4},{16,24},{20,28},{24,16},{28,20},{1,9},{5... | collective-permute-start | bytes 2433032 | tf_op jit(solution)/shard_map/ppermute | solution.py:785
  212.7 30.2 %collective-permute-start.36 = (bf16[96,4224]{1,0:T(8,128)(2,1)}, bf16[96,4224]{1,0:T(8,128)(2,1)}, u32[]{:S(2)}, u32[]{:S(2)}) collective-permute-start(bf16[96,4224]{1,0:T(8,128)(2,1)} %get-tuple-element.156), channel_id=1, source_target_pairs={{0,16},{4,20},{8,24},{12,28},{16,0},{20,4},{24,8},{28,12},{1,17},{... | collective-permute-start | bytes 2433032 | tf_op jit(solution)/shard_map/ppermute | solution.py:785
  213.5 43.7 %collective-permute-start.37 = (bf16[96,4224]{1,0:T(8,128)(2,1)}, bf16[96,4224]{1,0:T(8,128)(2,1)}, u32[]{:S(2)}, u32[]{:S(2)}) collective-permute-start(bf16[96,4224]{1,0:T(8,128)(2,1)} %get-tuple-element.157), channel_id=1, source_target_pairs={{0,24},{4,28},{8,16},{12,20},{16,8},{20,12},{24,0},{28,4},{1,25},{... | collective-permute-start | bytes 2433032 | tf_op jit(solution)/shard_map/ppermute | solution.py:785
  259.3 11.4 %collective-permute-start.46 = (bf16[24,4224]{1,0:T(8,128)(2,1)S(1)}, bf16[24,4224]{1,0:T(8,128)(2,1)S(1)}, u32[]{:S(2)}, u32[]{:S(2)}) collective-permute-start(bf16[24,4224]{1,0:T(8,128)(2,1)S(1)} %get-tuple-element.243), channel_id=1, source_target_pairs={{0,1},{1,0},{2,3},{3,2},{4,5},{5,4},{6,7},{7,6},{8,9},{9,8},{10,11... | collective-permute-start | bytes 608264 | tf_op jit(solution)/shard_map/ppermute | solution.py:785
  265.0 19.1 %collective-permute-start.45 = (bf16[24,4224]{1,0:T(8,128)(2,1)S(1)}, bf16[24,4224]{1,0:T(8,128)(2,1)S(1)}, u32[]{:S(2)}, u32[]{:S(2)}) collective-permute-start(bf16[24,4224]{1,0:T(8,128)(2,1)S(1)} %get-tuple-element.242), channel_id=1, source_target_pairs={{0,1},{1,0},{2,3},{3,2},{4,5},{5,4},{6,7},{7,6},{8,9},{9,8},{10,11... | collective-permute-start | bytes 608264 | tf_op jit(solution)/shard_map/ppermute | solution.py:785
  265.5 12.3 %collective-permute-start.38 = (bf16[3,4,24,768]{3,2,0,1:T(8,128)(2,1)S(1)}, bf16[3,4,24,768]{3,2,0,1:T(8,128)(2,1)S(1)}, u32[]{:S(2)}, u32[]{:S(2)}) collective-permute-start(bf16[3,4,24,768]{3,2,0,1:T(8,128)(2,1)S(1)} %copy_bitcast_fusion), channel_id=1, source_target_pairs={{0,4},{4,0},{8,12},{12,8},{16,20},{20,16},{24,28},{28,24},{1,5},{5... | collective-permute-start | bytes 1327112 | tf_op jit(solution)/shard_map/ppermute | solution.py:785
  270.7 13.4 %collective-permute-start.47 = (bf16[24,4224]{1,0:T(8,128)(2,1)S(1)}, bf16[24,4224]{1,0:T(8,128)(2,1)S(1)}, u32[]{:S(2)}, u32[]{:S(2)}) collective-permute-start(bf16[24,4224]{1,0:T(8,128)(2,1)S(1)} %fusion.30), channel_id=1, source_target_pairs={{0,2},{1,3},{2,0},{3,1},{4,6},{5,7},{6,4},{7,5},{8,10},{9,11},{10,... | collective-permute-start | bytes 608264 | tf_op jit(solution)/shard_map/ppermute | solution.py:785
  277.9 12.4 %collective-permute-start.39 = (bf16[3,24,768]{2,1,0:T(8,128)(2,1)S(1)}, bf16[3,24,768]{2,1,0:T(8,128)(2,1)S(1)}, u32[]{:S(2)}, u32[]{:S(2)}) collective-permute-start(bf16[3,24,768]{2,1,0:T(8,128)(2,1)S(1)} %get-tuple-element.237), channel_id=1, source_target_pairs={{0,8},{4,12},{8,0},{12,4},{16,24},{20,28},{24,16},{28,20},{1,9},{5... | collective-permute-start | bytes 331784 | tf_op jit(solution)/shard_map/ppermute | solution.py:785
  280.3 10.0 %collective-permute-start.41 = (bf16[3,24,768]{2,1,0:T(8,128)(2,1)S(1)}, bf16[3,24,768]{2,1,0:T(8,128)(2,1)S(1)}, u32[]{:S(2)}, u32[]{:S(2)}) collective-permute-start(bf16[3,24,768]{2,1,0:T(8,128)(2,1)S(1)} %get-tuple-element.238), channel_id=1, source_target_pairs={{0,24},{4,28},{8,16},{12,20},{16,8},{20,12},{24,0},{28,4},{1,25},{... | collective-permute-start | bytes 331784 | tf_op jit(solution)/shard_map/ppermute | solution.py:785
  281.7 8.6 %collective-permute-start.40 = (bf16[3,24,768]{2,1,0:T(8,128)(2,1)S(1)}, bf16[3,24,768]{2,1,0:T(8,128)(2,1)S(1)}, u32[]{:S(2)}, u32[]{:S(2)}) collective-permute-start(bf16[3,24,768]{2,1,0:T(8,128)(2,1)S(1)} %get-tuple-element.239), channel_id=1, source_target_pairs={{0,16},{4,20},{8,24},{12,28},{16,0},{20,4},{24,8},{28,12},{1,17},{... | collective-permute-start | bytes 331784 | tf_op jit(solution)/shard_map/ppermute | solution.py:785
  284.9 15.0 %collective-permute-start.49 = (bf16[24,4224]{1,0:T(8,128)(2,1)S(1)}, bf16[24,4224]{1,0:T(8,128)(2,1)S(1)}, u32[]{:S(2)}, u32[]{:S(2)}) collective-permute-start(bf16[24,4224]{1,0:T(8,128)(2,1)S(1)} %get-tuple-element.224.refs_0_.own), channel_id=1, source_target_pairs={{0,2},{1,3},{2,0},{3,1},{4,6},{5,7},{6,4},{7,5},{8,10},{9,11},{10,... | collective-permute-start | bytes 608264 | tf_op jit(solution)/shard_map/ppermute | solution.py:785
  286.6 22.7 %collective-permute-start.48 = (bf16[24,4224]{1,0:T(8,128)(2,1)S(1)}, bf16[24,4224]{1,0:T(8,128)(2,1)S(1)}, u32[]{:S(2)}, u32[]{:S(2)}) collective-permute-start(bf16[24,4224]{1,0:T(8,128)(2,1)S(1)} %get-tuple-element.224.refs_0_.own), channel_id=1, source_target_pairs={{0,1},{1,0},{2,3},{3,2},{4,5},{5,4},{6,7},{7,6},{8,9},{9,8},{10,11... | collective-permute-start | bytes 608264 | tf_op jit(solution)/shard_map/ppermute | solution.py:785
  290.4 14.0 %collective-permute-start.44 = (bf16[3,24,768]{2,1,0:T(8,128)(2,1)S(1)}, bf16[3,24,768]{2,1,0:T(8,128)(2,1)S(1)}, u32[]{:S(2)}, u32[]{:S(2)}) collective-permute-start(bf16[3,24,768]{2,1,0:T(8,128)(2,1)S(1)} %add_convert_fusion.6.refs_0_), channel_id=1, source_target_pairs={{0,3},{1,2},{2,1},{3,0},{4,7},{5,6},{6,5},{7,4},{8,11},{9,10},{10,... | collective-permute-start | bytes 331784 | tf_op jit(solution)/shard_map/ppermute | solution.py:785
  290.5 15.7 %collective-permute-start.43 = (bf16[3,24,768]{2,1,0:T(8,128)(2,1)S(1)}, bf16[3,24,768]{2,1,0:T(8,128)(2,1)S(1)}, u32[]{:S(2)}, u32[]{:S(2)}) collective-permute-start(bf16[3,24,768]{2,1,0:T(8,128)(2,1)S(1)} %add_convert_fusion.6.refs_0_), channel_id=1, source_target_pairs={{0,2},{1,3},{2,0},{3,1},{4,6},{5,7},{6,4},{7,5},{8,10},{9,11},{10,... | collective-permute-start | bytes 331784 | tf_op jit(solution)/shard_map/ppermute | solution.py:785
  291.9 14.2 %collective-permute-start.42 = (bf16[3,24,768]{2,1,0:T(8,128)(2,1)S(1)}, bf16[3,24,768]{2,1,0:T(8,128)(2,1)S(1)}, u32[]{:S(2)}, u32[]{:S(2)}) collective-permute-start(bf16[3,24,768]{2,1,0:T(8,128)(2,1)S(1)} %add_convert_fusion.6.refs_0_), channel_id=1, source_target_pairs={{0,1},{1,0},{2,3},{3,2},{4,5},{5,4},{6,7},{7,6},{8,9},{9,8},{10,11... | collective-permute-start | bytes 331784 | tf_op jit(solution)/shard_map/ppermute | solution.py:785
  299.9 9.5 %collective-permute-start.50 = (bf16[24,4224]{1,0:T(8,128)(2,1)S(1)}, bf16[24,4224]{1,0:T(8,128)(2,1)S(1)}, u32[]{:S(2)}, u32[]{:S(2)}) collective-permute-start(bf16[24,4224]{1,0:T(8,128)(2,1)S(1)} %collective-permute-done.49.refs_2_), channel_id=1, source_target_pairs={{0,1},{1,0},{2,3},{3,2},{4,5},{5,4},{6,7},{7,6},{8,9},{9,8},{10,11... | collective-permute-start | bytes 608264 | tf_op jit(solution)/shard_map/ppermute | solution.py:785
  316.8 9.0 %collective-permute-start.57 = (bf16[2,3,24,768]{3,2,1,0:T(8,128)(2,1)S(1)}, bf16[2,3,24,768]{3,2,1,0:T(8,128)(2,1)}, u32[]{:S(2)}, u32[]{:S(2)}) collective-permute-start(bf16[2,3,24,768]{3,2,1,0:T(8,128)(2,1)S(1)} %get-tuple-element.253.refs_0_), channel_id=1, source_target_pairs={{0,16},{4,20},{8,24},{12,28},{16,0},{20,4},{24,8},{28,12},{1,17},{... | collective-permute-start | bytes 663560 | tf_op jit(solution)/shard_map/ppermute | solution.py:785
  318.0 10.0 %collective-permute-start.53 = (bf16[2,3,24,768]{3,2,1,0:T(8,128)(2,1)S(1)}, bf16[2,3,24,768]{3,2,1,0:T(8,128)(2,1)S(1)}, u32[]{:S(2)}, u32[]{:S(2)}) collective-permute-start(bf16[2,3,24,768]{3,2,1,0:T(8,128)(2,1)S(1)} %get-tuple-element.253.refs_0_), channel_id=1, source_target_pairs={{0,8},{4,12},{8,0},{12,4},{16,24},{20,28},{24,16},{28,20},{1,9},{5... | collective-permute-start | bytes 663560 | tf_op jit(solution)/shard_map/ppermute | solution.py:785
  323.4 9.4 %collective-permute-start.62 = (bf16[2,3,24,768]{3,2,1,0:T(8,128)(2,1)}, bf16[2,3,24,768]{3,2,1,0:T(8,128)(2,1)S(1)}, u32[]{:S(2)}, u32[]{:S(2)}) collective-permute-start(bf16[2,3,24,768]{3,2,1,0:T(8,128)(2,1)} %collective-permute-done.58.refs_9_), channel_id=1, source_target_pairs={{0,8},{4,12},{8,0},{12,4},{16,24},{20,28},{24,16},{28,20},{1,9},{5... | collective-permute-start | bytes 663560 | tf_op jit(solution)/shard_map/ppermute | solution.py:785
  324.3 19.9 %collective-permute-start.68 = (bf16[2,24,4224]{2,1,0:T(8,128)(2,1)S(1)}, bf16[2,24,4224]{2,1,0:T(8,128)(2,1)}, u32[]{:S(2)}, u32[]{:S(2)}) collective-permute-start(bf16[2,24,4224]{2,1,0:T(8,128)(2,1)S(1)} %get-tuple-element.180.refs_1_), channel_id=1, source_target_pairs={{0,16},{4,20},{8,24},{12,28},{16,0},{20,4},{24,8},{28,12},{1,17},{... | collective-permute-start | bytes 1216520 | tf_op jit(solution)/shard_map/ppermute | solution.py:785
  325.8 18.4 %collective-permute-start.65 = (bf16[2,24,4224]{2,1,0:T(8,128)(2,1)}, bf16[2,24,4224]{2,1,0:T(8,128)(2,1)}, u32[]{:S(2)}, u32[]{:S(2)}) collective-permute-start(bf16[2,24,4224]{2,1,0:T(8,128)(2,1)} %get-tuple-element.179.refs_0_), channel_id=1, source_target_pairs={{0,8},{4,12},{8,0},{12,4},{16,24},{20,28},{24,16},{28,20},{1,9},{5... | collective-permute-start | bytes 1216520 | tf_op jit(solution)/shard_map/ppermute | solution.py:785
  336.1 9.9 %collective-permute-start.64 = (bf16[2,3,24,768]{3,2,1,0:T(8,128)(2,1)}, bf16[2,3,24,768]{3,2,1,0:T(8,128)(2,1)S(1)}, u32[]{:S(2)}, u32[]{:S(2)}) collective-permute-start(bf16[2,3,24,768]{3,2,1,0:T(8,128)(2,1)} %copy-done.39), channel_id=1, source_target_pairs={{0,4},{4,0},{8,12},{12,8},{16,20},{20,16},{24,28},{28,24},{1,5},{5... | collective-permute-start | bytes 663560 | tf_op jit(solution)/shard_map/ppermute | solution.py:785
  342.9 22.8 %collective-permute-start.66 = (bf16[2,24,4224]{2,1,0:T(8,128)(2,1)S(1)}, bf16[2,24,4224]{2,1,0:T(8,128)(2,1)}, u32[]{:S(2)}, u32[]{:S(2)}) collective-permute-start(bf16[2,24,4224]{2,1,0:T(8,128)(2,1)S(1)} %get-tuple-element.180.refs_1_), channel_id=1, source_target_pairs={{0,8},{4,12},{8,0},{12,4},{16,24},{20,28},{24,16},{28,20},{1,9},{5... | collective-permute-start | bytes 1216520 | tf_op jit(solution)/shard_map/ppermute | solution.py:785
  343.0 22.7 %collective-permute-start.67 = (bf16[2,24,4224]{2,1,0:T(8,128)(2,1)}, bf16[2,24,4224]{2,1,0:T(8,128)(2,1)}, u32[]{:S(2)}, u32[]{:S(2)}) collective-permute-start(bf16[2,24,4224]{2,1,0:T(8,128)(2,1)} %get-tuple-element.179.refs_0_), channel_id=1, source_target_pairs={{0,16},{4,20},{8,24},{12,28},{16,0},{20,4},{24,8},{28,12},{1,17},{... | collective-permute-start | bytes 1216520 | tf_op jit(solution)/shard_map/ppermute | solution.py:785
  344.2 21.5 %collective-permute-start.70 = (bf16[2,24,4224]{2,1,0:T(8,128)(2,1)}, bf16[2,24,4224]{2,1,0:T(8,128)(2,1)}, u32[]{:S(2)}, u32[]{:S(2)}) collective-permute-start(bf16[2,24,4224]{2,1,0:T(8,128)(2,1)} %collective-permute-done.68.refs_9_), channel_id=1, source_target_pairs={{0,8},{4,12},{8,0},{12,4},{16,24},{20,28},{24,16},{28,20},{1,9},{5... | collective-permute-start | bytes 1216520 | tf_op jit(solution)/shard_map/ppermute | solution.py:785
  346.0 19.7 %collective-permute-start.69 = (bf16[2,24,4224]{2,1,0:T(8,128)(2,1)}, bf16[2,24,4224]{2,1,0:T(8,128)(2,1)}, u32[]{:S(2)}, u32[]{:S(2)}) collective-permute-start(bf16[2,24,4224]{2,1,0:T(8,128)(2,1)} %collective-permute-done.65.refs_4_), channel_id=1, source_target_pairs={{0,16},{4,20},{8,24},{12,28},{16,0},{20,4},{24,8},{28,12},{1,17},{... | collective-permute-start | bytes 1216520 | tf_op jit(solution)/shard_map/ppermute | solution.py:785
  (121 other events, 985.5 us)
Sparse Core Ops, SparseCore 0:
  9.6 65.0 all-gather.4
  78.0 68.0 all-gather.8
  201.4 83.2 all-gather.6
  313.0 56.0 reduce-scatter.1
